TPU v7x, 32 devices: a whole 2x2x4 slice. The times are simulated.
32 devices in a mesh: ep: 4 (over y, x), tm: 8 (over z, core).
Axes of the slice: x: 2, y: 2, z: 4, core: 2. Of those that a mesh axis runs over, the one named last changes fastest.
Arguments:
- predictions: float32 [128, 262144], P('ep', 'tm'), may hold values from -6 to 6
- leaf_index: int32 [128, 262144], P('ep', 'tm'), may hold values from 0 to 63
- events: int32 [128, 262144], P('ep', 'tm'), may hold values 0 or 1
- tie_start: int32 [262144], P('tm'), may hold values from 0 to 1, as said below
Outputs:
- new_pred: float32 [128, 262144], P('ep', 'tm')
- leaf_weights: float32 [128, 64], P('ep')
- grad_hess: bfloat16 [2, 128, 8, 32768], P(None, None, 'tm', 'ep')
Inputs may be any that keep to these rules, and one draw needn't show every extreme that they name: `tie_start`: every row whose index is a multiple of 128 begins a tie group.
All inputs are finite; a program needn't handle non-finite values. No bound on the sum of `events` on one device may be relied on, other than what follows from the above.
Results may differ from a plain program's by a relative error of at most 0.0023.
Values may be sent and summed in bfloat16 or wider, within the bound.
No kernel may reach another device: no remote copies, remote signals or barrier semaphores. Data moves between devices by JAX's collectives and lax.ppermute only.
A program may use at most 128 MiB of HBM per device.

v0:
```python
import functools

import jax
import jax.numpy as jnp
from jax import lax
from jax.experimental import pallas as pl
from jax.experimental.pallas import tpu as pltpu
from jax.sharding import PartitionSpec as P

LEAVES = 64
LANES = 128
WIDE = 256
PARAMS = pltpu.CompilerParams(vmem_limit_bytes=24 * 1024 * 1024)
F32 = jnp.float32
BF16 = jnp.bfloat16


def resident(shape, dtype):
    return pltpu.VMEM(shape, dtype)


def near(array):
    return pltpu.with_memory_space_constraint(array, pltpu.VMEM)


def call(body, outs, *args, scratch=(), name=None):
    spec = pl.BlockSpec(memory_space=pltpu.VMEM)
    smem = pl.BlockSpec(memory_space=pltpu.SMEM)
    return pl.pallas_call(
        body,
        out_shape=outs,
        in_specs=[smem if a.ndim == 1 else spec for a in args],
        out_specs=[spec] * len(outs),
        scratch_shapes=list(scratch),
        compiler_params=PARAMS,
        name=name,
    )(*args)


def lane_sum(x):
    return jnp.broadcast_to(jnp.sum(x, axis=1, keepdims=True), (x.shape[0], LANES))


def fold(x):
    parts = [x[:, k : k + LANES] for k in range(0, x.shape[1], LANES)]
    while len(parts) > 1:
        parts = [a + b for a, b in zip(parts[::2], parts[1::2])] + parts[len(parts) & ~1 :]
    return parts[0]


def weights_body(pred, weight, total):
    rows, length = pred.shape
    step = min(length, 1024)

    def one(turn, acc):
        at = pl.ds(pl.multiple_of(turn * step, step), step)
        value = jnp.exp(pred[:, at])
        weight[:, at] = value
        return acc + fold(value)

    acc = lax.fori_loop(0, length // step, one, jnp.zeros((rows, LANES), F32), unroll=2)
    total[...] = lane_sum(acc)


def pair_dot(x, matrix):
    high = x.astype(BF16)
    low = (x - high.astype(F32)).astype(BF16)
    return jnp.dot(high, matrix, preferred_element_type=F32) + jnp.dot(low, matrix, preferred_element_type=F32)


def take(x, index):
    return jnp.take_along_axis(x, index, axis=1, mode="promise_in_bounds")


def tie_index(starts, from_end):
    lane = lax.broadcasted_iota(jnp.int32, starts.shape, 1)
    if not from_end:
        best = jnp.where(starts == 1, lane, 0)
        for shift in (1, 2, 4, 8, 16, 32, 64):
            moved = pltpu.roll(best, shift, 1)
            best = jnp.where(lane >= shift, jnp.maximum(best, moved), best)
        return best
    after = pltpu.roll(starts, LANES - 1, 1)
    best = jnp.where((after == 1) | (lane == LANES - 1), lane, LANES - 1)
    for shift in (1, 2, 4, 8, 16, 32, 64):
        moved = pltpu.roll(best, LANES - shift, 1)
        best = jnp.where(lane < LANES - shift, jnp.minimum(best, moved), best)
    return best


def stacked(ref, base, count, square=False):
    parts = [ref[:, pl.ds(pl.multiple_of(base + k * WIDE, WIDE), WIDE)] for k in range(count)]
    x = jnp.concatenate(parts, axis=0)
    return x * x if square else x


def scan_piece(out, index, summed, carry, base, rows, count, backward):
    order = range(count - 1, -1, -1) if backward else range(count)
    edge = 0 if backward else WIDE - 1
    for k in order:
        piece = summed[k * rows : (k + 1) * rows]
        for half in (0, 1):
            at = pl.multiple_of(base + k * WIDE + half * LANES, LANES)
            block = (base + k * WIDE) // LANES + half
            chosen = jnp.broadcast_to(index[pl.ds(block, 1), :], (rows, LANES))
            out[:, pl.ds(at, LANES)] = take(piece[:, half * LANES : (half + 1) * LANES], chosen) + carry
        carry = carry + jnp.broadcast_to(piece[:, edge : edge + 1], (rows, LANES))
    return carry


def risk_body(weight, tie, risk, last, first):
    rows, length = weight.shape
    count = min(8, length // WIDE)
    first[...] = tie_index(tie[...], False)
    last[...] = tie_index(tie[...], True)
    matrix = (lax.broadcasted_iota(jnp.int32, (WIDE, WIDE), 0) >= lax.broadcasted_iota(jnp.int32, (WIDE, WIDE), 1)).astype(BF16)
    steps = length // (WIDE * count)

    def one(turn, carry):
        base = (steps - 1 - turn) * (WIDE * count)
        summed = pair_dot(stacked(weight, base, count), matrix)
        return scan_piece(risk, first, summed, carry, base, rows, count, True)

    lax.fori_loop(0, steps, one, jnp.zeros((rows, LANES), F32))


def gathered_sum(masks, refs):
    out = None
    for k, ref in enumerate(refs):
        term = ref[...] * masks[k]
        out = term if out is None else out + term
    return out


def inverse_body(count, *refs):
    masks, others = refs[0], refs[1 : 1 + count]
    risk, events, inv, totals = refs[1 + count :]
    rows, length = risk.shape
    later = gathered_sum(masks, others)
    step = min(length, 512)

    def one(turn, acc):
        sum_one, sum_two = acc
        at = pl.ds(pl.multiple_of(turn * step, step), step)
        offset = jnp.concatenate([later] * (step // LANES), axis=1)
        value = events[:, at].astype(F32) / (risk[:, at] + offset)
        inv[:, at] = value
        return (sum_one + fold(value), sum_two + fold(value * value))

    empty = jnp.zeros((rows, LANES), F32)
    sum_one, sum_two = lax.fori_loop(0, length // step, one, (empty, empty))
    totals[:rows, :] = lane_sum(sum_one)
    totals[rows:, :] = lane_sum(sum_two)


def accum_body(inv, last, one_out, two_out):
    rows, length = inv.shape
    count = min(8, length // WIDE)
    matrix = (lax.broadcasted_iota(jnp.int32, (WIDE, WIDE), 0) <= lax.broadcasted_iota(jnp.int32, (WIDE, WIDE), 1)).astype(BF16)

    def one(turn, carry):
        base = turn * (WIDE * count)
        values = stacked(inv, base, count)
        first = scan_piece(one_out, last, pair_dot(values, matrix), carry[0], base, rows, count, False)
        second = scan_piece(two_out, last, pair_dot(values * values, matrix), carry[1], base, rows, count, False)
        return (first, second)

    empty = jnp.zeros((rows, LANES), F32)
    lax.fori_loop(0, length // (WIDE * count), one, (empty, empty))


def derivatives(weight, observed, accum_one, accum_two):
    scaled = weight * accum_one
    return scaled - observed, scaled - weight * weight * accum_two


def pieces_body(count, parts, *refs):
    masks, starts, others = refs[0], refs[1], refs[2 : 2 + count]
    weight, events, local_one, local_two = refs[2 + count : 6 + count]
    outs = refs[6 + count : 6 + count + parts]
    bases = refs[6 + count + parts]
    rows = weight.shape[0]
    length = outs[0].shape[2]
    earlier = gathered_sum(masks, others)
    bases[...] = earlier
    step = min(length, 512)

    for part in range(parts):

        def one(turn, carry):
            base_one = jnp.concatenate([bases[:rows, :]] * (step // LANES), axis=1)
            base_two = jnp.concatenate([bases[rows:, :]] * (step // LANES), axis=1)
            source = pl.ds(pl.multiple_of(starts[part] + turn * step, step), step)
            at = pl.ds(pl.multiple_of(turn * step, step), step)
            grad, hess = derivatives(
                weight[:, source],
                events[:, source].astype(F32),
                local_one[:, source] + base_one,
                local_two[:, source] + base_two,
            )
            outs[part][0, :, at] = grad.astype(BF16)
            outs[part][1, :, at] = hess.astype(BF16)
            return carry

        lax.fori_loop(0, length // step, one, 0)


GROUP = 16
LOW = 16
HIGH = LEAVES // LOW


def leaf_sums_body(leaf, weight, events, local_one, local_two, bases, sums, acc):
    rows, length = weight.shape
    step = min(length, 512)
    groups = rows // GROUP
    acc[...] = jnp.zeros_like(acc)

    def one(turn, carry):
        at = pl.ds(pl.multiple_of(turn * step, step), step)
        for group in range(groups):
            mine = pl.ds(group * GROUP, GROUP)
            base_one = jnp.concatenate([bases[mine, :]] * (step // LANES), axis=1)
            base_two = jnp.concatenate([bases[pl.ds(rows + group * GROUP, GROUP), :]] * (step // LANES), axis=1)
            pair = derivatives(
                weight[mine, at],
                events[mine, at].astype(F32),
                local_one[mine, at] + base_one,
                local_two[mine, at] + base_two,
            )
            label = leaf[mine, at]
            low = (label & (LOW - 1)).astype(F32).astype(BF16)
            high = (label // LOW).astype(F32).astype(BF16)
            terms = []
            for value in pair:
                upper = value.astype(BF16)
                terms += [upper, (value - upper.astype(F32)).astype(BF16)]
            zero = jnp.zeros((GROUP, step), BF16)
            unit = jnp.ones((GROUP, step), BF16)
            left = jnp.concatenate([jnp.where(high == h, term, zero) for term in terms for h in range(HIGH)], axis=0)
            right = jnp.concatenate([jnp.where(low == k, unit, zero) for k in range(LOW)], axis=0)
            acc[group] += lax.dot_general(left, right, (((1,), (1,)), ((), ())), preferred_element_type=F32)
        return carry

    lax.fori_loop(0, length // step, one, 0)
    width = LOW * GROUP
    side = HIGH * GROUP
    row_of = lax.broadcasted_iota(jnp.int32, (side, width), 0) % GROUP
    column_of = lax.broadcasted_iota(jnp.int32, (side, width), 1) % GROUP
    same = row_of == column_of
    source = lax.broadcasted_iota(jnp.int32, (width, LANES), 0) // GROUP
    target = lax.broadcasted_iota(jnp.int32, (width, LANES), 1)
    for group in range(groups):
        out = jnp.zeros((GROUP, LANES), F32)
        for value in (0, 1):
            both = acc[group, 2 * value * side : (2 * value + 1) * side] + acc[group, (2 * value + 1) * side : (2 * value + 2) * side]
            both = jnp.where(same, both, 0.0)
            for h in range(HIGH):
                place = (target == source + (h * LOW + value * LEAVES)).astype(F32)
                out = out + jnp.dot(
                    both[h * GROUP : (h + 1) * GROUP], place, precision=lax.Precision.HIGHEST, preferred_element_type=F32
                )
        sums[group * GROUP : (group + 1) * GROUP, :] = out


def update_body(pred, leaf, sums, new_pred, leaf_weights):
    rows, length = pred.shape
    both = sums[...]
    table = -both / (pltpu.roll(both, LANES - LEAVES, 1) + 1.0)
    leaf_weights[...] = table[:, :LEAVES]
    step = min(length, 512)

    def one(turn, carry):
        for k in range(step // LANES):
            at = pl.ds(pl.multiple_of(turn * step + k * LANES, LANES), LANES)
            new_pred[:, at] = pred[:, at] + take(table, leaf[:, at])
        return carry

    lax.fori_loop(0, length // step, one, 0)


def across(total, axis, fold_pairs):
    size = lax.axis_size(axis)
    mate = lax.ppermute(total, axis, [(i, i ^ 1) for i in range(size)])
    both = total + mate
    rest = [lax.ppermute(both, axis, [(i, i ^ d) for i in range(size)]) for d in range(2, size, 2)]
    return both, [mate] + rest


def masks_for(axis, later):
    size = lax.axis_size(axis)
    place = lax.axis_index(axis)
    others = [place ^ 1] + [place ^ d for d in range(2, size, 2)]
    wanted = [(o > place) if later else (o < place) for o in others]
    return jnp.stack(wanted).astype(F32)


def on_device(predictions, leaf_index, events, tie_start):
    rows, length = predictions.shape
    blocks = length // LANES
    parts = lax.axis_size("ep")
    place = lax.axis_index("ep")
    share = length // parts
    wide = (rows, length)
    pred = near(predictions)
    leaf = near(leaf_index)
    observed = near(events)
    tie = tie_start.reshape(blocks, LANES)
    later_masks = masks_for("tm", True)
    earlier_masks = masks_for("tm", False)
    starts = jnp.stack([(place ^ d) * share for d in range(parts)]).astype(jnp.int32)

    weight, total = call(weights_body, [resident(wide, F32), resident((rows, LANES), F32)], pred, name="weights")
    _, from_others = across(total, "tm", True)
    risk, last = call(
        risk_body,
        [resident(wide, F32), resident((blocks, LANES), jnp.int32)],
        weight,
        tie,
        scratch=[pltpu.VMEM((blocks, LANES), jnp.int32)],
        name="risk",
    )
    inv, totals = call(
        functools.partial(inverse_body, len(from_others)),
        [resident(wide, F32), resident((2 * rows, LANES), F32)],
        later_masks,
        *from_others,
        risk,
        observed,
        name="inverse",
    )
    _, from_earlier = across(totals, "tm", True)
    local_one, local_two = call(accum_body, [resident(wide, F32)] * 2, inv, last, name="accum")
    *pieces, bases = call(
        functools.partial(pieces_body, len(from_earlier), parts),
        [resident((2, rows, share), BF16)] * parts + [resident((2 * rows, LANES), F32)],
        earlier_masks,
        starts,
        *from_earlier,
        weight,
        observed,
        local_one,
        local_two,
        name="pieces",
    )
    received = [pieces[0]]
    for d in range(1, parts):
        received.append(lax.ppermute(pieces[d], "ep", [(i, i ^ d) for i in range(parts)]))
    (partial_sums,) = call(
        leaf_sums_body,
        [resident((rows, LANES), F32)],
        leaf,
        weight,
        observed,
        local_one,
        local_two,
        bases,
        scratch=[pltpu.VMEM((rows // GROUP, 4 * HIGH * GROUP, LOW * GROUP), F32)],
        name="leaf_sums",
    )
    both, others = across(partial_sums, "tm", True)
    sums = [both] + others[1:]
    while len(sums) > 1:
        sums = [a + b for a, b in zip(sums[::2], sums[1::2])]
    sums = sums[0]
    new_pred, leaf_weights = call(
        update_body,
        [jax.ShapeDtypeStruct(wide, F32), jax.ShapeDtypeStruct((rows, LEAVES), F32)],
        pred,
        leaf,
        sums,
        name="update",
    )
    grad_hess = jnp.zeros((2, rows * parts, 1, share), BF16)
    for d in range(parts):
        grad_hess = lax.dynamic_update_slice(grad_hess, received[d][:, :, None, :], (0, (place ^ d) * rows, 0, 0))
    return new_pred, leaf_weights, grad_hess


def solution(mesh):
    placed = (P("ep", "tm"), P("ep", "tm"), P("ep", "tm"), P("tm"))
    return jax.shard_map(
        on_device,
        mesh=mesh,
        in_specs=placed,
        out_specs=(P("ep", "tm"), P("ep", None), P(None, None, "tm", "ep")),
        check_vma=False,
    )
```

profile of v0, /device:TPU:0, one launch (start us, length us, event | category | flops | bytes accessed | tf_op | source)
XLA Modules:
  0.0 126.8 jit_solution(4083240600038005740)
XLA Ops:
  0.6 2.2 %copy-done.5 = f32[32,32768]{1,0:T(8,128)S(1)} copy-done((f32[32,32768]{1,0:T(8,128)S(1)}, f32[32,32768]{1,0:T(8,128)}, u32[]{:S(2)}) %copy-start.5) | copy-done | bytes 4194328
  2.8 0.8 weights.1
  3.7 2.0 %copy-done.2 = f32[32,32768]{1,0:T(8,128)} copy-done((f32[32,32768]{1,0:T(8,128)}, f32[32,32768]{1,0:T(8,128)S(1)}, u32[]{:S(2)}) %copy-start.2) | copy-done | bytes 4194328
  6.1 0.8 collective-permute-done.refs_1_
  7.0 2.9 %collective-permute-start.1 = (f32[32,128]{1,0:T(8,128)S(1)}, f32[32,128]{1,0:T(8,128)S(1)}, u32[]{:S(2)}, u32[]{:S(2)}) collective-permute-start(f32[32,128]{1,0:T(8,128)S(1)} %add.30), channel_id=1, source_target_pairs={{0,2},{1,3},{2,0},{3,1},{4,6},{5,7},{6,4},{7,5},{8,10},{9,11},{10,... | collective-permute-start | bytes 49160 | tf_op jit(solution)/shard_map/ppermute | solution.py:286
  9.9 2.6 %collective-permute-start.2 = (f32[32,128]{1,0:T(8,128)S(1)}, f32[32,128]{1,0:T(8,128)S(1)}, u32[]{:S(2)}, u32[]{:S(2)}) collective-permute-start(f32[32,128]{1,0:T(8,128)S(1)} %add.30), channel_id=1, source_target_pairs={{0,4},{1,5},{2,6},{3,7},{4,0},{5,1},{6,2},{7,3},{8,12},{9,13},{10,... | collective-permute-start | bytes 49160 | tf_op jit(solution)/shard_map/ppermute | solution.py:286
  12.6 2.3 %copy-done.3 = f32[32,32768]{1,0:T(8,128)S(1)} copy-done((f32[32,32768]{1,0:T(8,128)S(1)}, f32[32,32768]{1,0:T(8,128)}, u32[]{:S(2)}) %copy-start.3) | copy-done | bytes 4194328
  14.9 8.0 %risk.1 = (f32[32,32768]{1,0:T(8,128)S(1)}, s32[256,128]{1,0:T(8,128)S(1)}) custom-call(f32[32,32768]{1,0:T(8,128)S(1)} %copy-done.3, s32[256,128]{1,0:T(8,128)S(1)} %bitcast.29), custom_call_target="tpu_custom_call" | custom-call | tf_op jit(solution)/shard_map/risk/pallas_call | solution.py:29
  22.9 2.2 %inverse.1 = (f32[32,32768]{1,0:T(8,128)S(1)}, f32[64,128]{1,0:T(8,128)S(1)}) custom-call(f32[4]{0:T(128)S(1)} %add_convert_fusion.refs_0_, f32[32,128]{1,0:T(8,128)S(1)} %collective-permute-done.refs_1_, f32[32,128]{1,0:T(8,128)S(1)} %collective-permute-done.1.refs_2_, f32[32,128]{1,0:T(8,128)S(1)} %collective-permute-done.2.refs_3_, ...), custom_call_target="tpu_custom_call" | custom-call | tf_op jit(solution)/shard_map/inverse/pallas_call | solution.py:29
  25.1 2.0 %copy-done.9 = f32[32,32768]{1,0:T(8,128)} copy-done((f32[32,32768]{1,0:T(8,128)}, f32[32,32768]{1,0:T(8,128)S(1)}, u32[]{:S(2)}) %copy-start.9) | copy-done | bytes 4194328
  27.2 1.1 collective-permute-done.4.refs_2_
  28.3 0.9 collective-permute-start.5
  29.2 3.5 %collective-permute-start.6 = (f32[64,128]{1,0:T(8,128)S(1)}, f32[64,128]{1,0:T(8,128)S(1)}, u32[]{:S(2)}, u32[]{:S(2)}) collective-permute-start(f32[64,128]{1,0:T(8,128)S(1)} %add.31), channel_id=1, source_target_pairs={{0,4},{1,5},{2,6},{3,7},{4,0},{5,1},{6,2},{7,3},{8,12},{9,13},{10,... | collective-permute-start | bytes 98312 | tf_op jit(solution)/shard_map/ppermute | solution.py:286
  32.8 2.2 %copy-done.10 = f32[32,32768]{1,0:T(8,128)S(1)} copy-done((f32[32,32768]{1,0:T(8,128)S(1)}, f32[32,32768]{1,0:T(8,128)}, u32[]{:S(2)}) %copy-start.10) | copy-done | bytes 4194328
  35.0 11.9 %accum.1 = (f32[32,32768]{1,0:T(8,128)S(1)}, f32[32,32768]{1,0:T(8,128)S(1)}) custom-call(f32[32,32768]{1,0:T(8,128)S(1)} %copy-done.10, s32[256,128]{1,0:T(8,128)S(1)} %get-tuple-element.22.last), custom_call_target="tpu_custom_call" | custom-call | tf_op jit(solution)/shard_map/accum/pallas_call | solution.py:29
  46.9 2.2 %copy-done.4 = f32[32,32768]{1,0:T(8,128)S(1)} copy-done((f32[32,32768]{1,0:T(8,128)S(1)}, f32[32,32768]{1,0:T(8,128)}, u32[]{:S(2)}) %copy-start.4) | copy-done | bytes 4194328
  49.1 2.5 %pieces.1 = (bf16[2,32,8192]{2,1,0:T(8,128)(2,1)S(1)}, bf16[2,32,8192]{2,1,0:T(8,128)(2,1)S(1)}, bf16[2,32,8192]{2,1,0:T(8,128)(2,1)S(1)}, bf16[2,32,8192]{2,1,0:T(8,128)(2,1)S(1)}, f32[64,128]{1,0:T(8,128)S(1)}) custom-call(f32[4]{0:T(128)S(1)} %add_convert_fusion.1.refs_0_, s32[4]{0:T(128)S(1)} %pad_add_fusion.refs_1_, ...), custom_call_target="tpu_custom_call" | custom-call | tf_op jit(solution)/shard_map/pieces/pallas_call | solution.py:29
  51.6 23.5 %leaf_sums.1 = f32[32,128]{1,0:T(8,128)S(1)} custom-call(s32[32,32768]{1,0:T(8,128)S(1)} %copy-done.7, f32[32,32768]{1,0:T(8,128)S(1)} %copy-done.4, s32[32,32768]{1,0:T(8,128)S(1)} %copy-done.1, f32[32,32768]{1,0:T(8,128)S(1)} %get-tuple-element.23.refs_8_.local_one, f32[32,32768]{1,0:T(8,128)S(1)} %get-tuple-element.24.refs_9_.local_two, ...), custom_call_target="tpu_custom_call" | custom-call | tf_op jit(solution)/shard_map/leaf_sums/pallas_call | solution.py:29
  75.2 1.8 %collective-permute-start.12 = (bf16[2,32,8192]{2,1,0:T(8,128)(2,1)}, bf16[2,32,8192]{2,1,0:T(8,128)(2,1)S(1)}, u32[]{:S(2)}, u32[]{:S(2)}) collective-permute-start(bf16[2,32,8192]{2,1,0:T(8,128)(2,1)} %copy-done.12), channel_id=1, source_target_pairs={{0,8},{8,0},{16,24},{24,16},{1,9},{9,1},{17,25},{25,17},{2,10},{10... | collective-permute-start | bytes 3145736 | tf_op jit(solution)/shard_map/ppermute | solution.py:348
  76.9 1.5 %collective-permute-start.13 = (bf16[2,32,8192]{2,1,0:T(8,128)(2,1)S(1)}, bf16[2,32,8192]{2,1,0:T(8,128)(2,1)S(1)}, u32[]{:S(2)}, u32[]{:S(2)}) collective-permute-start(bf16[2,32,8192]{2,1,0:T(8,128)(2,1)S(1)} %get-tuple-element.31), channel_id=1, source_target_pairs={{0,16},{8,24},{16,0},{24,8},{1,17},{9,25},{17,1},{25,9},{2,18},{10... | collective-permute-start | bytes 3145736 | tf_op jit(solution)/shard_map/ppermute | solution.py:348
  78.5 1.4 %collective-permute-start.10 = (f32[32,128]{1,0:T(8,128)S(1)}, f32[32,128]{1,0:T(8,128)S(1)}, u32[]{:S(2)}, u32[]{:S(2)}) collective-permute-start(f32[32,128]{1,0:T(8,128)S(1)} %add.32), channel_id=1, source_target_pairs={{0,4},{1,5},{2,6},{3,7},{4,0},{5,1},{6,2},{7,3},{8,12},{9,13},{10,... | collective-permute-start | bytes 49160 | tf_op jit(solution)/shard_map/ppermute | solution.py:286
  79.8 2.4 %collective-permute-start.11 = (f32[32,128]{1,0:T(8,128)S(1)}, f32[32,128]{1,0:T(8,128)S(1)}, u32[]{:S(2)}, u32[]{:S(2)}) collective-permute-start(f32[32,128]{1,0:T(8,128)S(1)} %add.32), channel_id=1, source_target_pairs={{0,6},{1,7},{2,4},{3,5},{4,2},{5,3},{6,0},{7,1},{8,14},{9,15},{10,... | collective-permute-start | bytes 49160 | tf_op jit(solution)/shard_map/ppermute | solution.py:286
  82.2 0.5 collective-permute-start.9
  83.3 0.5 collective-permute-start.14
  83.8 1.5 %collective-permute-done.11 = f32[32,128]{1,0:T(8,128)S(1)} collective-permute-done((f32[32,128]{1,0:T(8,128)S(1)}, f32[32,128]{1,0:T(8,128)S(1)}, u32[]{:S(2)}, u32[]{:S(2)}) %collective-permute-start.11) | collective-permute-done | bytes 16416 | tf_op jit(solution)/shard_map/ppermute | solution.py:286
  85.4 0.6 collective-permute-done.9
  86.0 2.2 %copy-done.8 = s32[32,32768]{1,0:T(8,128)S(1)} copy-done((s32[32,32768]{1,0:T(8,128)S(1)}, s32[32,32768]{1,0:T(8,128)}, u32[]{:S(2)}) %copy-start.8) | copy-done | bytes 4194328
  88.2 9.2 %update.1 = (f32[32,32768]{1,0:T(8,128)}, f32[32,64]{1,0:T(8,128)}) custom-call(f32[32,32768]{1,0:T(8,128)S(1)} %copy-done.6, s32[32,32768]{1,0:T(8,128)S(1)} %copy-done.8, f32[32,128]{1,0:T(8,128)S(1)} %add_add_fusion.sums), custom_call_target="tpu_custom_call" | custom-call | tf_op jit(solution)/shard_map/update/pallas_call | solution.py:29
  97.4 4.0 %collective-permute-done.12 = bf16[2,32,8192]{2,1,0:T(8,128)(2,1)S(1)} collective-permute-done((bf16[2,32,8192]{2,1,0:T(8,128)(2,1)}, bf16[2,32,8192]{2,1,0:T(8,128)(2,1)S(1)}, u32[]{:S(2)}, u32[]{:S(2)}) %collective-permute-start.12) | collective-permute-done | bytes 1048608 | tf_op jit(solution)/shard_map/ppermute | solution.py:348
  101.5 22.2 %collective-permute-done.13 = bf16[2,32,8192]{2,1,0:T(8,128)(2,1)S(1)} collective-permute-done((bf16[2,32,8192]{2,1,0:T(8,128)(2,1)S(1)}, bf16[2,32,8192]{2,1,0:T(8,128)(2,1)S(1)}, u32[]{:S(2)}, u32[]{:S(2)}) %collective-permute-start.13) | collective-permute-done | bytes 1048608 | tf_op jit(solution)/shard_map/ppermute | solution.py:348
  123.8 0.8 collective-permute-done.14
  124.7 2.0 %copy-done.13 = bf16[2,128,1,8192]{3,1,2,0:T(8,128)(2,1)} copy-done((bf16[2,128,1,8192]{3,1,2,0:T(8,128)(2,1)}, bf16[2,128,1,8192]{3,1,2,0:T(8,128)(2,1)S(1)}, u32[]{:S(2)}) %copy-start.13) | copy-done | bytes 4194328
  (45 shorter events, 1.7 us)
Async XLA Ops:
  0.6 2.2 %copy-start.5 = (f32[32,32768]{1,0:T(8,128)S(1)}, f32[32,32768]{1,0:T(8,128)}, u32[]{:S(2)}) copy-start(f32[32,32768]{1,0:T(8,128)} %pred_.3) | copy-start | bytes 12582916
  2.8 9.7 %copy-start.11 = (s32[32768]{0:T(1024)S(1)}, s32[32768]{0:T(1024)}, u32[]{:S(2)}) copy-start(s32[32768]{0:T(1024)} %param.7) | copy-start | bytes 393220
  3.7 2.0 %copy-start.2 = (f32[32,32768]{1,0:T(8,128)}, f32[32,32768]{1,0:T(8,128)S(1)}, u32[]{:S(2)}) copy-start(f32[32,32768]{1,0:T(8,128)S(1)} %get-tuple-element.18.weight.refs_6_) | copy-start | bytes 12582916
  5.7 1.3 %collective-permute-start = (f32[32,128]{1,0:T(8,128)S(1)}, f32[32,128]{1,0:T(8,128)S(1)}, u32[]{:S(2)}, u32[]{:S(2)}) collective-permute-start(f32[32,128]{1,0:T(8,128)S(1)} %get-tuple-element.19), channel_id=1, source_target_pairs={{0,1},{1,0},{2,3},{3,2},{4,5},{5,4},{6,7},{7,6},{8,9},{9,8},{10,11... | collective-permute-start | bytes 49160 | tf_op jit(solution)/shard_map/ppermute | solution.py:284
  7.0 15.9 %collective-permute-start.1 = (f32[32,128]{1,0:T(8,128)S(1)}, f32[32,128]{1,0:T(8,128)S(1)}, u32[]{:S(2)}, u32[]{:S(2)}) collective-permute-start(f32[32,128]{1,0:T(8,128)S(1)} %add.30), channel_id=1, source_target_pairs={{0,2},{1,3},{2,0},{3,1},{4,6},{5,7},{6,4},{7,5},{8,10},{9,11},{10,... | collective-permute-start | bytes 49160 | tf_op jit(solution)/shard_map/ppermute | solution.py:286
  9.9 13.0 %collective-permute-start.2 = (f32[32,128]{1,0:T(8,128)S(1)}, f32[32,128]{1,0:T(8,128)S(1)}, u32[]{:S(2)}, u32[]{:S(2)}) collective-permute-start(f32[32,128]{1,0:T(8,128)S(1)} %add.30), channel_id=1, source_target_pairs={{0,4},{1,5},{2,6},{3,7},{4,0},{5,1},{6,2},{7,3},{8,12},{9,13},{10,... | collective-permute-start | bytes 49160 | tf_op jit(solution)/shard_map/ppermute | solution.py:286
  12.5 10.4 %collective-permute-start.3 = (f32[32,128]{1,0:T(8,128)S(1)}, f32[32,128]{1,0:T(8,128)S(1)}, u32[]{:S(2)}, u32[]{:S(2)}) collective-permute-start(f32[32,128]{1,0:T(8,128)S(1)} %add.30), channel_id=1, source_target_pairs={{0,6},{1,7},{2,4},{3,5},{4,2},{5,3},{6,0},{7,1},{8,14},{9,15},{10,... | collective-permute-start | bytes 49160 | tf_op jit(solution)/shard_map/ppermute | solution.py:286
  12.5 10.3 %copy-start = (s32[32,32768]{1,0:T(8,128)S(1)}, s32[32,32768]{1,0:T(8,128)}, u32[]{:S(2)}) copy-start(s32[32,32768]{1,0:T(8,128)} %events.1) | copy-start | bytes 12582916
  12.6 2.3 %copy-start.3 = (f32[32,32768]{1,0:T(8,128)S(1)}, f32[32,32768]{1,0:T(8,128)}, u32[]{:S(2)}) copy-start(f32[32,32768]{1,0:T(8,128)} %copy-done.2) | copy-start | bytes 12582916
  25.1 2.0 %copy-start.9 = (f32[32,32768]{1,0:T(8,128)}, f32[32,32768]{1,0:T(8,128)S(1)}, u32[]{:S(2)}) copy-start(f32[32,32768]{1,0:T(8,128)S(1)} %get-tuple-element.21.inv) | copy-start | bytes 12582916
  27.1 1.2 collective-permute-start.4
  27.2 19.7 %copy-start.1 = (s32[32,32768]{1,0:T(8,128)S(1)}, s32[32,32768]{1,0:T(8,128)}, u32[]{:S(2)}) copy-start(s32[32,32768]{1,0:T(8,128)} %events.1) | copy-start | bytes 12582916
  28.3 18.5 %collective-permute-start.5 = (f32[64,128]{1,0:T(8,128)S(1)}, f32[64,128]{1,0:T(8,128)S(1)}, u32[]{:S(2)}, u32[]{:S(2)}) collective-permute-start(f32[64,128]{1,0:T(8,128)S(1)} %add.31), channel_id=1, source_target_pairs={{0,2},{1,3},{2,0},{3,1},{4,6},{5,7},{6,4},{7,5},{8,10},{9,11},{10,... | collective-permute-start | bytes 98312 | tf_op jit(solution)/shard_map/ppermute | solution.py:286
  29.2 17.6 %collective-permute-start.6 = (f32[64,128]{1,0:T(8,128)S(1)}, f32[64,128]{1,0:T(8,128)S(1)}, u32[]{:S(2)}, u32[]{:S(2)}) collective-permute-start(f32[64,128]{1,0:T(8,128)S(1)} %add.31), channel_id=1, source_target_pairs={{0,4},{1,5},{2,6},{3,7},{4,0},{5,1},{6,2},{7,3},{8,12},{9,13},{10,... | collective-permute-start | bytes 98312 | tf_op jit(solution)/shard_map/ppermute | solution.py:286
  32.7 14.2 %collective-permute-start.7 = (f32[64,128]{1,0:T(8,128)S(1)}, f32[64,128]{1,0:T(8,128)S(1)}, u32[]{:S(2)}, u32[]{:S(2)}) collective-permute-start(f32[64,128]{1,0:T(8,128)S(1)} %add.31), channel_id=1, source_target_pairs={{0,6},{1,7},{2,4},{3,5},{4,2},{5,3},{6,0},{7,1},{8,14},{9,15},{10,... | collective-permute-start | bytes 98312 | tf_op jit(solution)/shard_map/ppermute | solution.py:286
  32.8 2.2 %copy-start.10 = (f32[32,32768]{1,0:T(8,128)S(1)}, f32[32,32768]{1,0:T(8,128)}, u32[]{:S(2)}) copy-start(f32[32,32768]{1,0:T(8,128)} %copy-done.9) | copy-start | bytes 12582916
  46.9 2.2 %copy-start.4 = (f32[32,32768]{1,0:T(8,128)S(1)}, f32[32,32768]{1,0:T(8,128)}, u32[]{:S(2)}) copy-start(f32[32,32768]{1,0:T(8,128)} %copy-done.2) | copy-start | bytes 12582916
  49.1 2.5 %copy-start.7 = (s32[32,32768]{1,0:T(8,128)S(1)}, s32[32,32768]{1,0:T(8,128)}, u32[]{:S(2)}) copy-start(s32[32,32768]{1,0:T(8,128)} %leaf.3) | copy-start | bytes 12582916
  51.6 23.5 %copy-start.12 = (bf16[2,32,8192]{2,1,0:T(8,128)(2,1)}, bf16[2,32,8192]{2,1,0:T(8,128)(2,1)S(1)}, u32[]{:S(2)}) copy-start(bf16[2,32,8192]{2,1,0:T(8,128)(2,1)S(1)} %get-tuple-element.30) | copy-start | bytes 3145732
  75.1 3.4 %collective-permute-start.8 = (f32[32,128]{1,0:T(8,128)S(1)}, f32[32,128]{1,0:T(8,128)S(1)}, u32[]{:S(2)}, u32[]{:S(2)}) collective-permute-start(f32[32,128]{1,0:T(8,128)S(1)} %leaf_sums.1), channel_id=1, source_target_pairs={{0,1},{1,0},{2,3},{3,2},{4,5},{5,4},{6,7},{7,6},{8,9},{9,8},{10,11... | collective-permute-start | bytes 49160 | tf_op jit(solution)/shard_map/ppermute | solution.py:284
  75.2 10.8 %copy-start.6 = (f32[32,32768]{1,0:T(8,128)S(1)}, f32[32,32768]{1,0:T(8,128)}, u32[]{:S(2)}) copy-start(f32[32,32768]{1,0:T(8,128)} %pred_.3) | copy-start | bytes 12582916
  75.2 26.2 %collective-permute-start.12 = (bf16[2,32,8192]{2,1,0:T(8,128)(2,1)}, bf16[2,32,8192]{2,1,0:T(8,128)(2,1)S(1)}, u32[]{:S(2)}, u32[]{:S(2)}) collective-permute-start(bf16[2,32,8192]{2,1,0:T(8,128)(2,1)} %copy-done.12), channel_id=1, source_target_pairs={{0,8},{8,0},{16,24},{24,16},{1,9},{9,1},{17,25},{25,17},{2,10},{10... | collective-permute-start | bytes 3145736 | tf_op jit(solution)/shard_map/ppermute | solution.py:348
  76.9 46.7 %collective-permute-start.13 = (bf16[2,32,8192]{2,1,0:T(8,128)(2,1)S(1)}, bf16[2,32,8192]{2,1,0:T(8,128)(2,1)S(1)}, u32[]{:S(2)}, u32[]{:S(2)}) collective-permute-start(bf16[2,32,8192]{2,1,0:T(8,128)(2,1)S(1)} %get-tuple-element.31), channel_id=1, source_target_pairs={{0,16},{8,24},{16,0},{24,8},{1,17},{9,25},{17,1},{25,9},{2,18},{10... | collective-permute-start | bytes 3145736 | tf_op jit(solution)/shard_map/ppermute | solution.py:348
  78.5 4.8 %collective-permute-start.10 = (f32[32,128]{1,0:T(8,128)S(1)}, f32[32,128]{1,0:T(8,128)S(1)}, u32[]{:S(2)}, u32[]{:S(2)}) collective-permute-start(f32[32,128]{1,0:T(8,128)S(1)} %add.32), channel_id=1, source_target_pairs={{0,4},{1,5},{2,6},{3,7},{4,0},{5,1},{6,2},{7,3},{8,12},{9,13},{10,... | collective-permute-start | bytes 49160 | tf_op jit(solution)/shard_map/ppermute | solution.py:286
  79.8 5.5 %collective-permute-start.11 = (f32[32,128]{1,0:T(8,128)S(1)}, f32[32,128]{1,0:T(8,128)S(1)}, u32[]{:S(2)}, u32[]{:S(2)}) collective-permute-start(f32[32,128]{1,0:T(8,128)S(1)} %add.32), channel_id=1, source_target_pairs={{0,6},{1,7},{2,4},{3,5},{4,2},{5,3},{6,0},{7,1},{8,14},{9,15},{10,... | collective-permute-start | bytes 49160 | tf_op jit(solution)/shard_map/ppermute | solution.py:286
  82.2 3.7 %collective-permute-start.9 = (f32[32,128]{1,0:T(8,128)S(1)}, f32[32,128]{1,0:T(8,128)S(1)}, u32[]{:S(2)}, u32[]{:S(2)}) collective-permute-start(f32[32,128]{1,0:T(8,128)S(1)} %add.32), channel_id=1, source_target_pairs={{0,2},{1,3},{2,0},{3,1},{4,6},{5,7},{6,4},{7,5},{8,10},{9,11},{10,... | collective-permute-start | bytes 49160 | tf_op jit(solution)/shard_map/ppermute | solution.py:286
  83.3 41.3 %collective-permute-start.14 = (bf16[2,32,8192]{2,1,0:T(8,128)(2,1)S(1)}, bf16[2,32,8192]{2,1,0:T(8,128)(2,1)S(1)}, u32[]{:S(2)}, u32[]{:S(2)}) collective-permute-start(bf16[2,32,8192]{2,1,0:T(8,128)(2,1)S(1)} %get-tuple-element.32), channel_id=1, source_target_pairs={{0,24},{8,16},{16,8},{24,0},{1,25},{9,17},{17,9},{25,1},{2,26},{10... | collective-permute-start | bytes 3145736 | tf_op jit(solution)/shard_map/ppermute | solution.py:348
  86.0 2.2 %copy-start.8 = (s32[32,32768]{1,0:T(8,128)S(1)}, s32[32,32768]{1,0:T(8,128)}, u32[]{:S(2)}) copy-start(s32[32,32768]{1,0:T(8,128)} %leaf.3) | copy-start | bytes 12582916
  124.7 2.0 %copy-start.13 = (bf16[2,128,1,8192]{3,1,2,0:T(8,128)(2,1)}, bf16[2,128,1,8192]{3,1,2,0:T(8,128)(2,1)S(1)}, u32[]{:S(2)}) copy-start(bf16[2,128,1,8192]{3,1,2,0:T(8,128)(2,1)S(1)} %bitcast_dynamic-update-slice_fusion) | copy-start | bytes 12582916
where the time goes:
time: 127 us
  Pallas kernels  58 us (46%)
  waiting for transfers between devices  31.1 us (24%)
  starting transfers between devices  18.5 us (15%)
  local copies, waits for them, and re-layouts  18 us (14%)
    pallas_call x7, Pallas kernels, call(): pl.pallas_call(body, out_shape=outs, in_specs=[smem if a.ndim == 1 else s...  58 us
    ppermute x3, waiting for transfers between devices, on_device(): lax.ppermute(pieces[d], 'ep', [(i, i ^ d) for i in range(parts)])  27.1 us
    unnamed x28, local copies, waits for them, and re-layouts  17.1 us
    ppermute x9, starting transfers between devices, across(): lax.ppermute(both, axis, [(i, i ^ d) for i in range(size)])  14.1 us
    ppermute x3, starting transfers between devices, on_device(): lax.ppermute(pieces[d], 'ep', [(i, i ^ d) for i in range(parts)])  3.85 us
  transfers between devices with their start and end apart: 15, of which 7 were waited for; matrix products, arithmetic and copies ran while one was open for 1% of the time, Pallas kernels for 23%

commit v1 on v0

v1 whole, which is shorter than its diff:
```python
import functools

import jax
import jax.numpy as jnp
from jax import lax
from jax.experimental import pallas as pl
from jax.experimental.pallas import tpu as pltpu
from jax.sharding import PartitionSpec as P

LEAVES = 64
LANES = 128
WIDE = 256
F32 = jnp.float32
BF16 = jnp.bfloat16
I16 = jnp.int16
CODE = 32766.0 / 6.0
MIB = 1024 * 1024


def resident(shape, dtype):
    return pltpu.VMEM(shape, dtype)


def near(array):
    return pltpu.with_memory_space_constraint(array, pltpu.VMEM)


def call(body, outs, *args, scratch=(), name=None, us=1.0, aliases=None, limit=12, hbm=(), hbm_out=()):
    vmem = pl.BlockSpec(memory_space=pltpu.VMEM)
    smem = pl.BlockSpec(memory_space=pltpu.SMEM)
    anywhere = pl.BlockSpec(memory_space=pltpu.HBM)
    return pl.pallas_call(
        body,
        out_shape=outs,
        in_specs=[anywhere if k in hbm else smem if a.ndim == 1 else vmem for k, a in enumerate(args)],
        out_specs=[anywhere if k in hbm_out else vmem for k in range(len(outs))],
        scratch_shapes=list(scratch),
        input_output_aliases=aliases or {},
        compiler_params=pltpu.CompilerParams(vmem_limit_bytes=limit * MIB),
        cost_estimate=pl.CostEstimate(flops=0, bytes_accessed=int(us * 3.5e6), transcendentals=0),
        name=name,
    )(*args)


def lane_sum(x):
    return jnp.broadcast_to(jnp.sum(x, axis=1, keepdims=True), (x.shape[0], LANES))


def fold(x):
    parts = [x[:, k : k + LANES] for k in range(0, x.shape[1], LANES)]
    while len(parts) > 1:
        parts = [a + b for a, b in zip(parts[::2], parts[1::2])] + parts[len(parts) & ~1 :]
    return parts[0]


def span(start, size):
    return pl.ds(pl.multiple_of(start, size), size)


def widen(x, step):
    return jnp.concatenate([x] * (step // LANES), axis=1)


def share_of(meta, d, size):
    return (meta[0] ^ d) * size


def front_body(parts, turns, meta, pred_in, events_in, pred, events, weight, total, *rest):
    messages, sems = rest[: parts - 1], rest[parts - 1]
    rows, length = pred.shape
    width = length // turns

    def copies(turn):
        at = span(turn * width, width)
        return [
            pltpu.make_async_copy(pred_in.at[:, at], pred.at[:, at], sems.at[0, turn]),
            pltpu.make_async_copy(events_in.at[:, at], events.at[:, at], sems.at[1, turn]),
        ]

    for turn in range(turns):
        for copy in copies(turn):
            copy.start()
    step = min(width, 1024)
    acc = jnp.zeros((rows, LANES), F32)
    for turn in range(turns):
        for copy in copies(turn):
            copy.wait()

        def one(k, acc):
            at = span(turn * width + k * step, step)
            value = jnp.exp(pred[:, at])
            weight[:, at] = value
            return acc + fold(value)

        acc = lax.fori_loop(0, width // step, one, acc, unroll=2)
    total[...] = lane_sum(acc)
    share = length // parts
    for d in range(1, parts):

        def code(k, carry):
            source = span(share_of(meta, d, share) + k * step, step)
            at = span(k * step, step)
            messages[d - 1][0, :, at] = jnp.round(pred[:, source] * CODE).astype(jnp.int32).astype(I16)
            messages[d - 1][1, :, at] = events[:, source].astype(I16)
            return carry

        lax.fori_loop(0, share // step, code, 0, unroll=2)


def pair_dot(x, matrix):
    high = x.astype(BF16)
    low = (x - high.astype(F32)).astype(BF16)
    return jnp.dot(high, matrix, preferred_element_type=F32) + jnp.dot(low, matrix, preferred_element_type=F32)


def take(x, index):
    return jnp.take_along_axis(x, index, axis=1, mode="promise_in_bounds")


def last_in_group(starts):
    lane = lax.broadcasted_iota(jnp.int32, starts.shape, 1)
    after = pltpu.roll(starts, LANES - 1, 1)
    best = jnp.where((after == 1) | (lane == LANES - 1), lane, LANES - 1)
    for shift in (1, 2, 4, 8, 16, 32, 64):
        moved = pltpu.roll(best, LANES - shift, 1)
        best = jnp.where(lane < LANES - shift, jnp.minimum(best, moved), best)
    return best


def triangle(backward):
    above = lax.broadcasted_iota(jnp.int32, (WIDE, WIDE), 0)
    along = lax.broadcasted_iota(jnp.int32, (WIDE, WIDE), 1)
    return (above >= along if backward else above <= along).astype(BF16)


def stacked(ref, base, count):
    return jnp.concatenate([ref[:, span(base + k * WIDE, WIDE)] for k in range(count)], axis=0)


def group_events(observed, counts, first, last):
    return jnp.where(first == 1, take(counts, last) - counts + observed, 0.0)


def scan_body(weight, events, tie, leaf_in, suffix, grouped, last, leaf, upper, lower, sem):
    rows, length = weight.shape
    fetch = pltpu.make_async_copy(leaf_in, leaf, sem)
    fetch.start()
    count = min(16, length // WIDE)
    last[...] = last_in_group(tie[...])
    upper[...] = triangle(True)
    lower[...] = triangle(False)
    steps = length // (WIDE * count)

    def one(turn, carry):
        base = (steps - 1 - turn) * (WIDE * count)
        observed = stacked(events, base, count).astype(F32)
        counts = jnp.dot(observed.astype(BF16), lower[...], preferred_element_type=F32)
        summed = pair_dot(stacked(weight, base, count), upper[...])
        for k in range(count - 1, -1, -1):
            mine = slice(k * rows, (k + 1) * rows)
            for half in (0, 1):
                lanes = slice(half * LANES, (half + 1) * LANES)
                at = span(base + k * WIDE + half * LANES, LANES)
                block = pl.ds((base + k * WIDE) // LANES + half, 1)
                suffix[:, at] = summed[mine, lanes] + carry
                grouped[:, at] = group_events(
                    observed[mine, lanes],
                    counts[mine, lanes],
                    jnp.broadcast_to(tie[block, :], (rows, LANES)),
                    jnp.broadcast_to(last[block, :], (rows, LANES)),
                )
            carry = carry + jnp.broadcast_to(summed[mine, 0:1], (rows, LANES))
        return carry

    lax.fori_loop(0, steps, one, jnp.zeros((rows, LANES), F32), unroll=2)
    fetch.wait()


def pair_body(left, right, out):
    out[...] = left[...] + right[...]


def gathered_sum(meta, refs, later):
    mine = meta[1]
    out = None
    for k, ref in enumerate(refs):
        other = mine ^ (1 if k == 0 else 2 * k)
        wanted = (other > mine) if later else (other < mine)
        term = ref[...] * wanted.astype(F32)
        out = term if out is None else out + term
    return out


def inverse_body(count, parts, *refs):
    meta, others = refs[0], refs[1 : 1 + count]
    suffix, grouped, inv_one, inv_two, totals, after = refs[1 + count :]
    rows, length = suffix.shape
    share = length // parts
    later = gathered_sum(meta, others, True)
    for part in range(parts - 1):
        after[part] = jnp.broadcast_to(suffix[:, (part + 1) * share : (part + 1) * share + 1], (rows, LANES)) + later
    after[parts - 1] = later
    step = min(length, 512)

    def one(turn, acc):
        sum_one, sum_two = acc
        at = span(turn * step, step)
        inverse = 1.0 / (suffix[:, at] + widen(later, step))
        first = grouped[:, at] * inverse
        second = first * inverse
        inv_one[:, at] = first
        inv_two[:, at] = second
        return (sum_one + fold(first), sum_two + fold(second))

    empty = jnp.zeros((rows, LANES), F32)
    sum_one, sum_two = lax.fori_loop(0, length // step, one, (empty, empty), unroll=2)
    totals[:rows, :] = lane_sum(sum_one)
    totals[rows:, :] = lane_sum(sum_two)


def accum_body(parts, inv_one, inv_two, one_out, two_out, before, lower):
    rows, length = inv_one.shape
    share = length // parts
    count = min(16, share // WIDE)
    lower[...] = triangle(False)
    empty = jnp.zeros((rows, LANES), F32)
    carry = (empty, empty)
    for part in range(parts):
        before[part, :rows] = carry[0]
        before[part, rows:] = carry[1]

        def one(turn, carry):
            base = part * share + turn * (WIDE * count)
            made = []
            for ref, out, so_far in ((inv_one, one_out, carry[0]), (inv_two, two_out, carry[1])):
                summed = pair_dot(stacked(ref, base, count), lower[...])
                for k in range(count):
                    piece = summed[k * rows : (k + 1) * rows]
                    out[:, span(base + k * WIDE, WIDE)] = piece + widen(so_far, WIDE)
                    so_far = so_far + jnp.broadcast_to(piece[:, WIDE - 1 :], (rows, LANES))
                made.append(so_far)
            return tuple(made)

        carry = lax.fori_loop(0, share // (WIDE * count), one, carry, unroll=2)


def bases_body(count, parts, *refs):
    meta, others = refs[0], refs[1 : 1 + count]
    after, before, bases, *messages = refs[1 + count :]
    rows = after.shape[1]
    earlier = gathered_sum(meta, others, False)
    bases[...] = earlier
    for d in range(1, parts):
        part = share_of(meta, d, 1)
        messages[d - 1][:rows] = after[part]
        messages[d - 1][rows:] = before[part] + earlier


def derivatives(weight, observed, accum_one, accum_two):
    scaled = weight * accum_one
    return scaled - observed, scaled - weight * weight * accum_two


def finish_body(partners, with_own, *refs):
    meta, tie, last = refs[:3]
    refs = refs[3:]
    messages, base = refs[: len(partners)], refs[len(partners) : 2 * len(partners)]
    refs = refs[2 * len(partners) :]
    if with_own:
        weight, events, local_one, local_two, own_bases = refs[:5]
        refs = refs[5:]
    else:
        refs = refs[1:]
    out, scratch, kept, inv_one, inv_two, upper, lower, sems = refs
    _, rows, share = kept.shape
    count = min(8, share // WIDE)
    steps = share // (WIDE * count)
    turn_width = WIDE * count
    first_block = share_of(meta, 0, share) // LANES
    upper[...] = triangle(True)
    lower[...] = triangle(False)
    places = list(partners) + ([0] if with_own else [])
    copies = []
    for slot, d in enumerate(places):
        where = pl.ds(pl.multiple_of(share_of(meta, d, rows), rows), rows)
        copies += [pltpu.make_async_copy(scratch.at[slot, v], out.at[v, where, :], sems.at[slot, v]) for v in (0, 1)]

    if with_own:
        slot = len(partners)
        step = min(share, 512)

        def own(turn, carry):
            source = span(share_of(meta, 0, share) + turn * step, step)
            at = span(turn * step, step)
            grad, hess = derivatives(
                weight[:, source],
                events[:, source].astype(F32),
                local_one[:, source] + widen(own_bases[:rows, :], step),
                local_two[:, source] + widen(own_bases[rows:, :], step),
            )
            scratch[slot, 0, :, at] = grad.astype(BF16)
            scratch[slot, 1, :, at] = hess.astype(BF16)
            return carry

        lax.fori_loop(0, share // step, own, 0, unroll=2)
        for v in (0, 1):
            copies[2 * slot + v].start()

    def one(turn, carry):
        at_base = (steps - 1 - turn) * turn_width
        made = []
        for slot in range(len(partners)):
            coded = jnp.concatenate([messages[slot][0, :, span(at_base + k * WIDE, WIDE)] for k in range(count)], axis=0)
            values = jnp.exp(coded.astype(jnp.int32).astype(F32) * (1.0 / CODE))
            seen = jnp.concatenate([messages[slot][1, :, span(at_base + k * WIDE, WIDE)] for k in range(count)], axis=0)
            observed = seen.astype(jnp.int32).astype(F32)
            counts = jnp.dot(observed.astype(BF16), lower[...], preferred_element_type=F32)
            summed = pair_dot(values, upper[...])
            so_far = carry[slot]
            for k in range(count - 1, -1, -1):
                mine = slice(k * rows, (k + 1) * rows)
                kept[slot, :, span(at_base + k * WIDE, WIDE)] = values[mine]
                for half in (0, 1):
                    lanes = slice(half * LANES, (half + 1) * LANES)
                    at = span(at_base + k * WIDE + half * LANES, LANES)
                    block = pl.ds(first_block + (at_base + k * WIDE) // LANES + half, 1)
                    inverse = 1.0 / (summed[mine, lanes] + so_far)
                    grouped = group_events(
                        observed[mine, lanes],
                        counts[mine, lanes],
                        jnp.broadcast_to(tie[block, :], (rows, LANES)),
                        jnp.broadcast_to(last[block, :], (rows, LANES)),
                    )
                    inv_one[slot, :, at] = grouped * inverse
                    inv_two[slot, :, at] = grouped * inverse * inverse
                so_far = so_far + jnp.broadcast_to(summed[mine, 0:1], (rows, LANES))
            made.append(so_far)
        return tuple(made)

    lax.fori_loop(0, steps, one, tuple(b[:rows, :] for b in base))

    def two(turn, carry):
        at_base = turn * turn_width
        made = []
        for slot in range(len(partners)):
            sum_one = pair_dot(stacked(inv_one.at[slot], at_base, count), lower[...])
            sum_two = pair_dot(stacked(inv_two.at[slot], at_base, count), lower[...])
            so_one, so_two = carry[slot]
            for k in range(count):
                mine = slice(k * rows, (k + 1) * rows)
                at = span(at_base + k * WIDE, WIDE)
                grad, hess = derivatives(
                    kept[slot, :, at],
                    messages[slot][1, :, at].astype(jnp.int32).astype(F32),
                    sum_one[mine] + widen(so_one, WIDE),
                    sum_two[mine] + widen(so_two, WIDE),
                )
                scratch[slot, 0, :, at] = grad.astype(BF16)
                scratch[slot, 1, :, at] = hess.astype(BF16)
                so_one = so_one + jnp.broadcast_to(sum_one[mine, WIDE - 1 :], (rows, LANES))
                so_two = so_two + jnp.broadcast_to(sum_two[mine, WIDE - 1 :], (rows, LANES))
            made.append((so_one, so_two))
        return tuple(made)

    lax.fori_loop(0, steps, two, tuple((b[rows : 2 * rows, :], b[2 * rows :, :]) for b in base))
    for copy in copies[: 2 * len(partners)]:
        copy.start()
    for copy in copies:
        copy.wait()


GROUP = 16
LOW = 16
HIGH = LEAVES // LOW


def leaf_sums_body(leaf, weight, events, local_one, local_two, bases, sums, acc):
    rows, length = weight.shape
    step = min(length, 1024)
    groups = rows // GROUP
    acc[...] = jnp.zeros_like(acc)

    def one(turn, carry):
        at = span(turn * step, step)
        for group in range(groups):
            mine = pl.ds(group * GROUP, GROUP)
            pair = derivatives(
                weight[mine, at],
                events[mine, at].astype(F32),
                local_one[mine, at] + widen(bases[mine, :], step),
                local_two[mine, at] + widen(bases[pl.ds(rows + group * GROUP, GROUP), :], step),
            )
            label = leaf[mine, at]
            low = (label & (LOW - 1)).astype(F32).astype(BF16)
            high = lax.shift_right_logical(label, LOW.bit_length() - 1).astype(F32).astype(BF16)
            terms = []
            for value in pair:
                upper = value.astype(BF16)
                terms += [upper, (value - upper.astype(F32)).astype(BF16)]
            zero = jnp.zeros((GROUP, step), BF16)
            unit = jnp.ones((GROUP, step), BF16)
            left = jnp.concatenate([jnp.where(high == h, term, zero) for term in terms for h in range(HIGH)], axis=0)
            right = jnp.concatenate([jnp.where(low == k, unit, zero) for k in range(LOW)], axis=0)
            acc[group] += lax.dot_general(left, right, (((1,), (1,)), ((), ())), preferred_element_type=F32)
        return carry

    lax.fori_loop(0, length // step, one, 0, unroll=4)
    width = LOW * GROUP
    side = HIGH * GROUP
    same = lax.broadcasted_iota(jnp.int32, (side, width), 0) % GROUP == lax.broadcasted_iota(jnp.int32, (side, width), 1) % GROUP
    source = lax.broadcasted_iota(jnp.int32, (width, LANES), 0) // GROUP
    target = lax.broadcasted_iota(jnp.int32, (width, LANES), 1)
    for group in range(groups):
        out = jnp.zeros((GROUP, LANES), F32)
        for value in (0, 1):
            both = acc[group, 2 * value * side : (2 * value + 1) * side] + acc[group, (2 * value + 1) * side : (2 * value + 2) * side]
            both = jnp.where(same, both, 0.0)
            for h in range(HIGH):
                place = (target == source + (h * LOW + value * LEAVES)).astype(F32)
                out = out + jnp.dot(
                    both[h * GROUP : (h + 1) * GROUP], place, precision=lax.Precision.HIGHEST, preferred_element_type=F32
                )
        sums[group * GROUP : (group + 1) * GROUP, :] = out


def update_body(turns, pred, leaf, *refs):
    sums, (new_pred, leaf_weights, scratch, sems) = refs[:-4], refs[-4:]
    rows, length = pred.shape
    both = [ref[...] for ref in sums]
    while len(both) > 1:
        both = [a + b for a, b in zip(both[::2], both[1::2])]
    table = -both[0] / (pltpu.roll(both[0], LANES - LEAVES, 1) + 1.0)
    leaf_weights[...] = table[:, :LEAVES]
    width = length // turns
    step = min(width, 512)
    copies = []
    for turn in range(turns):

        def one(k, carry):
            at = span(turn * width + k * step, step)
            label = leaf[:, at]
            picked = [take(table, label[:, j : j + LANES]) for j in range(0, step, LANES)]
            scratch[:, at] = pred[:, at] + jnp.concatenate(picked, axis=1)
            return carry

        lax.fori_loop(0, width // step, one, 0, unroll=4)
        at = pl.ds(turn * width, width)
        copies.append(pltpu.make_async_copy(scratch.at[:, at], new_pred.at[:, at], sems.at[turn]))
        copies[-1].start()
    for copy in copies:
        copy.wait()


def swap(array, axis, d):
    return lax.ppermute(array, axis, [(i, i ^ d) for i in range(lax.axis_size(axis))])


def across(total, axis):
    mate = swap(total, axis, 1)
    (both,) = call(pair_body, [resident(total.shape, F32)], total, mate, name="pair", us=0.3, limit=2)
    return both, [mate] + [swap(both, axis, d) for d in range(2, lax.axis_size(axis), 2)]


def on_device(predictions, leaf_index, events, tie_start):
    rows, length = predictions.shape
    blocks = length // LANES
    parts = lax.axis_size("ep")
    share = length // parts
    wide = (rows, length)
    turns = 8
    dma = pltpu.SemaphoreType.DMA
    tie = near(tie_start.reshape(blocks, LANES))
    meta = jnp.stack([lax.axis_index("ep"), lax.axis_index("tm")]).astype(jnp.int32)

    pred, observed, weight, total, *messages = call(
        functools.partial(front_body, parts, turns),
        [resident(wide, F32), resident(wide, jnp.int32), resident(wide, F32), resident((rows, LANES), F32)]
        + [resident((2, rows, share), I16)] * (parts - 1),
        meta,
        predictions,
        events,
        hbm=(1, 2),
        scratch=[dma((2, turns))],
        name="front",
        us=4,
    )
    coded = {d: swap(messages[d - 1], "ep", d) for d in range(parts - 1, 0, -1)}
    _, from_later = across(total, "tm")
    suffix, grouped, last, leaf = call(
        scan_body,
        [resident(wide, F32), resident(wide, F32), resident((blocks, LANES), jnp.int32), resident(wide, jnp.int32)],
        weight,
        observed,
        tie,
        leaf_index,
        hbm=(3,),
        scratch=[pltpu.VMEM((WIDE, WIDE), BF16)] * 2 + [dma],
        name="scan",
        us=5,
    )
    count = len(from_later)
    inv_one, inv_two, totals, after = call(
        functools.partial(inverse_body, count, parts),
        [resident(wide, F32), resident(wide, F32), resident((2 * rows, LANES), F32), resident((parts, rows, LANES), F32)],
        meta,
        *from_later,
        suffix,
        grouped,
        aliases={1 + count: 0, 2 + count: 1},
        name="inverse",
        us=1.5,
    )
    _, from_earlier = across(totals, "tm")
    local_one, local_two, before = call(
        functools.partial(accum_body, parts),
        [resident(wide, F32), resident(wide, F32), resident((parts, 2 * rows, LANES), F32)],
        inv_one,
        inv_two,
        aliases={0: 0, 1: 1},
        scratch=[pltpu.VMEM((WIDE, WIDE), BF16)],
        name="accum",
        us=3,
    )
    bases, *sent = call(
        functools.partial(bases_body, count, parts),
        [resident((2 * rows, LANES), F32)] + [resident((3 * rows, LANES), F32)] * (parts - 1),
        meta,
        *from_earlier,
        after,
        before,
        name="bases",
        us=0.5,
    )
    base = {d: swap(sent[d - 1], "ep", d) for d in range(parts - 1, 0, -1)}
    (partial_sums,) = call(
        leaf_sums_body,
        [resident((rows, LANES), F32)],
        leaf,
        weight,
        observed,
        local_one,
        local_two,
        bases,
        scratch=[pltpu.VMEM((rows // GROUP, 4 * HIGH * GROUP, LOW * GROUP), F32)],
        name="leaf_sums",
        us=10,
    )
    both, others = across(partial_sums, "tm")

    def finish(partners, more, out, name, us):
        held = len(partners) + (out is None)
        args = [meta, tie, last, *[coded[d] for d in partners], *[base[d] for d in partners], *more]
        made = [pltpu.VMEM((len(partners), rows, share), F32)] * 3
        return call(
            functools.partial(finish_body, partners, out is None),
            [jax.ShapeDtypeStruct((2, rows * parts, share), BF16)],
            *args,
            *([] if out is None else [out]),
            hbm=() if out is None else (len(args),),
            hbm_out=(0,),
            aliases=None if out is None else {len(args): 0},
            scratch=[pltpu.VMEM((held, 2, rows, share), BF16), *made, *[pltpu.VMEM((WIDE, WIDE), BF16)] * 2, dma((held, 2))],
            name=name,
            us=us,
        )[0]

    first = parts - 1
    grad_hess = finish([first], [weight, observed, local_one, local_two, bases], None, "finish_first", 5)
    new_pred, leaf_weights = call(
        functools.partial(update_body, turns),
        [jax.ShapeDtypeStruct(wide, F32), jax.ShapeDtypeStruct((rows, LEAVES), F32)],
        pred,
        leaf,
        both,
        *others[1:],
        hbm_out=(0,),
        scratch=[pltpu.VMEM(wide, F32), dma((turns,))],
        name="update",
        us=4,
    )
    grad_hess = finish(list(range(1, first)), [], grad_hess, "finish_rest", 6)
    return new_pred, leaf_weights, grad_hess.reshape(2, rows * parts, 1, share)


def solution(mesh):
    placed = (P("ep", "tm"), P("ep", "tm"), P("ep", "tm"), P("tm"))
    return jax.shard_map(
        on_device,
        mesh=mesh,
        in_specs=placed,
        out_specs=(P("ep", "tm"), P("ep", None), P(None, None, "tm", "ep")),
        check_vma=False,
    )
```

time: 127 us -> 88.8 us (0.70)
  Pallas kernels: 58 us -> 43.3 us
  local copies, waits for them, and re-layouts: 18 us -> 4.38 us
  waiting for transfers between devices: 31.1 us -> 19.2 us
  starting transfers between devices: 18.5 us -> 20.8 us
    pallas_call x7 -> x12, Pallas kernels: 58 us -> 43.3 us  [call(): pl.pallas_call(body, out_shape=outs, in_specs=[anywhere if k in hbm else...]
    unnamed x28 -> x8, local copies, waits for them, and re-layouts: 17.1 us -> 4.38 us
    ppermute x15 -> x18, waiting for transfers between devices: 31.1 us -> 19.2 us  [swap(): lax.ppermute(array, axis, [(i, i ^ d) for i in range(lax.axis_size(axis))])]
    ppermute x15 -> x18, starting transfers between devices: 18.5 us -> 20.8 us  [swap(): lax.ppermute(array, axis, [(i, i ^ d) for i in range(lax.axis_size(axis))])]
  transfers between devices with their start and end apart: 15 -> 18, of which waited for: 7 -> 8; matrix products, arithmetic and copies ran while one was open for 1% -> 0% of each run, Pallas kernels for 23% -> 38%
where the time goes in v1:
time: 88.8 us; the launch traced here: 88.6 us
  Pallas kernels  43.3 us (49%)
  starting transfers between devices  20.8 us (23%)
  waiting for transfers between devices  19.2 us (22%)
  local copies, waits for them, and re-layouts  4.38 us (5%)
    pallas_call x12, Pallas kernels, call(): pl.pallas_call(body, out_shape=outs, in_specs=[anywhere if k in hbm else...  43.3 us
    ppermute x18, starting transfers between devices, swap(): lax.ppermute(array, axis, [(i, i ^ d) for i in range(lax.axis_size(axis))])  20.8 us
    ppermute x18, waiting for transfers between devices, swap(): lax.ppermute(array, axis, [(i, i ^ d) for i in range(lax.axis_size(axis))])  19.2 us
    unnamed x8, local copies, waits for them, and re-layouts  4.38 us
  transfers between devices with their start and end apart: 18, of which 8 were waited for; matrix products, arithmetic and copies ran while one was open for 0% of the time, Pallas kernels for 38%

profile of v1, /device:TPU:0, one launch (start us, length us, event | category | flops | bytes accessed | tf_op | source)
XLA Modules:
  0.0 88.6 jit_solution(9542068035515114536)
XLA Ops:
  0.7 2.2 %copy-done.1 = f32[32,32768]{1,0:T(8,128)S(1)} copy-done((f32[32,32768]{1,0:T(8,128)S(1)}, f32[32,32768]{1,0:T(8,128)}, u32[]{:S(2)}) %copy-start.1) | copy-done | bytes 4194328
  2.9 2.2 %copy-done.2 = s32[32,32768]{1,0:T(8,128)S(1)} copy-done((s32[32,32768]{1,0:T(8,128)S(1)}, s32[32,32768]{1,0:T(8,128)}, u32[]{:S(2)}) %copy-start.2) | copy-done | bytes 4194328
  5.1 2.6 %front.1 = (f32[32,32768]{1,0:T(8,128)S(1)}, s32[32,32768]{1,0:T(8,128)S(1)}, f32[32,32768]{1,0:T(8,128)S(1)}, f32[32,128]{1,0:T(8,128)S(1)}, s16[2,32,8192]{2,1...) custom-call(s32[2]{0:T(128)S(1)} %pad_add_fusion.meta.refs_0_, ...), custom_call_target="tpu_custom_call" | custom-call | bytes 14000000 | tf_op jit(solution)/shard_map/front/pallas_call | solution.py:32
  7.7 4.0 %collective-permute-start.16 = (s16[2,32,8192]{2,1,0:T(8,128)(2,1)S(1)}, s16[2,32,8192]{2,1,0:T(8,128)(2,1)S(1)}, u32[]{:S(2)}, u32[]{:S(2)}) collective-permute-start(s16[2,32,8192]{2,1,0:T(8,128)(2,1)S(1)} %get-tuple-element.49), channel_id=1, source_target_pairs={{0,24},{8,16},{16,8},{24,0},{1,25},{9,17},{17,9},{25,1},{2,26},{10... | collective-permute-start | bytes 3145736 | tf_op jit(solution)/shard_map/ppermute | solution.py:455
  11.6 0.5 collective-permute-start.12
  12.2 0.1 collective-permute-start.13
  12.3 1.2 %collective-permute-done.right.refs_1_ = f32[32,128]{1,0:T(8,128)S(1)} collective-permute-done((f32[32,128]{1,0:T(8,128)S(1)}, f32[32,128]{1,0:T(8,128)S(1)}, u32[]{:S(2)}, u32[]{:S(2)}) %collective-permute-start) | collective-permute-done | bytes 16416 | tf_op jit(solution)/shard_map/ppermute | solution.py:455
  13.5 2.0 %collective-permute-start.1 = (f32[32,128]{1,0:T(8,128)S(1)}, f32[32,128]{1,0:T(8,128)S(1)}, u32[]{:S(2)}, u32[]{:S(2)}) collective-permute-start(f32[32,128]{1,0:T(8,128)S(1)} %pair.3), channel_id=1, source_target_pairs={{0,2},{1,3},{2,0},{3,1},{4,6},{5,7},{6,4},{7,5},{8,10},{9,11},{10,... | collective-permute-start | bytes 49160 | tf_op jit(solution)/shard_map/ppermute | solution.py:455
  15.4 2.6 %collective-permute-start.2 = (f32[32,128]{1,0:T(8,128)S(1)}, f32[32,128]{1,0:T(8,128)S(1)}, u32[]{:S(2)}, u32[]{:S(2)}) collective-permute-start(f32[32,128]{1,0:T(8,128)S(1)} %pair.3), channel_id=1, source_target_pairs={{0,4},{1,5},{2,6},{3,7},{4,0},{5,1},{6,2},{7,3},{8,12},{9,13},{10,... | collective-permute-start | bytes 49160 | tf_op jit(solution)/shard_map/ppermute | solution.py:455
  18.0 3.2 %collective-permute-start.3 = (f32[32,128]{1,0:T(8,128)S(1)}, f32[32,128]{1,0:T(8,128)S(1)}, u32[]{:S(2)}, u32[]{:S(2)}) collective-permute-start(f32[32,128]{1,0:T(8,128)S(1)} %pair.3), channel_id=1, source_target_pairs={{0,6},{1,7},{2,4},{3,5},{4,2},{5,3},{6,0},{7,1},{8,14},{9,15},{10,... | collective-permute-start | bytes 49160 | tf_op jit(solution)/shard_map/ppermute | solution.py:455
  21.2 5.5 %scan.1 = (f32[32,32768]{1,0:T(8,128)S(1)}, f32[32,32768]{1,0:T(8,128)S(1)}, s32[256,128]{1,0:T(8,128)S(1)}, s32[32,32768]{1,0:T(8,128)S(1)}) custom-call(f32[32,32768]{1,0:T(8,128)S(1)} %get-tuple-element.28.weight.refs_5_, s32[32,32768]{1,0:T(8,128)S(1)} %get-tuple-element.29.events.refs_6_, s32[256,128]{1,0:T(8,128)S(1)} %bitcast.6, s32[32,32768]{1,0:T(8,128)S(1)} %copy-done), custom_call_target="tpu_custom_call" | custom-call | bytes 17500000 | tf_op jit(solution)/shard_map/scan/pallas_call | solution.py:32
  26.7 2.0 %inverse.1 = (f32[32,32768]{1,0:T(8,128)S(1)}, f32[32,32768]{1,0:T(8,128)S(1)}, f32[64,128]{1,0:T(8,128)S(1)}, f32[4,32,128]{2,1,0:T(8,128)S(1)}) custom-call(s32[2]{0:T(128)S(1)} %pad_add_fusion.meta.refs_0_, f32[32,128]{1,0:T(8,128)S(1)} %collective-permute-done.right.refs_1_, ...), custom_call_target="tpu_custom_call", output_to_operand_aliasing={{0}: (5, {}), {1}: (6, {})} | custom-call | bytes 5250000 | tf_op jit(solution)/shard_map/inverse/pallas_call | solution.py:32
  28.8 1.2 %collective-permute-done.4.right.refs_1_ = f32[64,128]{1,0:T(8,128)S(1)} collective-permute-done((f32[64,128]{1,0:T(8,128)S(1)}, f32[64,128]{1,0:T(8,128)S(1)}, u32[]{:S(2)}, u32[]{:S(2)}) %collective-permute-start.4) | collective-permute-done | bytes 32800 | tf_op jit(solution)/shard_map/ppermute | solution.py:455
  30.0 1.2 %collective-permute-start.6 = (f32[64,128]{1,0:T(8,128)S(1)}, f32[64,128]{1,0:T(8,128)S(1)}, u32[]{:S(2)}, u32[]{:S(2)}) collective-permute-start(f32[64,128]{1,0:T(8,128)S(1)} %pair.4), channel_id=1, source_target_pairs={{0,4},{1,5},{2,6},{3,7},{4,0},{5,1},{6,2},{7,3},{8,12},{9,13},{10,... | collective-permute-start | bytes 98312 | tf_op jit(solution)/shard_map/ppermute | solution.py:455
  31.2 3.1 %collective-permute-done.5.refs_2_ = f32[64,128]{1,0:T(8,128)S(1)} collective-permute-done((f32[64,128]{1,0:T(8,128)S(1)}, f32[64,128]{1,0:T(8,128)S(1)}, u32[]{:S(2)}, u32[]{:S(2)}) %collective-permute-start.5) | collective-permute-done | bytes 32800 | tf_op jit(solution)/shard_map/ppermute | solution.py:455
  34.3 0.3 collective-permute-start.7
  34.6 2.9 %accum.1 = (f32[32,32768]{1,0:T(8,128)S(1)}, f32[32,32768]{1,0:T(8,128)S(1)}, f32[4,64,128]{2,1,0:T(8,128)S(1)}) custom-call(f32[32,32768]{1,0:T(8,128)S(1)} %get-tuple-element.34.inv_one, f32[32,32768]{1,0:T(8,128)S(1)} %get-tuple-element.35.inv_two), custom_call_target="tpu_custom_call", output_to_operand_aliasing={{0}: (0, {}), {1}: (1, {})} | custom-call | bytes 10500000 | tf_op jit(solution)/shard_map/accum/pallas_call | solution.py:32
  37.5 2.5 %collective-permute-done.7.refs_4_ = f32[64,128]{1,0:T(8,128)S(1)} collective-permute-done((f32[64,128]{1,0:T(8,128)S(1)}, f32[64,128]{1,0:T(8,128)S(1)}, u32[]{:S(2)}, u32[]{:S(2)}) %collective-permute-start.7) | collective-permute-done | bytes 32800 | tf_op jit(solution)/shard_map/ppermute | solution.py:455
  40.0 0.6 bases.1
  40.6 11.5 %leaf_sums.1.left = f32[32,128]{1,0:T(8,128)S(1)} custom-call(s32[32,32768]{1,0:T(8,128)S(1)} %get-tuple-element.30.leaf, f32[32,32768]{1,0:T(8,128)S(1)} %get-tuple-element.28.weight.refs_5_, s32[32,32768]{1,0:T(8,128)S(1)} %get-tuple-element.29.events.refs_6_, f32[32,32768]{1,0:T(8,128)S(1)} %get-tuple-element.36.local_one.refs_7_, ...), custom_call_target="tpu_custom_call" | custom-call | bytes 35000000 | tf_op jit(solution)/shard_map/leaf_sums/pallas_call | solution.py:32
  52.2 1.2 %collective-permute-done.8.right = f32[32,128]{1,0:T(8,128)S(1)} collective-permute-done((f32[32,128]{1,0:T(8,128)S(1)}, f32[32,128]{1,0:T(8,128)S(1)}, u32[]{:S(2)}, u32[]{:S(2)}) %collective-permute-start.8) | collective-permute-done | bytes 16416 | tf_op jit(solution)/shard_map/ppermute | solution.py:455
  53.3 2.5 %collective-permute-start.17 = (f32[96,128]{1,0:T(8,128)S(1)}, f32[96,128]{1,0:T(8,128)S(1)}, u32[]{:S(2)}, u32[]{:S(2)}) collective-permute-start(f32[96,128]{1,0:T(8,128)S(1)} %get-tuple-element.50), channel_id=1, source_target_pairs={{0,24},{8,16},{16,8},{24,0},{1,25},{9,17},{17,9},{25,1},{2,26},{10... | collective-permute-start | bytes 147464 | tf_op jit(solution)/shard_map/ppermute | solution.py:455
  55.8 1.2 %collective-permute-done.9.refs_1_ = f32[32,128]{1,0:T(8,128)S(1)} collective-permute-done((f32[32,128]{1,0:T(8,128)S(1)}, f32[32,128]{1,0:T(8,128)S(1)}, u32[]{:S(2)}, u32[]{:S(2)}) %collective-permute-start.9) | collective-permute-done | bytes 16416 | tf_op jit(solution)/shard_map/ppermute | solution.py:455
  57.1 0.3 collective-permute-start.10
  57.4 4.3 %collective-permute-done.10.refs_2_ = f32[32,128]{1,0:T(8,128)S(1)} collective-permute-done((f32[32,128]{1,0:T(8,128)S(1)}, f32[32,128]{1,0:T(8,128)S(1)}, u32[]{:S(2)}, u32[]{:S(2)}) %collective-permute-start.10) | collective-permute-done | bytes 16416 | tf_op jit(solution)/shard_map/ppermute | solution.py:455
  61.7 1.0 %collective-permute-start.11 = (f32[32,128]{1,0:T(8,128)S(1)}, f32[32,128]{1,0:T(8,128)S(1)}, u32[]{:S(2)}, u32[]{:S(2)}) collective-permute-start(f32[32,128]{1,0:T(8,128)S(1)} %pair.5.refs_0_), channel_id=1, source_target_pairs={{0,6},{1,7},{2,4},{3,5},{4,2},{5,3},{6,0},{7,1},{8,14},{9,15},{10,... | collective-permute-start | bytes 49160 | tf_op jit(solution)/shard_map/ppermute | solution.py:455
  62.7 4.5 %collective-permute-done.11.refs_3_ = f32[32,128]{1,0:T(8,128)S(1)} collective-permute-done((f32[32,128]{1,0:T(8,128)S(1)}, f32[32,128]{1,0:T(8,128)S(1)}, u32[]{:S(2)}, u32[]{:S(2)}) %collective-permute-start.11) | collective-permute-done | bytes 16416 | tf_op jit(solution)/shard_map/ppermute | solution.py:455
  67.2 1.5 %collective-permute-start.14 = (f32[96,128]{1,0:T(8,128)S(1)}, f32[96,128]{1,0:T(8,128)S(1)}, u32[]{:S(2)}, u32[]{:S(2)}) collective-permute-start(f32[96,128]{1,0:T(8,128)S(1)} %get-tuple-element.47), channel_id=1, source_target_pairs={{0,8},{8,0},{16,24},{24,16},{1,9},{9,1},{17,25},{25,17},{2,10},{10... | collective-permute-start | bytes 147464 | tf_op jit(solution)/shard_map/ppermute | solution.py:455
  68.7 1.5 %collective-permute-start.15 = (f32[96,128]{1,0:T(8,128)S(1)}, f32[96,128]{1,0:T(8,128)S(1)}, u32[]{:S(2)}, u32[]{:S(2)}) collective-permute-start(f32[96,128]{1,0:T(8,128)S(1)} %get-tuple-element.48), channel_id=1, source_target_pairs={{0,16},{8,24},{16,0},{24,8},{1,17},{9,25},{17,1},{25,9},{2,18},{10... | collective-permute-start | bytes 147464 | tf_op jit(solution)/shard_map/ppermute | solution.py:455
  70.3 5.5 %update.1 = (f32[32,32768]{1,0:T(8,128)}, f32[32,64]{1,0:T(8,128)}) custom-call(f32[32,32768]{1,0:T(8,128)S(1)} %get-tuple-element.27.pred, s32[32,32768]{1,0:T(8,128)S(1)} %get-tuple-element.30.leaf, f32[32,128]{1,0:T(8,128)S(1)} %pair.5.refs_0_, f32[32,128]{1,0:T(8,128)S(1)} %collective-permute-done.9.refs_1_, ...), custom_call_target="tpu_custom_call" | custom-call | bytes 14000000 | tf_op jit(solution)/shard_map/update/pallas_call | solution.py:32
  75.8 5.5 %finish_first.1.refs_7_ = bf16[2,128,8192]{2,1,0:T(8,128)(2,1)} custom-call(s32[2]{0:T(128)S(1)} %pad_add_fusion.meta.refs_0_, s32[256,128]{1,0:T(8,128)S(1)} %bitcast.7, s32[256,128]{1,0:T(8,128)S(1)} %get-tuple-element.44.refs_2_, s16[2,32,8192]{2,1,0:T(8,128)(2,1)S(1)} %collective-permute-done.16.refs_3_, f32[96,128]{1,0:T(8,128)S(1)} %collective-permute-done.17.refs_4_, ...), custom_call_target="tpu_custom_call" | custom-call | bytes 17500000 | tf_op jit(solution)/shard_map/finish_first/pallas_call | solution.py:32
  81.3 7.3 %finish_rest.1 = bf16[2,128,8192]{2,1,0:T(8,128)(2,1)} custom-call(s32[2]{0:T(128)S(1)} %pad_add_fusion.meta.refs_0_, s32[256,128]{1,0:T(8,128)S(1)} %bitcast.8, s32[256,128]{1,0:T(8,128)S(1)} %get-tuple-element.44.refs_2_, s16[2,32,8192]{2,1,0:T(8,128)(2,1)S(1)} %collective-permute-done.12.refs_3_, ...), custom_call_target="tpu_custom_call", output_to_operand_aliasing={{}: (7, {})} | custom-call | bytes 21000000 | tf_op jit(solution)/shard_map/finish_rest/pallas_call | solution.py:32
  (25 shorter events, 0.3 us)
Async XLA Ops:
  0.7 2.2 %copy-start.1 = (f32[32,32768]{1,0:T(8,128)S(1)}, f32[32,32768]{1,0:T(8,128)}, u32[]{:S(2)}) copy-start(f32[32,32768]{1,0:T(8,128)} %pred_in.1) | copy-start | bytes 12582916
  2.9 2.2 %copy-start.2 = (s32[32,32768]{1,0:T(8,128)S(1)}, s32[32,32768]{1,0:T(8,128)}, u32[]{:S(2)}) copy-start(s32[32,32768]{1,0:T(8,128)} %events_in.1) | copy-start | bytes 12582916
  5.1 16.1 %copy-start = (s32[32,32768]{1,0:T(8,128)S(1)}, s32[32,32768]{1,0:T(8,128)}, u32[]{:S(2)}) copy-start(s32[32,32768]{1,0:T(8,128)} %leaf_in.1) | copy-start | bytes 12582916
  5.1 16.1 %copy-start.3 = (s32[32768]{0:T(1024)S(1)}, s32[32768]{0:T(1024)}, u32[]{:S(2)}) copy-start(s32[32768]{0:T(1024)} %param.7) | copy-start | bytes 393220
  7.7 68.1 %collective-permute-start.16 = (s16[2,32,8192]{2,1,0:T(8,128)(2,1)S(1)}, s16[2,32,8192]{2,1,0:T(8,128)(2,1)S(1)}, u32[]{:S(2)}, u32[]{:S(2)}) collective-permute-start(s16[2,32,8192]{2,1,0:T(8,128)(2,1)S(1)} %get-tuple-element.49), channel_id=1, source_target_pairs={{0,24},{8,16},{16,8},{24,0},{1,25},{9,17},{17,9},{25,1},{2,26},{10... | collective-permute-start | bytes 3145736 | tf_op jit(solution)/shard_map/ppermute | solution.py:455
  11.6 69.7 %collective-permute-start.12 = (s16[2,32,8192]{2,1,0:T(8,128)(2,1)S(1)}, s16[2,32,8192]{2,1,0:T(8,128)(2,1)S(1)}, u32[]{:S(2)}, u32[]{:S(2)}) collective-permute-start(s16[2,32,8192]{2,1,0:T(8,128)(2,1)S(1)} %get-tuple-element.45), channel_id=1, source_target_pairs={{0,8},{8,0},{16,24},{24,16},{1,9},{9,1},{17,25},{25,17},{2,10},{10... | collective-permute-start | bytes 3145736 | tf_op jit(solution)/shard_map/ppermute | solution.py:455
  12.2 69.1 %collective-permute-start.13 = (s16[2,32,8192]{2,1,0:T(8,128)(2,1)S(1)}, s16[2,32,8192]{2,1,0:T(8,128)(2,1)S(1)}, u32[]{:S(2)}, u32[]{:S(2)}) collective-permute-start(s16[2,32,8192]{2,1,0:T(8,128)(2,1)S(1)} %get-tuple-element.46), channel_id=1, source_target_pairs={{0,16},{8,24},{16,0},{24,8},{1,17},{9,25},{17,1},{25,9},{2,18},{10... | collective-permute-start | bytes 3145736 | tf_op jit(solution)/shard_map/ppermute | solution.py:455
  12.3 1.2 %collective-permute-start = (f32[32,128]{1,0:T(8,128)S(1)}, f32[32,128]{1,0:T(8,128)S(1)}, u32[]{:S(2)}, u32[]{:S(2)}) collective-permute-start(f32[32,128]{1,0:T(8,128)S(1)} %get-tuple-element.31.left), channel_id=1, source_target_pairs={{0,1},{1,0},{2,3},{3,2},{4,5},{5,4},{6,7},{7,6},{8,9},{9,8},{10,11... | collective-permute-start | bytes 49160 | tf_op jit(solution)/shard_map/ppermute | solution.py:455
  13.5 4.6 %collective-permute-start.1 = (f32[32,128]{1,0:T(8,128)S(1)}, f32[32,128]{1,0:T(8,128)S(1)}, u32[]{:S(2)}, u32[]{:S(2)}) collective-permute-start(f32[32,128]{1,0:T(8,128)S(1)} %pair.3), channel_id=1, source_target_pairs={{0,2},{1,3},{2,0},{3,1},{4,6},{5,7},{6,4},{7,5},{8,10},{9,11},{10,... | collective-permute-start | bytes 49160 | tf_op jit(solution)/shard_map/ppermute | solution.py:455
  15.4 11.3 %collective-permute-start.2 = (f32[32,128]{1,0:T(8,128)S(1)}, f32[32,128]{1,0:T(8,128)S(1)}, u32[]{:S(2)}, u32[]{:S(2)}) collective-permute-start(f32[32,128]{1,0:T(8,128)S(1)} %pair.3), channel_id=1, source_target_pairs={{0,4},{1,5},{2,6},{3,7},{4,0},{5,1},{6,2},{7,3},{8,12},{9,13},{10,... | collective-permute-start | bytes 49160 | tf_op jit(solution)/shard_map/ppermute | solution.py:455
  18.0 8.7 %collective-permute-start.3 = (f32[32,128]{1,0:T(8,128)S(1)}, f32[32,128]{1,0:T(8,128)S(1)}, u32[]{:S(2)}, u32[]{:S(2)}) collective-permute-start(f32[32,128]{1,0:T(8,128)S(1)} %pair.3), channel_id=1, source_target_pairs={{0,6},{1,7},{2,4},{3,5},{4,2},{5,3},{6,0},{7,1},{8,14},{9,15},{10,... | collective-permute-start | bytes 49160 | tf_op jit(solution)/shard_map/ppermute | solution.py:455
  28.8 1.3 %collective-permute-start.4 = (f32[64,128]{1,0:T(8,128)S(1)}, f32[64,128]{1,0:T(8,128)S(1)}, u32[]{:S(2)}, u32[]{:S(2)}) collective-permute-start(f32[64,128]{1,0:T(8,128)S(1)} %get-tuple-element.38.left), channel_id=1, source_target_pairs={{0,1},{1,0},{2,3},{3,2},{4,5},{5,4},{6,7},{7,6},{8,9},{9,8},{10,11... | collective-permute-start | bytes 98312 | tf_op jit(solution)/shard_map/ppermute | solution.py:455
  30.0 4.3 %collective-permute-start.5 = (f32[64,128]{1,0:T(8,128)S(1)}, f32[64,128]{1,0:T(8,128)S(1)}, u32[]{:S(2)}, u32[]{:S(2)}) collective-permute-start(f32[64,128]{1,0:T(8,128)S(1)} %pair.4), channel_id=1, source_target_pairs={{0,2},{1,3},{2,0},{3,1},{4,6},{5,7},{6,4},{7,5},{8,10},{9,11},{10,... | collective-permute-start | bytes 98312 | tf_op jit(solution)/shard_map/ppermute | solution.py:455
  30.0 7.5 %collective-permute-start.6 = (f32[64,128]{1,0:T(8,128)S(1)}, f32[64,128]{1,0:T(8,128)S(1)}, u32[]{:S(2)}, u32[]{:S(2)}) collective-permute-start(f32[64,128]{1,0:T(8,128)S(1)} %pair.4), channel_id=1, source_target_pairs={{0,4},{1,5},{2,6},{3,7},{4,0},{5,1},{6,2},{7,3},{8,12},{9,13},{10,... | collective-permute-start | bytes 98312 | tf_op jit(solution)/shard_map/ppermute | solution.py:455
  34.3 5.7 %collective-permute-start.7 = (f32[64,128]{1,0:T(8,128)S(1)}, f32[64,128]{1,0:T(8,128)S(1)}, u32[]{:S(2)}, u32[]{:S(2)}) collective-permute-start(f32[64,128]{1,0:T(8,128)S(1)} %pair.4), channel_id=1, source_target_pairs={{0,6},{1,7},{2,4},{3,5},{4,2},{5,3},{6,0},{7,1},{8,14},{9,15},{10,... | collective-permute-start | bytes 98312 | tf_op jit(solution)/shard_map/ppermute | solution.py:455
  52.1 1.2 %collective-permute-start.8 = (f32[32,128]{1,0:T(8,128)S(1)}, f32[32,128]{1,0:T(8,128)S(1)}, u32[]{:S(2)}, u32[]{:S(2)}) collective-permute-start(f32[32,128]{1,0:T(8,128)S(1)} %leaf_sums.1.left), channel_id=1, source_target_pairs={{0,1},{1,0},{2,3},{3,2},{4,5},{5,4},{6,7},{7,6},{8,9},{9,8},{10,11... | collective-permute-start | bytes 49160 | tf_op jit(solution)/shard_map/ppermute | solution.py:455
  53.3 3.7 %collective-permute-start.9 = (f32[32,128]{1,0:T(8,128)S(1)}, f32[32,128]{1,0:T(8,128)S(1)}, u32[]{:S(2)}, u32[]{:S(2)}) collective-permute-start(f32[32,128]{1,0:T(8,128)S(1)} %pair.5.refs_0_), channel_id=1, source_target_pairs={{0,2},{1,3},{2,0},{3,1},{4,6},{5,7},{6,4},{7,5},{8,10},{9,11},{10,... | collective-permute-start | bytes 49160 | tf_op jit(solution)/shard_map/ppermute | solution.py:455
  53.3 15.4 %collective-permute-start.17 = (f32[96,128]{1,0:T(8,128)S(1)}, f32[96,128]{1,0:T(8,128)S(1)}, u32[]{:S(2)}, u32[]{:S(2)}) collective-permute-start(f32[96,128]{1,0:T(8,128)S(1)} %get-tuple-element.50), channel_id=1, source_target_pairs={{0,24},{8,16},{16,8},{24,0},{1,25},{9,17},{17,9},{25,1},{2,26},{10... | collective-permute-start | bytes 147464 | tf_op jit(solution)/shard_map/ppermute | solution.py:455
  57.1 4.6 %collective-permute-start.10 = (f32[32,128]{1,0:T(8,128)S(1)}, f32[32,128]{1,0:T(8,128)S(1)}, u32[]{:S(2)}, u32[]{:S(2)}) collective-permute-start(f32[32,128]{1,0:T(8,128)S(1)} %pair.5.refs_0_), channel_id=1, source_target_pairs={{0,4},{1,5},{2,6},{3,7},{4,0},{5,1},{6,2},{7,3},{8,12},{9,13},{10,... | collective-permute-start | bytes 49160 | tf_op jit(solution)/shard_map/ppermute | solution.py:455
  61.7 5.5 %collective-permute-start.11 = (f32[32,128]{1,0:T(8,128)S(1)}, f32[32,128]{1,0:T(8,128)S(1)}, u32[]{:S(2)}, u32[]{:S(2)}) collective-permute-start(f32[32,128]{1,0:T(8,128)S(1)} %pair.5.refs_0_), channel_id=1, source_target_pairs={{0,6},{1,7},{2,4},{3,5},{4,2},{5,3},{6,0},{7,1},{8,14},{9,15},{10,... | collective-permute-start | bytes 49160 | tf_op jit(solution)/shard_map/ppermute | solution.py:455
  67.2 14.0 %collective-permute-start.14 = (f32[96,128]{1,0:T(8,128)S(1)}, f32[96,128]{1,0:T(8,128)S(1)}, u32[]{:S(2)}, u32[]{:S(2)}) collective-permute-start(f32[96,128]{1,0:T(8,128)S(1)} %get-tuple-element.47), channel_id=1, source_target_pairs={{0,8},{8,0},{16,24},{24,16},{1,9},{9,1},{17,25},{25,17},{2,10},{10... | collective-permute-start | bytes 147464 | tf_op jit(solution)/shard_map/ppermute | solution.py:455
  68.7 12.5 %collective-permute-start.15 = (f32[96,128]{1,0:T(8,128)S(1)}, f32[96,128]{1,0:T(8,128)S(1)}, u32[]{:S(2)}, u32[]{:S(2)}) collective-permute-start(f32[96,128]{1,0:T(8,128)S(1)} %get-tuple-element.48), channel_id=1, source_target_pairs={{0,16},{8,24},{16,0},{24,8},{1,17},{9,25},{17,1},{25,9},{2,18},{10... | collective-permute-start | bytes 147464 | tf_op jit(solution)/shard_map/ppermute | solution.py:455

commit v2 on v1

--- a/solution.py
+++ b/solution.py
@@ -1,4 +1,5 @@
 import functools
+import math
 
 import jax
 import jax.numpy as jnp
@@ -23,6 +24,10 @@
 
 def near(array):
     return pltpu.with_memory_space_constraint(array, pltpu.VMEM)
+
+
+def far(array):
+    return pltpu.with_memory_space_constraint(array, pltpu.HBM)
 
 
 def call(body, outs, *args, scratch=(), name=None, us=1.0, aliases=None, limit=12, hbm=(), hbm_out=()):
@@ -65,8 +70,22 @@
     return (meta[0] ^ d) * size
 
 
-def front_body(parts, turns, meta, pred_in, events_in, pred, events, weight, total, *rest):
-    messages, sems = rest[: parts - 1], rest[parts - 1]
+def encode(meta, d, pred, events, message):
+    share = message.shape[2]
+    step = min(share, 1024)
+
+    def one(turn, carry):
+        source = span(share_of(meta, d, share) + turn * step, step)
+        at = span(turn * step, step)
+        message[0, :, at] = jnp.round(pred[:, source] * CODE).astype(jnp.int32).astype(I16)
+        message[1, :, at] = events[:, source].astype(I16)
+        return carry
+
+    lax.fori_loop(0, share // step, one, 0, unroll=2)
+
+
+def front_body(partners, turns, meta, pred_in, events_in, events, weight, total, *rest):
+    messages, pred, sems = rest[:-2], rest[-2], rest[-1]
     rows, length = pred.shape
     width = length // turns
 
@@ -94,17 +113,8 @@
 
         acc = lax.fori_loop(0, width // step, one, acc, unroll=2)
     total[...] = lane_sum(acc)
-    share = length // parts
-    for d in range(1, parts):
-
-        def code(k, carry):
-            source = span(share_of(meta, d, share) + k * step, step)
-            at = span(k * step, step)
-            messages[d - 1][0, :, at] = jnp.round(pred[:, source] * CODE).astype(jnp.int32).astype(I16)
-            messages[d - 1][1, :, at] = events[:, source].astype(I16)
-            return carry
-
-        lax.fori_loop(0, share // step, code, 0, unroll=2)
+    for d, message in zip(partners, messages):
+        encode(meta, d, pred, events, message)
 
 
 def pair_dot(x, matrix):
@@ -176,8 +186,14 @@
     fetch.wait()
 
 
-def pair_body(left, right, out):
-    out[...] = left[...] + right[...]
+def pair_body(left, right, *refs):
+    refs[-1][...] = left[...] + right[...]
+
+
+def join_body(*refs):
+    rows = refs[0].shape[0]
+    for k, ref in enumerate(refs[:-1]):
+        refs[-1][k * rows : (k + 1) * rows, :] = ref[...]
 
 
 def gathered_sum(meta, refs, later):
@@ -244,34 +260,72 @@
         carry = lax.fori_loop(0, share // (WIDE * count), one, carry, unroll=2)
 
 
-def bases_body(count, parts, *refs):
+def derivatives(weight, observed, accum_one, accum_two):
+    scaled = weight * accum_one
+    return scaled - observed, scaled - weight * weight * accum_two
+
+
+def pieces(first, at_rows, weight, events, local_one, local_two, bases, out, at_lanes=0):
+    rows, length = out.shape[1], at_rows
+    step = math.gcd(length, 512)
+
+    def one(turn, carry):
+        source = span(first + turn * step, step)
+        at = span(at_lanes + turn * step, step)
+        grad, hess = derivatives(
+            weight[:, source],
+            events[:, source].astype(F32),
+            local_one[:, source] + widen(bases[:rows, :], step),
+            local_two[:, source] + widen(bases[rows:, :], step),
+        )
+        out[0, :, at] = grad.astype(BF16)
+        out[1, :, at] = hess.astype(BF16)
+        return carry
+
+    lax.fori_loop(0, length // step, one, 0, unroll=2)
+
+
+def bases_body(count, links, diagonals, share, *refs):
     meta, others = refs[0], refs[1 : 1 + count]
-    after, before, bases, *messages = refs[1 + count :]
+    after, before, *scans = refs[1 + count : 7 + count]
+    bases, *messages = refs[len(refs) - 1 - len(links) - len(diagonals) :]
+    messages, early = messages[: len(links)], messages[len(links) :]
     rows = after.shape[1]
     earlier = gathered_sum(meta, others, False)
     bases[...] = earlier
-    for d in range(1, parts):
+    for d, message in zip(links, messages):
         part = share_of(meta, d, 1)
-        messages[d - 1][:rows] = after[part]
-        messages[d - 1][rows:] = before[part] + earlier
-
-
-def derivatives(weight, observed, accum_one, accum_two):
-    scaled = weight * accum_one
-    return scaled - observed, scaled - weight * weight * accum_two
-
-
-def finish_body(partners, with_own, *refs):
+        message[:rows] = after[part]
+        message[rows:] = before[part] + earlier
+    for d, out in zip(diagonals, early):
+        pieces(share_of(meta, d, share), out.shape[2], *scans, bases, out)
+
+
+def rest_body(diagonals, share, meta, *refs):
+    for d, out in zip(diagonals, refs[len(refs) - len(diagonals) :]):
+        size = out.shape[2]
+        pieces(share_of(meta, d, share) + share - size, size, *refs[:5], out)
+
+
+def place_pieces(meta, partners, arrived, out, sems, last=False):
+    copies = []
+    for k, (d, piece) in enumerate(zip(partners, arrived)):
+        _, rows, size = piece.shape
+        where = pl.ds(pl.multiple_of(share_of(meta, d, rows), rows), rows)
+        lanes = pl.ds(out.shape[2] - size if last else 0, size)
+        copies += [pltpu.make_async_copy(piece.at[v], out.at[v, where, lanes], sems.at[k, v]) for v in (0, 1)]
+    return copies
+
+
+def finish_body(partners, *refs):
     meta, tie, last = refs[:3]
     refs = refs[3:]
     messages, base = refs[: len(partners)], refs[len(partners) : 2 * len(partners)]
     refs = refs[2 * len(partners) :]
-    if with_own:
-        weight, events, local_one, local_two, own_bases = refs[:5]
-        refs = refs[5:]
-    else:
-        refs = refs[1:]
-    out, scratch, kept, inv_one, inv_two, upper, lower, sems = refs
+    weight, events, local_one, local_two, own_bases = refs[:5]
+    pred_in, out, pred, scratch, kept, inv_one, inv_two, upper, lower, sems, fetch_sem = refs[5:]
+    fetch = pltpu.make_async_copy(pred_in, pred, fetch_sem)
+    fetch.start()
     _, rows, share = kept.shape
     count = min(8, share // WIDE)
     steps = share // (WIDE * count)
@@ -279,32 +333,12 @@
     first_block = share_of(meta, 0, share) // LANES
     upper[...] = triangle(True)
     lower[...] = triangle(False)
-    places = list(partners) + ([0] if with_own else [])
-    copies = []
-    for slot, d in enumerate(places):
-        where = pl.ds(pl.multiple_of(share_of(meta, d, rows), rows), rows)
-        copies += [pltpu.make_async_copy(scratch.at[slot, v], out.at[v, where, :], sems.at[slot, v]) for v in (0, 1)]
-
-    if with_own:
-        slot = len(partners)
-        step = min(share, 512)
-
-        def own(turn, carry):
-            source = span(share_of(meta, 0, share) + turn * step, step)
-            at = span(turn * step, step)
-            grad, hess = derivatives(
-                weight[:, source],
-                events[:, source].astype(F32),
-                local_one[:, source] + widen(own_bases[:rows, :], step),
-                local_two[:, source] + widen(own_bases[rows:, :], step),
-            )
-            scratch[slot, 0, :, at] = grad.astype(BF16)
-            scratch[slot, 1, :, at] = hess.astype(BF16)
-            return carry
-
-        lax.fori_loop(0, share // step, own, 0, unroll=2)
-        for v in (0, 1):
-            copies[2 * slot + v].start()
+    places = list(partners) + [0]
+    copies = place_pieces(meta, places, [scratch.at[slot] for slot in range(len(places))], out, sems)
+    slot = len(partners)
+    pieces(share_of(meta, 0, share), share, weight, events, local_one, local_two, own_bases, scratch.at[slot])
+    for v in (0, 1):
+        copies[2 * slot + v].start()
 
     def one(turn, carry):
         at_base = (steps - 1 - turn) * turn_width
@@ -367,6 +401,7 @@
         copy.start()
     for copy in copies:
         copy.wait()
+    fetch.wait()
 
 
 GROUP = 16
@@ -374,34 +409,33 @@
 HIGH = LEAVES // LOW
 
 
-def leaf_sums_body(leaf, weight, events, local_one, local_two, bases, sums, acc):
+def leaf_sums_body(group, leaf, weight, events, local_one, local_two, bases, *rest):
+    sums, acc = rest[-2:]
     rows, length = weight.shape
-    step = min(length, 1024)
-    groups = rows // GROUP
+    step = min(length, 2048)
+    mine = pl.ds(group * GROUP, GROUP)
     acc[...] = jnp.zeros_like(acc)
 
     def one(turn, carry):
         at = span(turn * step, step)
-        for group in range(groups):
-            mine = pl.ds(group * GROUP, GROUP)
-            pair = derivatives(
-                weight[mine, at],
-                events[mine, at].astype(F32),
-                local_one[mine, at] + widen(bases[mine, :], step),
-                local_two[mine, at] + widen(bases[pl.ds(rows + group * GROUP, GROUP), :], step),
-            )
-            label = leaf[mine, at]
-            low = (label & (LOW - 1)).astype(F32).astype(BF16)
-            high = lax.shift_right_logical(label, LOW.bit_length() - 1).astype(F32).astype(BF16)
-            terms = []
-            for value in pair:
-                upper = value.astype(BF16)
-                terms += [upper, (value - upper.astype(F32)).astype(BF16)]
-            zero = jnp.zeros((GROUP, step), BF16)
-            unit = jnp.ones((GROUP, step), BF16)
-            left = jnp.concatenate([jnp.where(high == h, term, zero) for term in terms for h in range(HIGH)], axis=0)
-            right = jnp.concatenate([jnp.where(low == k, unit, zero) for k in range(LOW)], axis=0)
-            acc[group] += lax.dot_general(left, right, (((1,), (1,)), ((), ())), preferred_element_type=F32)
+        pair = derivatives(
+            weight[mine, at],
+            events[mine, at].astype(F32),
+            local_one[mine, at] + widen(bases[mine, :], step),
+            local_two[mine, at] + widen(bases[pl.ds(rows + group * GROUP, GROUP), :], step),
+        )
+        label = leaf[mine, at]
+        low = (label & (LOW - 1)).astype(F32).astype(BF16)
+        high = lax.shift_right_logical(label, LOW.bit_length() - 1).astype(F32).astype(BF16)
+        terms = []
+        for value in pair:
+            upper = value.astype(BF16)
+            terms += [upper, (value - upper.astype(F32)).astype(BF16)]
+        zero = jnp.zeros((GROUP, step), BF16)
+        unit = jnp.ones((GROUP, step), BF16)
+        left = jnp.concatenate([jnp.where(high == h, term, zero) for term in terms for h in range(HIGH)], axis=0)
+        right = jnp.concatenate([jnp.where(low == k, unit, zero) for k in range(LOW)], axis=0)
+        acc[...] += lax.dot_general(left, right, (((1,), (1,)), ((), ())), preferred_element_type=F32)
         return carry
 
     lax.fori_loop(0, length // step, one, 0, unroll=4)
@@ -410,22 +444,24 @@
     same = lax.broadcasted_iota(jnp.int32, (side, width), 0) % GROUP == lax.broadcasted_iota(jnp.int32, (side, width), 1) % GROUP
     source = lax.broadcasted_iota(jnp.int32, (width, LANES), 0) // GROUP
     target = lax.broadcasted_iota(jnp.int32, (width, LANES), 1)
-    for group in range(groups):
-        out = jnp.zeros((GROUP, LANES), F32)
-        for value in (0, 1):
-            both = acc[group, 2 * value * side : (2 * value + 1) * side] + acc[group, (2 * value + 1) * side : (2 * value + 2) * side]
-            both = jnp.where(same, both, 0.0)
-            for h in range(HIGH):
-                place = (target == source + (h * LOW + value * LEAVES)).astype(F32)
-                out = out + jnp.dot(
-                    both[h * GROUP : (h + 1) * GROUP], place, precision=lax.Precision.HIGHEST, preferred_element_type=F32
-                )
-        sums[group * GROUP : (group + 1) * GROUP, :] = out
-
-
-def update_body(turns, pred, leaf, *refs):
-    sums, (new_pred, leaf_weights, scratch, sems) = refs[:-4], refs[-4:]
-    rows, length = pred.shape
+    out = jnp.zeros((GROUP, LANES), F32)
+    for value in (0, 1):
+        both = acc[2 * value * side : (2 * value + 1) * side] + acc[(2 * value + 1) * side : (2 * value + 2) * side]
+        both = jnp.where(same, both, 0.0)
+        for h in range(HIGH):
+            place = (target == source + (h * LOW + value * LEAVES)).astype(F32)
+            out = out + jnp.dot(both[h * GROUP : (h + 1) * GROUP], place, precision=lax.Precision.HIGHEST, preferred_element_type=F32)
+    sums[...] = out
+
+
+def update_body(turns, partners, meta, pred, leaf, *refs):
+    early, late, refs = refs[: len(partners)], refs[len(partners) : 2 * len(partners)], refs[2 * len(partners) + 1 :]
+    sums, (new_pred, leaf_weights, out, scratch, sems, early_sems, late_sems) = refs[:-7], refs[-7:]
+    rows, length = leaf.shape
+    copies = place_pieces(meta, partners, early, out, early_sems)
+    copies += place_pieces(meta, partners, late, out, late_sems, True)
+    for copy in copies:
+        copy.start()
     both = [ref[...] for ref in sums]
     while len(both) > 1:
         both = [a + b for a, b in zip(both[::2], both[1::2])]
@@ -433,7 +469,6 @@
     leaf_weights[...] = table[:, :LEAVES]
     width = length // turns
     step = min(width, 512)
-    copies = []
     for turn in range(turns):
 
         def one(k, carry):
@@ -443,7 +478,7 @@
             scratch[:, at] = pred[:, at] + jnp.concatenate(picked, axis=1)
             return carry
 
-        lax.fori_loop(0, width // step, one, 0, unroll=4)
+        lax.fori_loop(0, width // step, one, 0, unroll=8)
         at = pl.ds(turn * width, width)
         copies.append(pltpu.make_async_copy(scratch.at[:, at], new_pred.at[:, at], sems.at[turn]))
         copies[-1].start()
@@ -455,9 +490,9 @@
     return lax.ppermute(array, axis, [(i, i ^ d) for i in range(lax.axis_size(axis))])
 
 
-def across(total, axis):
+def across(total, axis, arrived=()):
     mate = swap(total, axis, 1)
-    (both,) = call(pair_body, [resident(total.shape, F32)], total, mate, name="pair", us=0.3, limit=2)
+    (both,) = call(pair_body, [resident(total.shape, F32)], total, mate, *arrived, name="pair", us=0.3, limit=4)
     return both, [mate] + [swap(both, axis, d) for d in range(2, lax.axis_size(axis), 2)]
 
 
@@ -472,19 +507,21 @@
     tie = near(tie_start.reshape(blocks, LANES))
     meta = jnp.stack([lax.axis_index("ep"), lax.axis_index("tm")]).astype(jnp.int32)
 
-    pred, observed, weight, total, *messages = call(
-        functools.partial(front_body, parts, turns),
-        [resident(wide, F32), resident(wide, jnp.int32), resident(wide, F32), resident((rows, LANES), F32)]
-        + [resident((2, rows, share), I16)] * (parts - 1),
+    links = [d for d in range(1, parts) if d & (d - 1) == 0]
+    diagonals = [d for d in range(1, parts) if d not in links]
+    message = resident((2, rows, share), I16)
+    observed, weight, total, *messages = call(
+        functools.partial(front_body, links, turns),
+        [resident(wide, jnp.int32), resident(wide, F32), resident((rows, LANES), F32)] + [message] * len(links),
         meta,
-        predictions,
-        events,
+        far(predictions),
+        far(events),
         hbm=(1, 2),
-        scratch=[dma((2, turns))],
+        scratch=[pltpu.VMEM(wide, F32), dma((2, turns))],
         name="front",
         us=4,
     )
-    coded = {d: swap(messages[d - 1], "ep", d) for d in range(parts - 1, 0, -1)}
+    coded = {d: swap(m, "ep", d) for d, m in zip(links, messages)}
     _, from_later = across(total, "tm")
     suffix, grouped, last, leaf = call(
         scan_body,
@@ -492,7 +529,7 @@
         weight,
         observed,
         tie,
-        leaf_index,
+        far(leaf_index),
         hbm=(3,),
         scratch=[pltpu.VMEM((WIDE, WIDE), BF16)] * 2 + [dma],
         name="scan",
@@ -521,64 +558,90 @@
         name="accum",
         us=3,
     )
+    scans = (weight, observed, local_one, local_two)
+    early_rows = share // 4
     bases, *sent = call(
-        functools.partial(bases_body, count, parts),
-        [resident((2 * rows, LANES), F32)] + [resident((3 * rows, LANES), F32)] * (parts - 1),
+        functools.partial(bases_body, count, links, diagonals, share),
+        [resident((2 * rows, LANES), F32)]
+        + [resident((3 * rows, LANES), F32)] * len(links)
+        + [resident((2, rows, early_rows), BF16)] * len(diagonals),
         meta,
         *from_earlier,
         after,
         before,
+        *scans,
+        *coded.values(),
         name="bases",
-        us=0.5,
-    )
-    base = {d: swap(sent[d - 1], "ep", d) for d in range(parts - 1, 0, -1)}
-    (partial_sums,) = call(
-        leaf_sums_body,
-        [resident((rows, LANES), F32)],
-        leaf,
-        weight,
-        observed,
-        local_one,
-        local_two,
-        bases,
-        scratch=[pltpu.VMEM((rows // GROUP, 4 * HIGH * GROUP, LOW * GROUP), F32)],
-        name="leaf_sums",
-        us=10,
-    )
-    both, others = across(partial_sums, "tm")
-
-    def finish(partners, more, out, name, us):
-        held = len(partners) + (out is None)
-        args = [meta, tie, last, *[coded[d] for d in partners], *[base[d] for d in partners], *more]
-        made = [pltpu.VMEM((len(partners), rows, share), F32)] * 3
-        return call(
-            functools.partial(finish_body, partners, out is None),
-            [jax.ShapeDtypeStruct((2, rows * parts, share), BF16)],
-            *args,
-            *([] if out is None else [out]),
-            hbm=() if out is None else (len(args),),
-            hbm_out=(0,),
-            aliases=None if out is None else {len(args): 0},
-            scratch=[pltpu.VMEM((held, 2, rows, share), BF16), *made, *[pltpu.VMEM((WIDE, WIDE), BF16)] * 2, dma((held, 2))],
-            name=name,
-            us=us,
-        )[0]
-
-    first = parts - 1
-    grad_hess = finish([first], [weight, observed, local_one, local_two, bases], None, "finish_first", 5)
-    new_pred, leaf_weights = call(
-        functools.partial(update_body, turns),
-        [jax.ShapeDtypeStruct(wide, F32), jax.ShapeDtypeStruct((rows, LEAVES), F32)],
+        us=1,
+    )
+    base = {d: swap(m, "ep", d) for d, m in zip(links, sent)}
+    early = [swap(m, "ep", d) for d, m in zip(diagonals, sent[len(links) :])]
+    late = []
+    partial_sums = []
+    for group in range(rows // GROUP):
+        partial_sums += call(
+            functools.partial(leaf_sums_body, group),
+            [resident((GROUP, LANES), F32)],
+            leaf,
+            *scans,
+            bases,
+            *(sent if late else []),
+            scratch=[pltpu.VMEM((4 * HIGH * GROUP, LOW * GROUP), F32)],
+            name="leaf_sums",
+            us=5,
+        )
+        if not late:
+            sent = call(
+                functools.partial(rest_body, diagonals, share),
+                [resident((2, rows, share - early_rows), BF16)] * len(diagonals),
+                meta,
+                *scans,
+                bases,
+                *partial_sums,
+                *base.values(),
+                *early,
+                name="rest",
+                us=1,
+            )
+            late = [swap(m, "ep", d) for d, m in zip(diagonals, sent)]
+    (own_sums,) = call(join_body, [resident((rows, LANES), F32)], *partial_sums, name="join", us=0.3, limit=2)
+    both, others = across(own_sums, "tm", base.values())
+    piece = pltpu.VMEM((len(links), rows, share), F32)
+    args = [meta, tie, last, *[coded[d] for d in links], *[base[d] for d in links], *scans, bases]
+    grad_hess, pred = call(
+        functools.partial(finish_body, links),
+        [jax.ShapeDtypeStruct((2, rows * parts, share), BF16), resident(wide, F32)],
+        *args,
+        far(predictions),
+        hbm=(len(args),),
+        hbm_out=(0,),
+        scratch=[pltpu.VMEM((len(links) + 1, 2, rows, share), BF16)]
+        + [piece] * 3
+        + [pltpu.VMEM((WIDE, WIDE), BF16)] * 2
+        + [dma((len(links) + 1, 2)), dma],
+        name="finish",
+        us=8,
+        limit=14,
+    )
+    at_out = 3 + 2 * len(diagonals)
+    new_pred, leaf_weights, grad_hess = call(
+        functools.partial(update_body, turns, diagonals),
+        [jax.ShapeDtypeStruct(wide, F32), jax.ShapeDtypeStruct((rows, LEAVES), F32), jax.ShapeDtypeStruct(grad_hess.shape, BF16)],
+        meta,
         pred,
         leaf,
+        *early,
+        *late,
+        grad_hess,
         both,
         *others[1:],
-        hbm_out=(0,),
-        scratch=[pltpu.VMEM(wide, F32), dma((turns,))],
+        hbm=range(3, at_out + 1),
+        hbm_out=(0, 2),
+        aliases={at_out: 2},
+        scratch=[pltpu.VMEM(wide, F32), dma((turns,)), dma((max(1, len(diagonals)), 2)), dma((max(1, len(diagonals)), 2))],
         name="update",
         us=4,
     )
-    grad_hess = finish(list(range(1, first)), [], grad_hess, "finish_rest", 6)
     return new_pred, leaf_weights, grad_hess.reshape(2, rows * parts, 1, share)
 
 

time: 88.8 us -> 70.2 us (0.79)
  waiting for transfers between devices: 19.2 us -> 6.11 us
  local copies, waits for them, and re-layouts: 4.38 us -> 0.01 us
  Pallas kernels: 43.3 us -> 41.1 us
  starting transfers between devices: 20.8 us -> 22 us
    ppermute x18, waiting for transfers between devices: 19.2 us -> 6.11 us  [swap(): lax.ppermute(array, axis, [(i, i ^ d) for i in range(lax.axis_size(axis))])]
    unnamed x8 -> x2, local copies, waits for them, and re-layouts: 4.38 us -> 0.01 us
    pallas_call x12 -> x14, Pallas kernels: 43.3 us -> 41.1 us  [call(): pl.pallas_call(body, out_shape=outs, in_specs=[anywhere if k in hbm else...]
    ppermute x18, starting transfers between devices: 20.8 us -> 22 us  [swap(): lax.ppermute(array, axis, [(i, i ^ d) for i in range(lax.axis_size(axis))])]
  transfers between devices with their start and end apart: 18 -> 18, of which waited for: 8 -> 4; matrix products, arithmetic and copies ran while one was open for 0% -> 0% of each run, Pallas kernels for 38% -> 42%
where the time goes in v2:
time: 70.2 us; the launch traced here: 70.1 us
  Pallas kernels  41.1 us (59%)
  starting transfers between devices  22 us (31%)
  waiting for transfers between devices  6.11 us (9%)
  between operations  0.8 us (1%)
    pallas_call x14, Pallas kernels, call(): pl.pallas_call(body, out_shape=outs, in_specs=[anywhere if k in hbm else...  41.1 us
    ppermute x18, starting transfers between devices, swap(): lax.ppermute(array, axis, [(i, i ^ d) for i in range(lax.axis_size(axis))])  22 us
    ppermute x18, waiting for transfers between devices, swap(): lax.ppermute(array, axis, [(i, i ^ d) for i in range(lax.axis_size(axis))])  6.11 us
  transfers between devices with their start and end apart: 18, of which 4 were waited for; matrix products, arithmetic and copies ran while one was open for 0% of the time, Pallas kernels for 42%

profile of v2, /device:TPU:0, one launch (start us, length us, event | category | flops | bytes accessed | tf_op | source)
XLA Modules:
  0.0 70.1 jit_solution(12208916676041516639)
XLA Ops:
  0.6 0.1 pad_add_fusion.meta.refs_0_
  0.7 4.5 %front.1 = (s32[32,32768]{1,0:T(8,128)S(1)}, f32[32,32768]{1,0:T(8,128)S(1)}, f32[32,128]{1,0:T(8,128)S(1)}, s16[2,32,8192]{2,1,0:T(8,128)(2,1)S(1)}, s16[2,32,8192]{2,1,0:T(8,128)(2,1)S(1)}) custom-call(s32[2]{0:T(128)S(1)} %pad_add_fusion.meta.refs_0_, f32[32,32768]{1,0:T(8,128)} %refs_12_.1, s32[32,32768]{1,0:T(8,128)} %events_in.1), custom_call_target="tpu_custom_call" | custom-call | bytes 14000000 | tf_op jit(solution)/shard_map/front/pallas_call | solution.py:37
  5.2 3.0 %collective-permute-start = (s16[2,32,8192]{2,1,0:T(8,128)(2,1)S(1)}, s16[2,32,8192]{2,1,0:T(8,128)(2,1)S(1)}, u32[]{:S(2)}, u32[]{:S(2)}) collective-permute-start(s16[2,32,8192]{2,1,0:T(8,128)(2,1)S(1)} %get-tuple-element.31), channel_id=1, source_target_pairs={{0,8},{8,0},{16,24},{24,16},{1,9},{9,1},{17,25},{25,17},{2,10},{10... | collective-permute-start | bytes 3145736 | tf_op jit(solution)/shard_map/ppermute | solution.py:490
  8.2 1.5 %collective-permute-start.1 = (s16[2,32,8192]{2,1,0:T(8,128)(2,1)S(1)}, s16[2,32,8192]{2,1,0:T(8,128)(2,1)S(1)}, u32[]{:S(2)}, u32[]{:S(2)}) collective-permute-start(s16[2,32,8192]{2,1,0:T(8,128)(2,1)S(1)} %get-tuple-element.32), channel_id=1, source_target_pairs={{0,16},{8,24},{16,0},{24,8},{1,17},{9,25},{17,1},{25,9},{2,18},{10... | collective-permute-start | bytes 3145736 | tf_op jit(solution)/shard_map/ppermute | solution.py:490
  9.8 1.2 %collective-permute-done.2.right.refs_1_ = f32[32,128]{1,0:T(8,128)S(1)} collective-permute-done((f32[32,128]{1,0:T(8,128)S(1)}, f32[32,128]{1,0:T(8,128)S(1)}, u32[]{:S(2)}, u32[]{:S(2)}) %collective-permute-start.2) | collective-permute-done | bytes 16416 | tf_op jit(solution)/shard_map/ppermute | solution.py:490
  11.0 1.6 %collective-permute-start.3 = (f32[32,128]{1,0:T(8,128)S(1)}, f32[32,128]{1,0:T(8,128)S(1)}, u32[]{:S(2)}, u32[]{:S(2)}) collective-permute-start(f32[32,128]{1,0:T(8,128)S(1)} %pair.3), channel_id=1, source_target_pairs={{0,2},{1,3},{2,0},{3,1},{4,6},{5,7},{6,4},{7,5},{8,10},{9,11},{10,... | collective-permute-start | bytes 49160 | tf_op jit(solution)/shard_map/ppermute | solution.py:490
  12.5 2.6 %collective-permute-start.4 = (f32[32,128]{1,0:T(8,128)S(1)}, f32[32,128]{1,0:T(8,128)S(1)}, u32[]{:S(2)}, u32[]{:S(2)}) collective-permute-start(f32[32,128]{1,0:T(8,128)S(1)} %pair.3), channel_id=1, source_target_pairs={{0,4},{1,5},{2,6},{3,7},{4,0},{5,1},{6,2},{7,3},{8,12},{9,13},{10,... | collective-permute-start | bytes 49160 | tf_op jit(solution)/shard_map/ppermute | solution.py:490
  15.1 0.2 collective-permute-start.5
  15.3 5.2 %scan.1 = (f32[32,32768]{1,0:T(8,128)S(1)}, f32[32,32768]{1,0:T(8,128)S(1)}, s32[256,128]{1,0:T(8,128)S(1)}, s32[32,32768]{1,0:T(8,128)S(1)}) custom-call(f32[32,32768]{1,0:T(8,128)S(1)} %get-tuple-element.28.weight.refs_7_.refs_0_, s32[32,32768]{1,0:T(8,128)S(1)} %get-tuple-element.29.events.refs_8_.refs_1_, s32[256,128]{1,0:T(8,128)S(1)} %bitcast.6, ...), custom_call_target="tpu_custom_call" | custom-call | bytes 17500000 | tf_op jit(solution)/shard_map/scan/pallas_call | solution.py:37
  20.7 2.0 %inverse.1 = (f32[32,32768]{1,0:T(8,128)S(1)}, f32[32,32768]{1,0:T(8,128)S(1)}, f32[64,128]{1,0:T(8,128)S(1)}, f32[4,32,128]{2,1,0:T(8,128)S(1)}) custom-call(s32[2]{0:T(128)S(1)} %pad_add_fusion.meta.refs_0_, f32[32,128]{1,0:T(8,128)S(1)} %collective-permute-done.2.right.refs_1_, ...), custom_call_target="tpu_custom_call", output_to_operand_aliasing={{0}: (5, {}), {1}: (6, {})} | custom-call | bytes 5250000 | tf_op jit(solution)/shard_map/inverse/pallas_call | solution.py:37
  22.7 0.1 collective-permute-start.6
  22.8 1.2 %collective-permute-done.6.right.refs_1_ = f32[64,128]{1,0:T(8,128)S(1)} collective-permute-done((f32[64,128]{1,0:T(8,128)S(1)}, f32[64,128]{1,0:T(8,128)S(1)}, u32[]{:S(2)}, u32[]{:S(2)}) %collective-permute-start.6) | collective-permute-done | bytes 32800 | tf_op jit(solution)/shard_map/ppermute | solution.py:490
  24.0 0.7 collective-permute-start.7
  24.6 3.5 %collective-permute-start.8 = (f32[64,128]{1,0:T(8,128)S(1)}, f32[64,128]{1,0:T(8,128)S(1)}, u32[]{:S(2)}, u32[]{:S(2)}) collective-permute-start(f32[64,128]{1,0:T(8,128)S(1)} %pair.4), channel_id=1, source_target_pairs={{0,4},{1,5},{2,6},{3,7},{4,0},{5,1},{6,2},{7,3},{8,12},{9,13},{10,... | collective-permute-start | bytes 98312 | tf_op jit(solution)/shard_map/ppermute | solution.py:490
  28.1 0.3 collective-permute-start.9
  28.3 2.9 %accum.1 = (f32[32,32768]{1,0:T(8,128)S(1)}, f32[32,32768]{1,0:T(8,128)S(1)}, f32[4,64,128]{2,1,0:T(8,128)S(1)}) custom-call(f32[32,32768]{1,0:T(8,128)S(1)} %get-tuple-element.38.inv_one, f32[32,32768]{1,0:T(8,128)S(1)} %get-tuple-element.39.inv_two), custom_call_target="tpu_custom_call", output_to_operand_aliasing={{0}: (0, {}), {1}: (1, {})} | custom-call | bytes 10500000 | tf_op jit(solution)/shard_map/accum/pallas_call | solution.py:37
  31.3 2.5 %collective-permute-done.9.refs_4_ = f32[64,128]{1,0:T(8,128)S(1)} collective-permute-done((f32[64,128]{1,0:T(8,128)S(1)}, f32[64,128]{1,0:T(8,128)S(1)}, u32[]{:S(2)}, u32[]{:S(2)}) %collective-permute-start.9) | collective-permute-done | bytes 32800 | tf_op jit(solution)/shard_map/ppermute | solution.py:490
  33.8 0.7 bases.1
  34.5 0.6 collective-permute-start.12
  35.1 1.5 %collective-permute-start.10 = (f32[96,128]{1,0:T(8,128)S(1)}, f32[96,128]{1,0:T(8,128)S(1)}, u32[]{:S(2)}, u32[]{:S(2)}) collective-permute-start(f32[96,128]{1,0:T(8,128)S(1)} %get-tuple-element.43), channel_id=1, source_target_pairs={{0,8},{8,0},{16,24},{24,16},{1,9},{9,1},{17,25},{25,17},{2,10},{10... | collective-permute-start | bytes 147464 | tf_op jit(solution)/shard_map/ppermute | solution.py:490
  36.6 1.5 %collective-permute-start.11 = (f32[96,128]{1,0:T(8,128)S(1)}, f32[96,128]{1,0:T(8,128)S(1)}, u32[]{:S(2)}, u32[]{:S(2)}) collective-permute-start(f32[96,128]{1,0:T(8,128)S(1)} %get-tuple-element.44), channel_id=1, source_target_pairs={{0,16},{8,24},{16,0},{24,8},{1,17},{9,25},{17,1},{25,9},{2,18},{10... | collective-permute-start | bytes 147464 | tf_op jit(solution)/shard_map/ppermute | solution.py:490
  38.0 5.9 %leaf_sums.2.refs_5_.refs_0_ = f32[16,128]{1,0:T(8,128)S(1)} custom-call(s32[32,32768]{1,0:T(8,128)S(1)} %get-tuple-element.47.leaf, f32[32,32768]{1,0:T(8,128)S(1)} %get-tuple-element.28.weight.refs_7_.refs_0_, s32[32,32768]{1,0:T(8,128)S(1)} %get-tuple-element.29.events.refs_8_.refs_1_, f32[32,32768]{1,0:T(8,128)S(1)} %get-tuple-element.41.refs_9_.local_one.refs_2_, ...), custom_call_target="tpu_custom_call" | custom-call | bytes 17500000 | tf_op jit(solution)/shard_map/leaf_sums/pallas_call | solution.py:37
  43.9 0.9 %rest.1.rest_0_ = bf16[2,32,6144]{2,1,0:T(8,128)(2,1)S(1)} custom-call(s32[2]{0:T(128)S(1)} %pad_add_fusion.meta.refs_0_, f32[32,32768]{1,0:T(8,128)S(1)} %get-tuple-element.28.weight.refs_7_.refs_0_, s32[32,32768]{1,0:T(8,128)S(1)} %get-tuple-element.29.events.refs_8_.refs_1_, f32[32,32768]{1,0:T(8,128)S(1)} %get-tuple-element.41.refs_9_.local_one.refs_2_, ...), custom_call_target="tpu_custom_call" | custom-call | bytes 3500000 | tf_op jit(solution)/shard_map/rest/pallas_call | solution.py:37
  44.8 0.6 collective-permute-start.13
  45.4 5.9 %leaf_sums.3.refs_1_ = f32[16,128]{1,0:T(8,128)S(1)} custom-call(s32[32,32768]{1,0:T(8,128)S(1)} %get-tuple-element.47.leaf, f32[32,32768]{1,0:T(8,128)S(1)} %get-tuple-element.28.weight.refs_7_.refs_0_, s32[32,32768]{1,0:T(8,128)S(1)} %get-tuple-element.29.events.refs_8_.refs_1_, f32[32,32768]{1,0:T(8,128)S(1)} %get-tuple-element.41.refs_9_.local_one.refs_2_, ...), custom_call_target="tpu_custom_call" | custom-call | bytes 17500000 | tf_op jit(solution)/shard_map/leaf_sums/pallas_call | solution.py:37
  51.3 0.1 collective-permute-start.14
  51.4 1.2 %collective-permute-done.14.right = f32[32,128]{1,0:T(8,128)S(1)} collective-permute-done((f32[32,128]{1,0:T(8,128)S(1)}, f32[32,128]{1,0:T(8,128)S(1)}, u32[]{:S(2)}, u32[]{:S(2)}) %collective-permute-start.14) | collective-permute-done | bytes 16416 | tf_op jit(solution)/shard_map/ppermute | solution.py:490
  52.6 1.6 %collective-permute-start.15 = (f32[32,128]{1,0:T(8,128)S(1)}, f32[32,128]{1,0:T(8,128)S(1)}, u32[]{:S(2)}, u32[]{:S(2)}) collective-permute-start(f32[32,128]{1,0:T(8,128)S(1)} %pair.5.refs_3_), channel_id=1, source_target_pairs={{0,2},{1,3},{2,0},{3,1},{4,6},{5,7},{6,4},{7,5},{8,10},{9,11},{10,... | collective-permute-start | bytes 49160 | tf_op jit(solution)/shard_map/ppermute | solution.py:490
  54.1 2.6 %collective-permute-start.16 = (f32[32,128]{1,0:T(8,128)S(1)}, f32[32,128]{1,0:T(8,128)S(1)}, u32[]{:S(2)}, u32[]{:S(2)}) collective-permute-start(f32[32,128]{1,0:T(8,128)S(1)} %pair.5.refs_3_), channel_id=1, source_target_pairs={{0,4},{1,5},{2,6},{3,7},{4,0},{5,1},{6,2},{7,3},{8,12},{9,13},{10,... | collective-permute-start | bytes 49160 | tf_op jit(solution)/shard_map/ppermute | solution.py:490
  56.7 0.2 collective-permute-start.17
  57.0 7.7 %finish.1 = (bf16[2,128,8192]{2,1,0:T(8,128)(2,1)}, f32[32,32768]{1,0:T(8,128)S(1)}) custom-call(s32[2]{0:T(128)S(1)} %pad_add_fusion.meta.refs_0_, s32[256,128]{1,0:T(8,128)S(1)} %bitcast.7, s32[256,128]{1,0:T(8,128)S(1)} %get-tuple-element.30.refs_2_, s16[2,32,8192]{2,1,0:T(8,128)(2,1)S(1)} %collective-permute-done.refs_11_.refs_3_, ...), custom_call_target="tpu_custom_call" | custom-call | bytes 28000000 | tf_op jit(solution)/shard_map/finish/pallas_call | solution.py:37
  64.7 5.3 %update.1 = (f32[32,32768]{1,0:T(8,128)}, f32[32,64]{1,0:T(8,128)}, bf16[2,128,8192]{2,1,0:T(8,128)(2,1)}) custom-call(s32[2]{0:T(128)S(1)} %pad_add_fusion.meta.refs_0_, f32[32,32768]{1,0:T(8,128)S(1)} %get-tuple-element.46.pred, s32[32,32768]{1,0:T(8,128)S(1)} %get-tuple-element.47.leaf, ...), custom_call_target="tpu_custom_call", output_to_operand_aliasing={{2}: (5, {})} | custom-call | bytes 14000000 | tf_op jit(solution)/shard_map/update/pallas_call | solution.py:37
  (21 shorter events, 0.1 us)
Async XLA Ops:
  0.7 14.6 %copy-start = (s32[32768]{0:T(1024)S(1)}, s32[32768]{0:T(1024)}, u32[]{:S(2)}) copy-start(s32[32768]{0:T(1024)} %param.7) | copy-start | bytes 393220
  5.2 28.6 %collective-permute-start = (s16[2,32,8192]{2,1,0:T(8,128)(2,1)S(1)}, s16[2,32,8192]{2,1,0:T(8,128)(2,1)S(1)}, u32[]{:S(2)}, u32[]{:S(2)}) collective-permute-start(s16[2,32,8192]{2,1,0:T(8,128)(2,1)S(1)} %get-tuple-element.31), channel_id=1, source_target_pairs={{0,8},{8,0},{16,24},{24,16},{1,9},{9,1},{17,25},{25,17},{2,10},{10... | collective-permute-start | bytes 3145736 | tf_op jit(solution)/shard_map/ppermute | solution.py:490
  8.2 25.6 %collective-permute-start.1 = (s16[2,32,8192]{2,1,0:T(8,128)(2,1)S(1)}, s16[2,32,8192]{2,1,0:T(8,128)(2,1)S(1)}, u32[]{:S(2)}, u32[]{:S(2)}) collective-permute-start(s16[2,32,8192]{2,1,0:T(8,128)(2,1)S(1)} %get-tuple-element.32), channel_id=1, source_target_pairs={{0,16},{8,24},{16,0},{24,8},{1,17},{9,25},{17,1},{25,9},{2,18},{10... | collective-permute-start | bytes 3145736 | tf_op jit(solution)/shard_map/ppermute | solution.py:490
  9.8 1.2 %collective-permute-start.2 = (f32[32,128]{1,0:T(8,128)S(1)}, f32[32,128]{1,0:T(8,128)S(1)}, u32[]{:S(2)}, u32[]{:S(2)}) collective-permute-start(f32[32,128]{1,0:T(8,128)S(1)} %get-tuple-element.33.left), channel_id=1, source_target_pairs={{0,1},{1,0},{2,3},{3,2},{4,5},{5,4},{6,7},{7,6},{8,9},{9,8},{10,11... | collective-permute-start | bytes 49160 | tf_op jit(solution)/shard_map/ppermute | solution.py:490
  11.0 9.6 %collective-permute-start.3 = (f32[32,128]{1,0:T(8,128)S(1)}, f32[32,128]{1,0:T(8,128)S(1)}, u32[]{:S(2)}, u32[]{:S(2)}) collective-permute-start(f32[32,128]{1,0:T(8,128)S(1)} %pair.3), channel_id=1, source_target_pairs={{0,2},{1,3},{2,0},{3,1},{4,6},{5,7},{6,4},{7,5},{8,10},{9,11},{10,... | collective-permute-start | bytes 49160 | tf_op jit(solution)/shard_map/ppermute | solution.py:490
  12.5 8.1 %collective-permute-start.4 = (f32[32,128]{1,0:T(8,128)S(1)}, f32[32,128]{1,0:T(8,128)S(1)}, u32[]{:S(2)}, u32[]{:S(2)}) collective-permute-start(f32[32,128]{1,0:T(8,128)S(1)} %pair.3), channel_id=1, source_target_pairs={{0,4},{1,5},{2,6},{3,7},{4,0},{5,1},{6,2},{7,3},{8,12},{9,13},{10,... | collective-permute-start | bytes 49160 | tf_op jit(solution)/shard_map/ppermute | solution.py:490
  15.1 5.5 %collective-permute-start.5 = (f32[32,128]{1,0:T(8,128)S(1)}, f32[32,128]{1,0:T(8,128)S(1)}, u32[]{:S(2)}, u32[]{:S(2)}) collective-permute-start(f32[32,128]{1,0:T(8,128)S(1)} %pair.3), channel_id=1, source_target_pairs={{0,6},{1,7},{2,4},{3,5},{4,2},{5,3},{6,0},{7,1},{8,14},{9,15},{10,... | collective-permute-start | bytes 49160 | tf_op jit(solution)/shard_map/ppermute | solution.py:490
  22.7 1.3 %collective-permute-start.6 = (f32[64,128]{1,0:T(8,128)S(1)}, f32[64,128]{1,0:T(8,128)S(1)}, u32[]{:S(2)}, u32[]{:S(2)}) collective-permute-start(f32[64,128]{1,0:T(8,128)S(1)} %get-tuple-element.36.left), channel_id=1, source_target_pairs={{0,1},{1,0},{2,3},{3,2},{4,5},{5,4},{6,7},{7,6},{8,9},{9,8},{10,11... | collective-permute-start | bytes 98312 | tf_op jit(solution)/shard_map/ppermute | solution.py:490
  24.0 7.3 %collective-permute-start.7 = (f32[64,128]{1,0:T(8,128)S(1)}, f32[64,128]{1,0:T(8,128)S(1)}, u32[]{:S(2)}, u32[]{:S(2)}) collective-permute-start(f32[64,128]{1,0:T(8,128)S(1)} %pair.4), channel_id=1, source_target_pairs={{0,2},{1,3},{2,0},{3,1},{4,6},{5,7},{6,4},{7,5},{8,10},{9,11},{10,... | collective-permute-start | bytes 98312 | tf_op jit(solution)/shard_map/ppermute | solution.py:490
  24.6 6.7 %collective-permute-start.8 = (f32[64,128]{1,0:T(8,128)S(1)}, f32[64,128]{1,0:T(8,128)S(1)}, u32[]{:S(2)}, u32[]{:S(2)}) collective-permute-start(f32[64,128]{1,0:T(8,128)S(1)} %pair.4), channel_id=1, source_target_pairs={{0,4},{1,5},{2,6},{3,7},{4,0},{5,1},{6,2},{7,3},{8,12},{9,13},{10,... | collective-permute-start | bytes 98312 | tf_op jit(solution)/shard_map/ppermute | solution.py:490
  28.1 5.7 %collective-permute-start.9 = (f32[64,128]{1,0:T(8,128)S(1)}, f32[64,128]{1,0:T(8,128)S(1)}, u32[]{:S(2)}, u32[]{:S(2)}) collective-permute-start(f32[64,128]{1,0:T(8,128)S(1)} %pair.4), channel_id=1, source_target_pairs={{0,6},{1,7},{2,4},{3,5},{4,2},{5,3},{6,0},{7,1},{8,14},{9,15},{10,... | collective-permute-start | bytes 98312 | tf_op jit(solution)/shard_map/ppermute | solution.py:490
  34.5 9.4 %collective-permute-start.12 = (bf16[2,32,2048]{2,1,0:T(8,128)(2,1)S(1)}, bf16[2,32,2048]{2,1,0:T(8,128)(2,1)S(1)}, u32[]{:S(2)}, u32[]{:S(2)}) collective-permute-start(bf16[2,32,2048]{2,1,0:T(8,128)(2,1)S(1)} %get-tuple-element.48), channel_id=1, source_target_pairs={{0,24},{8,16},{16,8},{24,0},{1,25},{9,17},{17,9},{25,1},{2,26},{10... | collective-permute-start | bytes 786440 | tf_op jit(solution)/shard_map/ppermute | solution.py:490
  35.1 8.8 %collective-permute-start.10 = (f32[96,128]{1,0:T(8,128)S(1)}, f32[96,128]{1,0:T(8,128)S(1)}, u32[]{:S(2)}, u32[]{:S(2)}) collective-permute-start(f32[96,128]{1,0:T(8,128)S(1)} %get-tuple-element.43), channel_id=1, source_target_pairs={{0,8},{8,0},{16,24},{24,16},{1,9},{9,1},{17,25},{25,17},{2,10},{10... | collective-permute-start | bytes 147464 | tf_op jit(solution)/shard_map/ppermute | solution.py:490
  36.6 7.3 %collective-permute-start.11 = (f32[96,128]{1,0:T(8,128)S(1)}, f32[96,128]{1,0:T(8,128)S(1)}, u32[]{:S(2)}, u32[]{:S(2)}) collective-permute-start(f32[96,128]{1,0:T(8,128)S(1)} %get-tuple-element.44), channel_id=1, source_target_pairs={{0,16},{8,24},{16,0},{24,8},{1,17},{9,25},{17,1},{25,9},{2,18},{10... | collective-permute-start | bytes 147464 | tf_op jit(solution)/shard_map/ppermute | solution.py:490
  44.8 19.9 %collective-permute-start.13 = (bf16[2,32,6144]{2,1,0:T(8,128)(2,1)S(1)}, bf16[2,32,6144]{2,1,0:T(8,128)(2,1)S(1)}, u32[]{:S(2)}, u32[]{:S(2)}) collective-permute-start(bf16[2,32,6144]{2,1,0:T(8,128)(2,1)S(1)} %rest.1.rest_0_), channel_id=1, source_target_pairs={{0,24},{8,16},{16,8},{24,0},{1,25},{9,17},{17,9},{25,1},{2,26},{10... | collective-permute-start | bytes 2359304 | tf_op jit(solution)/shard_map/ppermute | solution.py:490
  51.3 1.2 %collective-permute-start.14 = (f32[32,128]{1,0:T(8,128)S(1)}, f32[32,128]{1,0:T(8,128)S(1)}, u32[]{:S(2)}, u32[]{:S(2)}) collective-permute-start(f32[32,128]{1,0:T(8,128)S(1)} %join.1.left), channel_id=1, source_target_pairs={{0,1},{1,0},{2,3},{3,2},{4,5},{5,4},{6,7},{7,6},{8,9},{9,8},{10,11... | collective-permute-start | bytes 49160 | tf_op jit(solution)/shard_map/ppermute | solution.py:490
  52.6 12.1 %collective-permute-start.15 = (f32[32,128]{1,0:T(8,128)S(1)}, f32[32,128]{1,0:T(8,128)S(1)}, u32[]{:S(2)}, u32[]{:S(2)}) collective-permute-start(f32[32,128]{1,0:T(8,128)S(1)} %pair.5.refs_3_), channel_id=1, source_target_pairs={{0,2},{1,3},{2,0},{3,1},{4,6},{5,7},{6,4},{7,5},{8,10},{9,11},{10,... | collective-permute-start | bytes 49160 | tf_op jit(solution)/shard_map/ppermute | solution.py:490
  54.1 10.6 %collective-permute-start.16 = (f32[32,128]{1,0:T(8,128)S(1)}, f32[32,128]{1,0:T(8,128)S(1)}, u32[]{:S(2)}, u32[]{:S(2)}) collective-permute-start(f32[32,128]{1,0:T(8,128)S(1)} %pair.5.refs_3_), channel_id=1, source_target_pairs={{0,4},{1,5},{2,6},{3,7},{4,0},{5,1},{6,2},{7,3},{8,12},{9,13},{10,... | collective-permute-start | bytes 49160 | tf_op jit(solution)/shard_map/ppermute | solution.py:490
  56.7 8.0 %collective-permute-start.17 = (f32[32,128]{1,0:T(8,128)S(1)}, f32[32,128]{1,0:T(8,128)S(1)}, u32[]{:S(2)}, u32[]{:S(2)}) collective-permute-start(f32[32,128]{1,0:T(8,128)S(1)} %pair.5.refs_3_), channel_id=1, source_target_pairs={{0,6},{1,7},{2,4},{3,5},{4,2},{5,3},{6,0},{7,1},{8,14},{9,15},{10,... | collective-permute-start | bytes 49160 | tf_op jit(solution)/shard_map/ppermute | solution.py:490

commit v3 on v2

--- a/solution.py
+++ b/solution.py
@@ -15,6 +15,7 @@
 BF16 = jnp.bfloat16
 I16 = jnp.int16
 CODE = 32766.0 / 6.0
+MIDDLE = 32768
 MIB = 1024 * 1024
 
 
@@ -77,33 +78,34 @@
     def one(turn, carry):
         source = span(share_of(meta, d, share) + turn * step, step)
         at = span(turn * step, step)
-        message[0, :, at] = jnp.round(pred[:, source] * CODE).astype(jnp.int32).astype(I16)
+        above = (pred[:, source] * CODE + (MIDDLE + 0.5)).astype(jnp.int32)
+        message[0, :, at] = (above - MIDDLE).astype(I16)
         message[1, :, at] = events[:, source].astype(I16)
         return carry
 
     lax.fori_loop(0, share // step, one, 0, unroll=2)
 
 
-def front_body(partners, turns, meta, pred_in, events_in, events, weight, total, *rest):
-    messages, pred, sems = rest[:-2], rest[-2], rest[-1]
+def front_body(partners, turns, parts, meta, pred_in, events_in, events, weight, total, *rest):
+    messages, pred, sems, share_sems = rest[:-3], rest[-3], rest[-2], rest[-1]
     rows, length = pred.shape
     width = length // turns
-
-    def copies(turn):
+    share = length // parts
+    loads = []
+    for turn in range(turns):
         at = span(turn * width, width)
-        return [
-            pltpu.make_async_copy(pred_in.at[:, at], pred.at[:, at], sems.at[0, turn]),
-            pltpu.make_async_copy(events_in.at[:, at], events.at[:, at], sems.at[1, turn]),
-        ]
-
-    for turn in range(turns):
-        for copy in copies(turn):
-            copy.start()
+        loads.append(pltpu.make_async_copy(pred_in.at[:, at], pred.at[:, at], sems.at[turn]))
+    order = list(partners) + [d for d in range(parts) if d not in partners]
+    fetches = []
+    for k, d in enumerate(order):
+        at = span(share_of(meta, d, share), share)
+        fetches.append(pltpu.make_async_copy(events_in.at[:, at], events.at[:, at], share_sems.at[k]))
+    for copy in loads + fetches:
+        copy.start()
     step = min(width, 1024)
     acc = jnp.zeros((rows, LANES), F32)
     for turn in range(turns):
-        for copy in copies(turn):
-            copy.wait()
+        loads[turn].wait()
 
         def one(k, acc):
             at = span(turn * width + k * step, step)
@@ -113,8 +115,11 @@
 
         acc = lax.fori_loop(0, width // step, one, acc, unroll=2)
     total[...] = lane_sum(acc)
-    for d, message in zip(partners, messages):
+    for k, (d, message) in enumerate(zip(partners, messages)):
+        fetches[k].wait()
         encode(meta, d, pred, events, message)
+    for copy in fetches[len(partners) :]:
+        copy.wait()
 
 
 def pair_dot(x, matrix):
@@ -147,8 +152,25 @@
     return jnp.concatenate([ref[:, span(base + k * WIDE, WIDE)] for k in range(count)], axis=0)
 
 
+FIELDS = 4
+BITS = 8
+
+
+def pack(x):
+    size = x.shape[0] // FIELDS
+    out = x[:size]
+    for k in range(1, FIELDS):
+        out = out + lax.shift_left(x[k * size : (k + 1) * size], BITS * k)
+    return out
+
+
+def unpack(x):
+    return jnp.concatenate([(lax.shift_right_logical(x, BITS * k) & 255).astype(F32) for k in range(FIELDS)], axis=0)
+
+
 def group_events(observed, counts, first, last):
-    return jnp.where(first == 1, take(counts, last) - counts + observed, 0.0)
+    held = pack(counts.astype(jnp.int32))
+    return jnp.where(first == 1, take(held, last) - held + pack(observed), 0)
 
 
 def scan_body(weight, events, tie, leaf_in, suffix, grouped, last, leaf, upper, lower, sem):
@@ -163,8 +185,8 @@
 
     def one(turn, carry):
         base = (steps - 1 - turn) * (WIDE * count)
-        observed = stacked(events, base, count).astype(F32)
-        counts = jnp.dot(observed.astype(BF16), lower[...], preferred_element_type=F32)
+        observed = stacked(events, base, count)
+        counts = jnp.dot(observed.astype(F32).astype(BF16), lower[...], preferred_element_type=F32)
         summed = pair_dot(stacked(weight, base, count), upper[...])
         for k in range(count - 1, -1, -1):
             mine = slice(k * rows, (k + 1) * rows)
@@ -176,8 +198,8 @@
                 grouped[:, at] = group_events(
                     observed[mine, lanes],
                     counts[mine, lanes],
-                    jnp.broadcast_to(tie[block, :], (rows, LANES)),
-                    jnp.broadcast_to(last[block, :], (rows, LANES)),
+                    jnp.broadcast_to(tie[block, :], (rows // FIELDS, LANES)),
+                    jnp.broadcast_to(last[block, :], (rows // FIELDS, LANES)),
                 )
             carry = carry + jnp.broadcast_to(summed[mine, 0:1], (rows, LANES))
         return carry
@@ -188,12 +210,6 @@
 
 def pair_body(left, right, *refs):
     refs[-1][...] = left[...] + right[...]
-
-
-def join_body(*refs):
-    rows = refs[0].shape[0]
-    for k, ref in enumerate(refs[:-1]):
-        refs[-1][k * rows : (k + 1) * rows, :] = ref[...]
 
 
 def gathered_sum(meta, refs, later):
@@ -222,7 +238,7 @@
         sum_one, sum_two = acc
         at = span(turn * step, step)
         inverse = 1.0 / (suffix[:, at] + widen(later, step))
-        first = grouped[:, at] * inverse
+        first = unpack(grouped[:, at]) * inverse
         second = first * inverse
         inv_one[:, at] = first
         inv_two[:, at] = second
@@ -265,31 +281,10 @@
     return scaled - observed, scaled - weight * weight * accum_two
 
 
-def pieces(first, at_rows, weight, events, local_one, local_two, bases, out, at_lanes=0):
-    rows, length = out.shape[1], at_rows
-    step = math.gcd(length, 512)
-
-    def one(turn, carry):
-        source = span(first + turn * step, step)
-        at = span(at_lanes + turn * step, step)
-        grad, hess = derivatives(
-            weight[:, source],
-            events[:, source].astype(F32),
-            local_one[:, source] + widen(bases[:rows, :], step),
-            local_two[:, source] + widen(bases[rows:, :], step),
-        )
-        out[0, :, at] = grad.astype(BF16)
-        out[1, :, at] = hess.astype(BF16)
-        return carry
-
-    lax.fori_loop(0, length // step, one, 0, unroll=2)
-
-
-def bases_body(count, links, diagonals, share, *refs):
+def bases_body(count, links, *refs):
     meta, others = refs[0], refs[1 : 1 + count]
-    after, before, *scans = refs[1 + count : 7 + count]
-    bases, *messages = refs[len(refs) - 1 - len(links) - len(diagonals) :]
-    messages, early = messages[: len(links)], messages[len(links) :]
+    after, before = refs[1 + count : 3 + count]
+    bases, *messages = refs[len(refs) - 1 - len(links) :]
     rows = after.shape[1]
     earlier = gathered_sum(meta, others, False)
     bases[...] = earlier
@@ -297,23 +292,18 @@
         part = share_of(meta, d, 1)
         message[:rows] = after[part]
         message[rows:] = before[part] + earlier
-    for d, out in zip(diagonals, early):
-        pieces(share_of(meta, d, share), out.shape[2], *scans, bases, out)
-
-
-def rest_body(diagonals, share, meta, *refs):
-    for d, out in zip(diagonals, refs[len(refs) - len(diagonals) :]):
-        size = out.shape[2]
-        pieces(share_of(meta, d, share) + share - size, size, *refs[:5], out)
-
-
-def place_pieces(meta, partners, arrived, out, sems, last=False):
+
+
+def release_body(*refs):
+    pass
+
+
+def place_pieces(meta, partners, arrived, out, sems):
     copies = []
     for k, (d, piece) in enumerate(zip(partners, arrived)):
-        _, rows, size = piece.shape
+        rows = piece.shape[1]
         where = pl.ds(pl.multiple_of(share_of(meta, d, rows), rows), rows)
-        lanes = pl.ds(out.shape[2] - size if last else 0, size)
-        copies += [pltpu.make_async_copy(piece.at[v], out.at[v, where, lanes], sems.at[k, v]) for v in (0, 1)]
+        copies += [pltpu.make_async_copy(piece.at[v], out.at[v, where, :], sems.at[k, v]) for v in (0, 1)]
     return copies
 
 
@@ -321,24 +311,19 @@
     meta, tie, last = refs[:3]
     refs = refs[3:]
     messages, base = refs[: len(partners)], refs[len(partners) : 2 * len(partners)]
-    refs = refs[2 * len(partners) :]
-    weight, events, local_one, local_two, own_bases = refs[:5]
-    pred_in, out, pred, scratch, kept, inv_one, inv_two, upper, lower, sems, fetch_sem = refs[5:]
+    own, pred_in, out, pred, scratch, kept, inv_one, inv_two, upper, lower, sems, own_sems, fetch_sem = refs[2 * len(partners) :]
     fetch = pltpu.make_async_copy(pred_in, pred, fetch_sem)
     fetch.start()
+    own_copies = place_pieces(meta, [0], [own], out, own_sems)
+    for copy in own_copies:
+        copy.start()
     _, rows, share = kept.shape
-    count = min(8, share // WIDE)
+    count = share // (WIDE * sems.shape[2])
     steps = share // (WIDE * count)
     turn_width = WIDE * count
     first_block = share_of(meta, 0, share) // LANES
     upper[...] = triangle(True)
     lower[...] = triangle(False)
-    places = list(partners) + [0]
-    copies = place_pieces(meta, places, [scratch.at[slot] for slot in range(len(places))], out, sems)
-    slot = len(partners)
-    pieces(share_of(meta, 0, share), share, weight, events, local_one, local_two, own_bases, scratch.at[slot])
-    for v in (0, 1):
-        copies[2 * slot + v].start()
 
     def one(turn, carry):
         at_base = (steps - 1 - turn) * turn_width
@@ -347,8 +332,8 @@
             coded = jnp.concatenate([messages[slot][0, :, span(at_base + k * WIDE, WIDE)] for k in range(count)], axis=0)
             values = jnp.exp(coded.astype(jnp.int32).astype(F32) * (1.0 / CODE))
             seen = jnp.concatenate([messages[slot][1, :, span(at_base + k * WIDE, WIDE)] for k in range(count)], axis=0)
-            observed = seen.astype(jnp.int32).astype(F32)
-            counts = jnp.dot(observed.astype(BF16), lower[...], preferred_element_type=F32)
+            observed = seen.astype(jnp.int32)
+            counts = jnp.dot(observed.astype(F32).astype(BF16), lower[...], preferred_element_type=F32)
             summed = pair_dot(values, upper[...])
             so_far = carry[slot]
             for k in range(count - 1, -1, -1):
@@ -358,20 +343,32 @@
                     lanes = slice(half * LANES, (half + 1) * LANES)
                     at = span(at_base + k * WIDE + half * LANES, LANES)
                     block = pl.ds(first_block + (at_base + k * WIDE) // LANES + half, 1)
-                    inverse = 1.0 / (summed[mine, lanes] + so_far)
                     grouped = group_events(
                         observed[mine, lanes],
                         counts[mine, lanes],
-                        jnp.broadcast_to(tie[block, :], (rows, LANES)),
-                        jnp.broadcast_to(last[block, :], (rows, LANES)),
+                        jnp.broadcast_to(tie[block, :], (rows // FIELDS, LANES)),
+                        jnp.broadcast_to(last[block, :], (rows // FIELDS, LANES)),
                     )
-                    inv_one[slot, :, at] = grouped * inverse
-                    inv_two[slot, :, at] = grouped * inverse * inverse
+                    inverse = 1.0 / (summed[mine, lanes] + so_far)
+                    first = unpack(grouped) * inverse
+                    inv_one[slot, :, at] = first
+                    inv_two[slot, :, at] = first * inverse
                 so_far = so_far + jnp.broadcast_to(summed[mine, 0:1], (rows, LANES))
             made.append(so_far)
         return tuple(made)
 
     lax.fori_loop(0, steps, one, tuple(b[:rows, :] for b in base))
+
+    def copies(turn):
+        lanes = span(turn * turn_width, turn_width)
+        made = []
+        for slot, d in enumerate(partners):
+            where = pl.ds(pl.multiple_of(share_of(meta, d, rows), rows), rows)
+            made += [
+                pltpu.make_async_copy(scratch.at[slot, v, :, lanes], out.at[v, where, lanes], sems.at[slot, v, turn])
+                for v in (0, 1)
+            ]
+        return made
 
     def two(turn, carry):
         at_base = turn * turn_width
@@ -394,12 +391,15 @@
                 so_one = so_one + jnp.broadcast_to(sum_one[mine, WIDE - 1 :], (rows, LANES))
                 so_two = so_two + jnp.broadcast_to(sum_two[mine, WIDE - 1 :], (rows, LANES))
             made.append((so_one, so_two))
+        for copy in copies(turn):
+            copy.start()
         return tuple(made)
 
     lax.fori_loop(0, steps, two, tuple((b[rows : 2 * rows, :], b[2 * rows :, :]) for b in base))
-    for copy in copies[: 2 * len(partners)]:
-        copy.start()
-    for copy in copies:
+    for turn in range(steps):
+        for copy in copies(turn):
+            copy.wait()
+    for copy in own_copies:
         copy.wait()
     fetch.wait()
 
@@ -409,15 +409,13 @@
 HIGH = LEAVES // LOW
 
 
-def leaf_sums_body(group, leaf, weight, events, local_one, local_two, bases, *rest):
-    sums, acc = rest[-2:]
-    rows, length = weight.shape
-    step = min(length, 2048)
-    mine = pl.ds(group * GROUP, GROUP)
-    acc[...] = jnp.zeros_like(acc)
-
-    def one(turn, carry):
-        at = span(turn * step, step)
+def leaf_step(at, leaf, weight, events, local_one, local_two, bases, acc, out, at_out):
+    rows = weight.shape[0]
+    step = at.size
+    zero = jnp.zeros((GROUP, step), BF16)
+    unit = jnp.ones((GROUP, step), BF16)
+    for group in range(rows // GROUP):
+        mine = pl.ds(group * GROUP, GROUP)
         pair = derivatives(
             weight[mine, at],
             events[mine, at].astype(F32),
@@ -431,35 +429,59 @@
         for value in pair:
             upper = value.astype(BF16)
             terms += [upper, (value - upper.astype(F32)).astype(BF16)]
-        zero = jnp.zeros((GROUP, step), BF16)
-        unit = jnp.ones((GROUP, step), BF16)
+        if out is not None:
+            out[0, mine, at_out] = terms[0]
+            out[1, mine, at_out] = terms[2]
         left = jnp.concatenate([jnp.where(high == h, term, zero) for term in terms for h in range(HIGH)], axis=0)
         right = jnp.concatenate([jnp.where(low == k, unit, zero) for k in range(LOW)], axis=0)
-        acc[...] += lax.dot_general(left, right, (((1,), (1,)), ((), ())), preferred_element_type=F32)
-        return carry
-
-    lax.fori_loop(0, length // step, one, 0, unroll=4)
+        acc[group] += lax.dot_general(left, right, (((1,), (1,)), ((), ())), preferred_element_type=F32)
+
+
+def leaf_shares(shares, size, meta, ins, outs, acc):
+    step = min(size, 2048)
+    for k, d in enumerate(shares):
+        start = share_of(meta, d, size)
+
+        def one(turn, carry):
+            at = turn * step
+            leaf_step(span(start + at, step), *ins, acc, outs[k] if k < len(outs) else None, span(at, step))
+            return carry
+
+        lax.fori_loop(0, size // step, one, 0, unroll=4)
+
+
+def leaf_first_body(shares, size, meta, *refs):
+    acc = refs[-1]
+    acc[...] = jnp.zeros_like(acc)
+    leaf_shares(shares, size, meta, refs[:6], refs[6:-1], acc)
+
+
+def leaf_rest_body(shares, size, meta, *refs):
+    own, sums, acc = refs[-3:]
+    leaf_shares(shares, size, meta, refs[:6], [own], acc)
     width = LOW * GROUP
     side = HIGH * GROUP
     same = lax.broadcasted_iota(jnp.int32, (side, width), 0) % GROUP == lax.broadcasted_iota(jnp.int32, (side, width), 1) % GROUP
     source = lax.broadcasted_iota(jnp.int32, (width, LANES), 0) // GROUP
     target = lax.broadcasted_iota(jnp.int32, (width, LANES), 1)
-    out = jnp.zeros((GROUP, LANES), F32)
-    for value in (0, 1):
-        both = acc[2 * value * side : (2 * value + 1) * side] + acc[(2 * value + 1) * side : (2 * value + 2) * side]
-        both = jnp.where(same, both, 0.0)
-        for h in range(HIGH):
-            place = (target == source + (h * LOW + value * LEAVES)).astype(F32)
-            out = out + jnp.dot(both[h * GROUP : (h + 1) * GROUP], place, precision=lax.Precision.HIGHEST, preferred_element_type=F32)
-    sums[...] = out
+    for group in range(acc.shape[0]):
+        out = jnp.zeros((GROUP, LANES), F32)
+        for value in (0, 1):
+            both = acc[group, 2 * value * side : (2 * value + 1) * side] + acc[group, (2 * value + 1) * side : (2 * value + 2) * side]
+            both = jnp.where(same, both, 0.0)
+            for h in range(HIGH):
+                place = (target == source + (h * LOW + value * LEAVES)).astype(F32)
+                out = out + jnp.dot(
+                    both[h * GROUP : (h + 1) * GROUP], place, precision=lax.Precision.HIGHEST, preferred_element_type=F32
+                )
+        sums[group * GROUP : (group + 1) * GROUP, :] = out
 
 
 def update_body(turns, partners, meta, pred, leaf, *refs):
-    early, late, refs = refs[: len(partners)], refs[len(partners) : 2 * len(partners)], refs[2 * len(partners) + 1 :]
-    sums, (new_pred, leaf_weights, out, scratch, sems, early_sems, late_sems) = refs[:-7], refs[-7:]
+    arrived, refs = refs[: len(partners)], refs[len(partners) + 1 :]
+    sums, (new_pred, leaf_weights, out, scratch, sems, piece_sems) = refs[:-6], refs[-6:]
     rows, length = leaf.shape
-    copies = place_pieces(meta, partners, early, out, early_sems)
-    copies += place_pieces(meta, partners, late, out, late_sems, True)
+    copies = place_pieces(meta, partners, arrived, out, piece_sems)
     for copy in copies:
         copy.start()
     both = [ref[...] for ref in sums]
@@ -511,13 +533,13 @@
     diagonals = [d for d in range(1, parts) if d not in links]
     message = resident((2, rows, share), I16)
     observed, weight, total, *messages = call(
-        functools.partial(front_body, links, turns),
+        functools.partial(front_body, links, turns, parts),
         [resident(wide, jnp.int32), resident(wide, F32), resident((rows, LANES), F32)] + [message] * len(links),
         meta,
         far(predictions),
         far(events),
         hbm=(1, 2),
-        scratch=[pltpu.VMEM(wide, F32), dma((2, turns))],
+        scratch=[pltpu.VMEM(wide, F32), dma((turns,)), dma((parts,))],
         name="front",
         us=4,
     )
@@ -525,7 +547,12 @@
     _, from_later = across(total, "tm")
     suffix, grouped, last, leaf = call(
         scan_body,
-        [resident(wide, F32), resident(wide, F32), resident((blocks, LANES), jnp.int32), resident(wide, jnp.int32)],
+        [
+            resident(wide, F32),
+            resident((rows // FIELDS, length), jnp.int32),
+            resident((blocks, LANES), jnp.int32),
+            resident(wide, jnp.int32),
+        ],
         weight,
         observed,
         tie,
@@ -543,7 +570,7 @@
         *from_later,
         suffix,
         grouped,
-        aliases={1 + count: 0, 2 + count: 1},
+        aliases={1 + count: 0},
         name="inverse",
         us=1.5,
     )
@@ -559,55 +586,57 @@
         us=3,
     )
     scans = (weight, observed, local_one, local_two)
-    early_rows = share // 4
     bases, *sent = call(
-        functools.partial(bases_body, count, links, diagonals, share),
-        [resident((2 * rows, LANES), F32)]
-        + [resident((3 * rows, LANES), F32)] * len(links)
-        + [resident((2, rows, early_rows), BF16)] * len(diagonals),
+        functools.partial(bases_body, count, links),
+        [resident((2 * rows, LANES), F32)] + [resident((3 * rows, LANES), F32)] * len(links),
         meta,
         *from_earlier,
         after,
         before,
-        *scans,
-        *coded.values(),
         name="bases",
         us=1,
     )
     base = {d: swap(m, "ep", d) for d, m in zip(links, sent)}
-    early = [swap(m, "ep", d) for d, m in zip(diagonals, sent[len(links) :])]
-    late = []
-    partial_sums = []
-    for group in range(rows // GROUP):
-        partial_sums += call(
-            functools.partial(leaf_sums_body, group),
-            [resident((GROUP, LANES), F32)],
-            leaf,
-            *scans,
-            bases,
-            *(sent if late else []),
-            scratch=[pltpu.VMEM((4 * HIGH * GROUP, LOW * GROUP), F32)],
-            name="leaf_sums",
-            us=5,
-        )
-        if not late:
-            sent = call(
-                functools.partial(rest_body, diagonals, share),
-                [resident((2, rows, share - early_rows), BF16)] * len(diagonals),
-                meta,
-                *scans,
-                bases,
-                *partial_sums,
-                *base.values(),
-                *early,
-                name="rest",
-                us=1,
-            )
-            late = [swap(m, "ep", d) for d, m in zip(diagonals, sent)]
-    (own_sums,) = call(join_body, [resident((rows, LANES), F32)], *partial_sums, name="join", us=0.3, limit=2)
+    finished = resident((2, rows, share), BF16)
+    sums_shape = resident((rows // GROUP, 4 * HIGH * GROUP, LOW * GROUP), F32)
+    *sent, acc = call(
+        functools.partial(leaf_first_body, diagonals, share),
+        [finished] * len(diagonals) + [sums_shape],
+        meta,
+        leaf,
+        *scans,
+        bases,
+        name="leaf_first",
+        us=3,
+    )
+    sent = call(
+        release_body,
+        [finished] * len(diagonals),
+        *sent,
+        *base.values(),
+        *coded.values(),
+        aliases={k: k for k in range(len(diagonals))},
+        name="release",
+        us=0.1,
+        limit=2,
+    )
+    arrived = [swap(m, "ep", d) for d, m in zip(diagonals, sent)]
+    own, own_sums, _ = call(
+        functools.partial(leaf_rest_body, [0] + links, share),
+        [finished, resident((rows, LANES), F32), sums_shape],
+        meta,
+        leaf,
+        *scans,
+        bases,
+        acc,
+        *sent,
+        aliases={7: 2},
+        name="leaf_rest",
+        us=9,
+    )
     both, others = across(own_sums, "tm", base.values())
     piece = pltpu.VMEM((len(links), rows, share), F32)
-    args = [meta, tie, last, *[coded[d] for d in links], *[base[d] for d in links], *scans, bases]
+    args = [meta, tie, last, *[coded[d] for d in links], *[base[d] for d in links], own]
     grad_hess, pred = call(
         functools.partial(finish_body, links),
         [jax.ShapeDtypeStruct((2, rows * parts, share), BF16), resident(wide, F32)],
@@ -615,30 +644,29 @@
         far(predictions),
         hbm=(len(args),),
         hbm_out=(0,),
-        scratch=[pltpu.VMEM((len(links) + 1, 2, rows, share), BF16)]
+        scratch=[pltpu.VMEM((len(links), 2, rows, share), BF16)]
         + [piece] * 3
         + [pltpu.VMEM((WIDE, WIDE), BF16)] * 2
-        + [dma((len(links) + 1, 2)), dma],
+        + [dma((len(links), 2, 4)), dma((1, 2)), dma],
         name="finish",
         us=8,
         limit=14,
     )
-    at_out = 3 + 2 * len(diagonals)
+    at_out = 3 + len(diagonals)
     new_pred, leaf_weights, grad_hess = call(
         functools.partial(update_body, turns, diagonals),
         [jax.ShapeDtypeStruct(wide, F32), jax.ShapeDtypeStruct((rows, LEAVES), F32), jax.ShapeDtypeStruct(grad_hess.shape, BF16)],
         meta,
         pred,
         leaf,
-        *early,
-        *late,
+        *arrived,
         grad_hess,
         both,
         *others[1:],
         hbm=range(3, at_out + 1),
         hbm_out=(0, 2),
         aliases={at_out: 2},
-        scratch=[pltpu.VMEM(wide, F32), dma((turns,)), dma((max(1, len(diagonals)), 2)), dma((max(1, len(diagonals)), 2))],
+        scratch=[pltpu.VMEM(wide, F32), dma((turns,)), dma((max(1, len(diagonals)), 2))],
         name="update",
         us=4,
     )

time: 70.2 us -> 67.1 us (0.956)
  Pallas kernels: 41.1 us -> 37.7 us
  waiting for transfers between devices: 6.11 us -> 7.41 us
  starting transfers between devices: 22 us -> 20.8 us
    pallas_call x14 -> x13, Pallas kernels: 41.1 us -> 37.7 us  [call(): pl.pallas_call(body, out_shape=outs, in_specs=[anywhere if k in hbm else...]
    ppermute x18 -> x17, waiting for transfers between devices: 6.11 us -> 7.41 us  [swap(): lax.ppermute(array, axis, [(i, i ^ d) for i in range(lax.axis_size(axis))])]
    ppermute x18 -> x17, starting transfers between devices: 22 us -> 20.8 us  [swap(): lax.ppermute(array, axis, [(i, i ^ d) for i in range(lax.axis_size(axis))])]
  transfers between devices with their start and end apart: 18 -> 17, of which waited for: 4 -> 8; matrix products, arithmetic and copies ran while one was open for 0% -> 0% of each run, Pallas kernels for 42% -> 42%
where the time goes in v3:
time: 67.1 us; the launch traced here: 67 us
  Pallas kernels  37.7 us (56%)
  starting transfers between devices  20.8 us (31%)
  waiting for transfers between devices  7.41 us (11%)
  between operations  0.96 us (1%)
    pallas_call x13, Pallas kernels, call(): pl.pallas_call(body, out_shape=outs, in_specs=[anywhere if k in hbm else...  37.7 us
    ppermute x17, starting transfers between devices, swap(): lax.ppermute(array, axis, [(i, i ^ d) for i in range(lax.axis_size(axis))])  20.8 us
    ppermute x17, waiting for transfers between devices, swap(): lax.ppermute(array, axis, [(i, i ^ d) for i in range(lax.axis_size(axis))])  7.41 us
  transfers between devices with their start and end apart: 17, of which 8 were waited for; matrix products, arithmetic and copies ran while one was open for 0% of the time, Pallas kernels for 42%

profile of v3, /device:TPU:0, one launch (start us, length us, event | category | flops | bytes accessed | tf_op | source)
XLA Modules:
  0.0 67.0 jit_solution(12151885661965855839)
XLA Ops:
  0.6 0.1 pad_add_fusion.meta.refs_0_
  0.7 4.4 %front.1 = (s32[32,32768]{1,0:T(8,128)S(1)}, f32[32,32768]{1,0:T(8,128)S(1)}, f32[32,128]{1,0:T(8,128)S(1)}, s16[2,32,8192]{2,1,0:T(8,128)(2,1)S(1)}, s16[2,32,8192]{2,1,0:T(8,128)(2,1)S(1)}) custom-call(s32[2]{0:T(128)S(1)} %pad_add_fusion.meta.refs_0_, f32[32,32768]{1,0:T(8,128)} %refs_8_.1, s32[32,32768]{1,0:T(8,128)} %events_in.1), custom_call_target="tpu_custom_call" | custom-call | bytes 14000000 | tf_op jit(solution)/shard_map/front/pallas_call | solution.py:38
  5.1 3.0 %collective-permute-start = (s16[2,32,8192]{2,1,0:T(8,128)(2,1)S(1)}, s16[2,32,8192]{2,1,0:T(8,128)(2,1)S(1)}, u32[]{:S(2)}, u32[]{:S(2)}) collective-permute-start(s16[2,32,8192]{2,1,0:T(8,128)(2,1)S(1)} %get-tuple-element.34), channel_id=1, source_target_pairs={{0,8},{8,0},{16,24},{24,16},{1,9},{9,1},{17,25},{25,17},{2,10},{10... | collective-permute-start | bytes 3145736 | tf_op jit(solution)/shard_map/ppermute | solution.py:512
  8.1 1.5 %collective-permute-start.1 = (s16[2,32,8192]{2,1,0:T(8,128)(2,1)S(1)}, s16[2,32,8192]{2,1,0:T(8,128)(2,1)S(1)}, u32[]{:S(2)}, u32[]{:S(2)}) collective-permute-start(s16[2,32,8192]{2,1,0:T(8,128)(2,1)S(1)} %get-tuple-element.35), channel_id=1, source_target_pairs={{0,16},{8,24},{16,0},{24,8},{1,17},{9,25},{17,1},{25,9},{2,18},{10... | collective-permute-start | bytes 3145736 | tf_op jit(solution)/shard_map/ppermute | solution.py:512
  9.6 1.2 %collective-permute-done.2.right.refs_1_ = f32[32,128]{1,0:T(8,128)S(1)} collective-permute-done((f32[32,128]{1,0:T(8,128)S(1)}, f32[32,128]{1,0:T(8,128)S(1)}, u32[]{:S(2)}, u32[]{:S(2)}) %collective-permute-start.2) | collective-permute-done | bytes 16416 | tf_op jit(solution)/shard_map/ppermute | solution.py:512
  10.8 1.6 %collective-permute-start.3 = (f32[32,128]{1,0:T(8,128)S(1)}, f32[32,128]{1,0:T(8,128)S(1)}, u32[]{:S(2)}, u32[]{:S(2)}) collective-permute-start(f32[32,128]{1,0:T(8,128)S(1)} %pair.3), channel_id=1, source_target_pairs={{0,2},{1,3},{2,0},{3,1},{4,6},{5,7},{6,4},{7,5},{8,10},{9,11},{10,... | collective-permute-start | bytes 49160 | tf_op jit(solution)/shard_map/ppermute | solution.py:512
  12.4 2.6 %collective-permute-start.4 = (f32[32,128]{1,0:T(8,128)S(1)}, f32[32,128]{1,0:T(8,128)S(1)}, u32[]{:S(2)}, u32[]{:S(2)}) collective-permute-start(f32[32,128]{1,0:T(8,128)S(1)} %pair.3), channel_id=1, source_target_pairs={{0,4},{1,5},{2,6},{3,7},{4,0},{5,1},{6,2},{7,3},{8,12},{9,13},{10,... | collective-permute-start | bytes 49160 | tf_op jit(solution)/shard_map/ppermute | solution.py:512
  15.0 0.2 collective-permute-start.5
  15.2 4.2 %scan.1 = (f32[32,32768]{1,0:T(8,128)S(1)}, s32[8,32768]{1,0:T(8,128)S(1)}, s32[256,128]{1,0:T(8,128)S(1)}, s32[32,32768]{1,0:T(8,128)S(1)}) custom-call(f32[32,32768]{1,0:T(8,128)S(1)} %get-tuple-element.31.weight.refs_1_, s32[32,32768]{1,0:T(8,128)S(1)} %get-tuple-element.32.events.refs_2_, s32[256,128]{1,0:T(8,128)S(1)} %bitcast.6, s32[32,32768]{1,0:T(8,128)} %leaf_in.1), custom_call_target="tpu_custom_call" | custom-call | bytes 17500000 | tf_op jit(solution)/shard_map/scan/pallas_call | solution.py:38
  19.4 1.1 %collective-permute-done.5.refs_4_ = f32[32,128]{1,0:T(8,128)S(1)} collective-permute-done((f32[32,128]{1,0:T(8,128)S(1)}, f32[32,128]{1,0:T(8,128)S(1)}, u32[]{:S(2)}, u32[]{:S(2)}) %collective-permute-start.5) | collective-permute-done | bytes 16416 | tf_op jit(solution)/shard_map/ppermute | solution.py:512
  20.5 2.3 %inverse.1 = (f32[32,32768]{1,0:T(8,128)S(1)}, f32[32,32768]{1,0:T(8,128)S(1)}, f32[64,128]{1,0:T(8,128)S(1)}, f32[4,32,128]{2,1,0:T(8,128)S(1)}) custom-call(s32[2]{0:T(128)S(1)} %pad_add_fusion.meta.refs_0_, f32[32,128]{1,0:T(8,128)S(1)} %collective-permute-done.2.right.refs_1_, ...), custom_call_target="tpu_custom_call", output_to_operand_aliasing={{0}: (5, {})} | custom-call | bytes 5250000 | tf_op jit(solution)/shard_map/inverse/pallas_call | solution.py:38
  22.8 0.0 collective-permute-start.6
  22.9 1.2 %collective-permute-done.6.right.refs_1_ = f32[64,128]{1,0:T(8,128)S(1)} collective-permute-done((f32[64,128]{1,0:T(8,128)S(1)}, f32[64,128]{1,0:T(8,128)S(1)}, u32[]{:S(2)}, u32[]{:S(2)}) %collective-permute-start.6) | collective-permute-done | bytes 32800 | tf_op jit(solution)/shard_map/ppermute | solution.py:512
  24.1 3.1 %collective-permute-start.8 = (f32[64,128]{1,0:T(8,128)S(1)}, f32[64,128]{1,0:T(8,128)S(1)}, u32[]{:S(2)}, u32[]{:S(2)}) collective-permute-start(f32[64,128]{1,0:T(8,128)S(1)} %pair.4), channel_id=1, source_target_pairs={{0,4},{1,5},{2,6},{3,7},{4,0},{5,1},{6,2},{7,3},{8,12},{9,13},{10,... | collective-permute-start | bytes 98312 | tf_op jit(solution)/shard_map/ppermute | solution.py:512
  27.2 1.3 %collective-permute-start.9 = (f32[64,128]{1,0:T(8,128)S(1)}, f32[64,128]{1,0:T(8,128)S(1)}, u32[]{:S(2)}, u32[]{:S(2)}) collective-permute-start(f32[64,128]{1,0:T(8,128)S(1)} %pair.4), channel_id=1, source_target_pairs={{0,6},{1,7},{2,4},{3,5},{4,2},{5,3},{6,0},{7,1},{8,14},{9,15},{10,... | collective-permute-start | bytes 98312 | tf_op jit(solution)/shard_map/ppermute | solution.py:512
  28.5 2.9 %accum.1 = (f32[32,32768]{1,0:T(8,128)S(1)}, f32[32,32768]{1,0:T(8,128)S(1)}, f32[4,64,128]{2,1,0:T(8,128)S(1)}) custom-call(f32[32,32768]{1,0:T(8,128)S(1)} %get-tuple-element.41.inv_one, f32[32,32768]{1,0:T(8,128)S(1)} %get-tuple-element.42.inv_two), custom_call_target="tpu_custom_call", output_to_operand_aliasing={{0}: (0, {}), {1}: (1, {})} | custom-call | bytes 10500000 | tf_op jit(solution)/shard_map/accum/pallas_call | solution.py:38
  31.4 1.5 %collective-permute-done.9.refs_4_ = f32[64,128]{1,0:T(8,128)S(1)} collective-permute-done((f32[64,128]{1,0:T(8,128)S(1)}, f32[64,128]{1,0:T(8,128)S(1)}, u32[]{:S(2)}, u32[]{:S(2)}) %collective-permute-start.9) | collective-permute-done | bytes 32800 | tf_op jit(solution)/shard_map/ppermute | solution.py:512
  32.9 0.6 bases.1
  33.5 0.6 collective-permute-start.10
  34.1 0.5 collective-permute-start.11
  34.6 2.9 %leaf_first.1 = (bf16[2,32,8192]{2,1,0:T(8,128)(2,1)S(1)}, f32[2,256,256]{2,1,0:T(8,128)S(1)}) custom-call(s32[2]{0:T(128)S(1)} %pad_add_fusion.meta.refs_0_, s32[32,32768]{1,0:T(8,128)S(1)} %get-tuple-element.46.refs_0_.leaf, f32[32,32768]{1,0:T(8,128)S(1)} %get-tuple-element.31.weight.refs_1_, s32[32,32768]{1,0:T(8,128)S(1)} %get-tuple-element.32.events.refs_2_, ...), custom_call_target="tpu_custom_call" | custom-call | bytes 10500000 | tf_op jit(solution)/shard_map/leaf_first/pallas_call | solution.py:38
  37.5 0.1 collective-permute-done.10.refs_1_.refs_5_.refs_0_
  37.6 0.5 collective-permute-done.11.refs_2_.refs_6_.refs_1_
  38.2 1.9 %collective-permute-start.12 = (bf16[2,32,8192]{2,1,0:T(8,128)(2,1)S(1)}, bf16[2,32,8192]{2,1,0:T(8,128)(2,1)S(1)}, u32[]{:S(2)}, u32[]{:S(2)}) collective-permute-start(bf16[2,32,8192]{2,1,0:T(8,128)(2,1)S(1)} %release.1.refs_7_), channel_id=1, source_target_pairs={{0,24},{8,16},{16,8},{24,0},{1,25},{9,17},{17,9},{25,1},{2,26},{10... | collective-permute-start | bytes 3145736 | tf_op jit(solution)/shard_map/ppermute | solution.py:512
  40.1 8.4 %leaf_rest.1 = (bf16[2,32,8192]{2,1,0:T(8,128)(2,1)S(1)}, f32[32,128]{1,0:T(8,128)S(1)}, f32[2,256,256]{2,1,0:T(8,128)S(1)}) custom-call(s32[2]{0:T(128)S(1)} %pad_add_fusion.meta.refs_0_, s32[32,32768]{1,0:T(8,128)S(1)} %get-tuple-element.46.refs_0_.leaf, f32[32,32768]{1,0:T(8,128)S(1)} %get-tuple-element.31.weight.refs_1_, ...), custom_call_target="tpu_custom_call", output_to_operand_aliasing={{2}: (7, {})} | custom-call | bytes 31500000 | tf_op jit(solution)/shard_map/leaf_rest/pallas_call | solution.py:38
  48.5 0.1 collective-permute-start.13
  48.6 1.2 %collective-permute-done.13.right = f32[32,128]{1,0:T(8,128)S(1)} collective-permute-done((f32[32,128]{1,0:T(8,128)S(1)}, f32[32,128]{1,0:T(8,128)S(1)}, u32[]{:S(2)}, u32[]{:S(2)}) %collective-permute-start.13) | collective-permute-done | bytes 16416 | tf_op jit(solution)/shard_map/ppermute | solution.py:512
  49.8 1.8 %collective-permute-start.15 = (f32[32,128]{1,0:T(8,128)S(1)}, f32[32,128]{1,0:T(8,128)S(1)}, u32[]{:S(2)}, u32[]{:S(2)}) collective-permute-start(f32[32,128]{1,0:T(8,128)S(1)} %pair.5.refs_2_), channel_id=1, source_target_pairs={{0,4},{1,5},{2,6},{3,7},{4,0},{5,1},{6,2},{7,3},{8,12},{9,13},{10,... | collective-permute-start | bytes 49160 | tf_op jit(solution)/shard_map/ppermute | solution.py:512
  51.6 2.6 %collective-permute-start.16 = (f32[32,128]{1,0:T(8,128)S(1)}, f32[32,128]{1,0:T(8,128)S(1)}, u32[]{:S(2)}, u32[]{:S(2)}) collective-permute-start(f32[32,128]{1,0:T(8,128)S(1)} %pair.5.refs_2_), channel_id=1, source_target_pairs={{0,6},{1,7},{2,4},{3,5},{4,2},{5,3},{6,0},{7,1},{8,14},{9,15},{10,... | collective-permute-start | bytes 49160 | tf_op jit(solution)/shard_map/ppermute | solution.py:512
  54.1 6.6 %finish.1 = (bf16[2,128,8192]{2,1,0:T(8,128)(2,1)}, f32[32,32768]{1,0:T(8,128)S(1)}) custom-call(s32[2]{0:T(128)S(1)} %pad_add_fusion.meta.refs_0_, s32[256,128]{1,0:T(8,128)S(1)} %bitcast.7, s32[256,128]{1,0:T(8,128)S(1)} %get-tuple-element.33.refs_2_, s16[2,32,8192]{2,1,0:T(8,128)(2,1)S(1)} %collective-permute-done.refs_3_, ...), custom_call_target="tpu_custom_call" | custom-call | bytes 28000000 | tf_op jit(solution)/shard_map/finish/pallas_call | solution.py:38
  60.8 0.6 collective-permute-done.12.refs_0_
  61.5 5.3 %update.1 = (f32[32,32768]{1,0:T(8,128)}, f32[32,64]{1,0:T(8,128)}, bf16[2,128,8192]{2,1,0:T(8,128)(2,1)}) custom-call(s32[2]{0:T(128)S(1)} %pad_add_fusion.meta.refs_0_, f32[32,32768]{1,0:T(8,128)S(1)} %get-tuple-element.53.pred, s32[32,32768]{1,0:T(8,128)S(1)} %get-tuple-element.46.refs_0_.leaf, ...), custom_call_target="tpu_custom_call", output_to_operand_aliasing={{2}: (4, {})} | custom-call | bytes 14000000 | tf_op jit(solution)/shard_map/update/pallas_call | solution.py:38
  (18 shorter events, 0.0 us)
Async XLA Ops:
  0.7 14.5 %copy-start = (s32[32768]{0:T(1024)S(1)}, s32[32768]{0:T(1024)}, u32[]{:S(2)}) copy-start(s32[32768]{0:T(1024)} %param.7) | copy-start | bytes 393220
  5.1 33.1 %collective-permute-start = (s16[2,32,8192]{2,1,0:T(8,128)(2,1)S(1)}, s16[2,32,8192]{2,1,0:T(8,128)(2,1)S(1)}, u32[]{:S(2)}, u32[]{:S(2)}) collective-permute-start(s16[2,32,8192]{2,1,0:T(8,128)(2,1)S(1)} %get-tuple-element.34), channel_id=1, source_target_pairs={{0,8},{8,0},{16,24},{24,16},{1,9},{9,1},{17,25},{25,17},{2,10},{10... | collective-permute-start | bytes 3145736 | tf_op jit(solution)/shard_map/ppermute | solution.py:512
  8.1 30.1 %collective-permute-start.1 = (s16[2,32,8192]{2,1,0:T(8,128)(2,1)S(1)}, s16[2,32,8192]{2,1,0:T(8,128)(2,1)S(1)}, u32[]{:S(2)}, u32[]{:S(2)}) collective-permute-start(s16[2,32,8192]{2,1,0:T(8,128)(2,1)S(1)} %get-tuple-element.35), channel_id=1, source_target_pairs={{0,16},{8,24},{16,0},{24,8},{1,17},{9,25},{17,1},{25,9},{2,18},{10... | collective-permute-start | bytes 3145736 | tf_op jit(solution)/shard_map/ppermute | solution.py:512
  9.6 1.2 %collective-permute-start.2 = (f32[32,128]{1,0:T(8,128)S(1)}, f32[32,128]{1,0:T(8,128)S(1)}, u32[]{:S(2)}, u32[]{:S(2)}) collective-permute-start(f32[32,128]{1,0:T(8,128)S(1)} %get-tuple-element.36.left), channel_id=1, source_target_pairs={{0,1},{1,0},{2,3},{3,2},{4,5},{5,4},{6,7},{7,6},{8,9},{9,8},{10,11... | collective-permute-start | bytes 49160 | tf_op jit(solution)/shard_map/ppermute | solution.py:512
  10.8 8.6 %collective-permute-start.3 = (f32[32,128]{1,0:T(8,128)S(1)}, f32[32,128]{1,0:T(8,128)S(1)}, u32[]{:S(2)}, u32[]{:S(2)}) collective-permute-start(f32[32,128]{1,0:T(8,128)S(1)} %pair.3), channel_id=1, source_target_pairs={{0,2},{1,3},{2,0},{3,1},{4,6},{5,7},{6,4},{7,5},{8,10},{9,11},{10,... | collective-permute-start | bytes 49160 | tf_op jit(solution)/shard_map/ppermute | solution.py:512
  12.4 7.1 %collective-permute-start.4 = (f32[32,128]{1,0:T(8,128)S(1)}, f32[32,128]{1,0:T(8,128)S(1)}, u32[]{:S(2)}, u32[]{:S(2)}) collective-permute-start(f32[32,128]{1,0:T(8,128)S(1)} %pair.3), channel_id=1, source_target_pairs={{0,4},{1,5},{2,6},{3,7},{4,0},{5,1},{6,2},{7,3},{8,12},{9,13},{10,... | collective-permute-start | bytes 49160 | tf_op jit(solution)/shard_map/ppermute | solution.py:512
  15.0 5.5 %collective-permute-start.5 = (f32[32,128]{1,0:T(8,128)S(1)}, f32[32,128]{1,0:T(8,128)S(1)}, u32[]{:S(2)}, u32[]{:S(2)}) collective-permute-start(f32[32,128]{1,0:T(8,128)S(1)} %pair.3), channel_id=1, source_target_pairs={{0,6},{1,7},{2,4},{3,5},{4,2},{5,3},{6,0},{7,1},{8,14},{9,15},{10,... | collective-permute-start | bytes 49160 | tf_op jit(solution)/shard_map/ppermute | solution.py:512
  22.8 1.2 %collective-permute-start.6 = (f32[64,128]{1,0:T(8,128)S(1)}, f32[64,128]{1,0:T(8,128)S(1)}, u32[]{:S(2)}, u32[]{:S(2)}) collective-permute-start(f32[64,128]{1,0:T(8,128)S(1)} %get-tuple-element.39.left), channel_id=1, source_target_pairs={{0,1},{1,0},{2,3},{3,2},{4,5},{5,4},{6,7},{7,6},{8,9},{9,8},{10,11... | collective-permute-start | bytes 98312 | tf_op jit(solution)/shard_map/ppermute | solution.py:512
  24.1 7.3 %collective-permute-start.7 = (f32[64,128]{1,0:T(8,128)S(1)}, f32[64,128]{1,0:T(8,128)S(1)}, u32[]{:S(2)}, u32[]{:S(2)}) collective-permute-start(f32[64,128]{1,0:T(8,128)S(1)} %pair.4), channel_id=1, source_target_pairs={{0,2},{1,3},{2,0},{3,1},{4,6},{5,7},{6,4},{7,5},{8,10},{9,11},{10,... | collective-permute-start | bytes 98312 | tf_op jit(solution)/shard_map/ppermute | solution.py:512
  24.1 7.3 %collective-permute-start.8 = (f32[64,128]{1,0:T(8,128)S(1)}, f32[64,128]{1,0:T(8,128)S(1)}, u32[]{:S(2)}, u32[]{:S(2)}) collective-permute-start(f32[64,128]{1,0:T(8,128)S(1)} %pair.4), channel_id=1, source_target_pairs={{0,4},{1,5},{2,6},{3,7},{4,0},{5,1},{6,2},{7,3},{8,12},{9,13},{10,... | collective-permute-start | bytes 98312 | tf_op jit(solution)/shard_map/ppermute | solution.py:512
  27.2 5.7 %collective-permute-start.9 = (f32[64,128]{1,0:T(8,128)S(1)}, f32[64,128]{1,0:T(8,128)S(1)}, u32[]{:S(2)}, u32[]{:S(2)}) collective-permute-start(f32[64,128]{1,0:T(8,128)S(1)} %pair.4), channel_id=1, source_target_pairs={{0,6},{1,7},{2,4},{3,5},{4,2},{5,3},{6,0},{7,1},{8,14},{9,15},{10,... | collective-permute-start | bytes 98312 | tf_op jit(solution)/shard_map/ppermute | solution.py:512
  33.5 4.2 %collective-permute-start.10 = (f32[96,128]{1,0:T(8,128)S(1)}, f32[96,128]{1,0:T(8,128)S(1)}, u32[]{:S(2)}, u32[]{:S(2)}) collective-permute-start(f32[96,128]{1,0:T(8,128)S(1)} %get-tuple-element.44), channel_id=1, source_target_pairs={{0,8},{8,0},{16,24},{24,16},{1,9},{9,1},{17,25},{25,17},{2,10},{10... | collective-permute-start | bytes 147464 | tf_op jit(solution)/shard_map/ppermute | solution.py:512
  34.1 4.1 %collective-permute-start.11 = (f32[96,128]{1,0:T(8,128)S(1)}, f32[96,128]{1,0:T(8,128)S(1)}, u32[]{:S(2)}, u32[]{:S(2)}) collective-permute-start(f32[96,128]{1,0:T(8,128)S(1)} %get-tuple-element.45), channel_id=1, source_target_pairs={{0,16},{8,24},{16,0},{24,8},{1,17},{9,25},{17,1},{25,9},{2,18},{10... | collective-permute-start | bytes 147464 | tf_op jit(solution)/shard_map/ppermute | solution.py:512
  38.2 23.3 %collective-permute-start.12 = (bf16[2,32,8192]{2,1,0:T(8,128)(2,1)S(1)}, bf16[2,32,8192]{2,1,0:T(8,128)(2,1)S(1)}, u32[]{:S(2)}, u32[]{:S(2)}) collective-permute-start(bf16[2,32,8192]{2,1,0:T(8,128)(2,1)S(1)} %release.1.refs_7_), channel_id=1, source_target_pairs={{0,24},{8,16},{16,8},{24,0},{1,25},{9,17},{17,9},{25,1},{2,26},{10... | collective-permute-start | bytes 3145736 | tf_op jit(solution)/shard_map/ppermute | solution.py:512
  48.5 1.2 %collective-permute-start.13 = (f32[32,128]{1,0:T(8,128)S(1)}, f32[32,128]{1,0:T(8,128)S(1)}, u32[]{:S(2)}, u32[]{:S(2)}) collective-permute-start(f32[32,128]{1,0:T(8,128)S(1)} %get-tuple-element.55.left), channel_id=1, source_target_pairs={{0,1},{1,0},{2,3},{3,2},{4,5},{5,4},{6,7},{7,6},{8,9},{9,8},{10,11... | collective-permute-start | bytes 49160 | tf_op jit(solution)/shard_map/ppermute | solution.py:512
  49.8 11.0 %collective-permute-start.14 = (f32[32,128]{1,0:T(8,128)S(1)}, f32[32,128]{1,0:T(8,128)S(1)}, u32[]{:S(2)}, u32[]{:S(2)}) collective-permute-start(f32[32,128]{1,0:T(8,128)S(1)} %pair.5.refs_2_), channel_id=1, source_target_pairs={{0,2},{1,3},{2,0},{3,1},{4,6},{5,7},{6,4},{7,5},{8,10},{9,11},{10,... | collective-permute-start | bytes 49160 | tf_op jit(solution)/shard_map/ppermute | solution.py:512
  49.8 11.0 %collective-permute-start.15 = (f32[32,128]{1,0:T(8,128)S(1)}, f32[32,128]{1,0:T(8,128)S(1)}, u32[]{:S(2)}, u32[]{:S(2)}) collective-permute-start(f32[32,128]{1,0:T(8,128)S(1)} %pair.5.refs_2_), channel_id=1, source_target_pairs={{0,4},{1,5},{2,6},{3,7},{4,0},{5,1},{6,2},{7,3},{8,12},{9,13},{10,... | collective-permute-start | bytes 49160 | tf_op jit(solution)/shard_map/ppermute | solution.py:512
  51.6 9.2 %collective-permute-start.16 = (f32[32,128]{1,0:T(8,128)S(1)}, f32[32,128]{1,0:T(8,128)S(1)}, u32[]{:S(2)}, u32[]{:S(2)}) collective-permute-start(f32[32,128]{1,0:T(8,128)S(1)} %pair.5.refs_2_), channel_id=1, source_target_pairs={{0,6},{1,7},{2,4},{3,5},{4,2},{5,3},{6,0},{7,1},{8,14},{9,15},{10,... | collective-permute-start | bytes 49160 | tf_op jit(solution)/shard_map/ppermute | solution.py:512

commit v4 on v3

--- a/solution.py
+++ b/solution.py
@@ -17,6 +17,7 @@
 CODE = 32766.0 / 6.0
 MIDDLE = 32768
 MIB = 1024 * 1024
+PIECE = 2048
 
 
 def resident(shape, dtype):
@@ -122,10 +123,18 @@
         copy.wait()
 
 
-def pair_dot(x, matrix):
+def scan_matrix(backward):
+    above = lax.broadcasted_iota(jnp.int32, (WIDE, WIDE), 0) % LANES
+    along = lax.broadcasted_iota(jnp.int32, (WIDE, WIDE), 1)
+    inside = above >= along if backward else above <= along
+    return (inside | (along >= LANES)).astype(BF16)
+
+
+def block_sums(x, matrix):
     high = x.astype(BF16)
     low = (x - high.astype(F32)).astype(BF16)
-    return jnp.dot(high, matrix, preferred_element_type=F32) + jnp.dot(low, matrix, preferred_element_type=F32)
+    both = jnp.dot(jnp.concatenate([high, low], axis=1), matrix, preferred_element_type=F32)
+    return both[:, :LANES], both[:, LANES:]
 
 
 def take(x, index):
@@ -148,8 +157,8 @@
     return (above >= along if backward else above <= along).astype(BF16)
 
 
-def stacked(ref, base, count):
-    return jnp.concatenate([ref[:, span(base + k * WIDE, WIDE)] for k in range(count)], axis=0)
+def stacked(ref, base, count, width=WIDE):
+    return jnp.concatenate([ref[:, span(base + k * width, width)] for k in range(count)], axis=0)
 
 
 FIELDS = 4
@@ -179,7 +188,7 @@
     fetch.start()
     count = min(16, length // WIDE)
     last[...] = last_in_group(tie[...])
-    upper[...] = triangle(True)
+    upper[...] = scan_matrix(True)
     lower[...] = triangle(False)
     steps = length // (WIDE * count)
 
@@ -187,21 +196,22 @@
         base = (steps - 1 - turn) * (WIDE * count)
         observed = stacked(events, base, count)
         counts = jnp.dot(observed.astype(F32).astype(BF16), lower[...], preferred_element_type=F32)
-        summed = pair_dot(stacked(weight, base, count), upper[...])
+        summed, totals = block_sums(stacked(weight, base, 2 * count, LANES), upper[...])
         for k in range(count - 1, -1, -1):
             mine = slice(k * rows, (k + 1) * rows)
-            for half in (0, 1):
+            for half in (1, 0):
                 lanes = slice(half * LANES, (half + 1) * LANES)
                 at = span(base + k * WIDE + half * LANES, LANES)
                 block = pl.ds((base + k * WIDE) // LANES + half, 1)
-                suffix[:, at] = summed[mine, lanes] + carry
+                here = slice((2 * k + half) * rows, (2 * k + half + 1) * rows)
+                suffix[:, at] = summed[here] + carry
+                carry = carry + totals[here]
                 grouped[:, at] = group_events(
                     observed[mine, lanes],
                     counts[mine, lanes],
                     jnp.broadcast_to(tie[block, :], (rows // FIELDS, LANES)),
                     jnp.broadcast_to(last[block, :], (rows // FIELDS, LANES)),
                 )
-            carry = carry + jnp.broadcast_to(summed[mine, 0:1], (rows, LANES))
         return carry
 
     lax.fori_loop(0, steps, one, jnp.zeros((rows, LANES), F32), unroll=2)
@@ -254,7 +264,7 @@
     rows, length = inv_one.shape
     share = length // parts
     count = min(16, share // WIDE)
-    lower[...] = triangle(False)
+    lower[...] = scan_matrix(False)
     empty = jnp.zeros((rows, LANES), F32)
     carry = (empty, empty)
     for part in range(parts):
@@ -265,11 +275,11 @@
             base = part * share + turn * (WIDE * count)
             made = []
             for ref, out, so_far in ((inv_one, one_out, carry[0]), (inv_two, two_out, carry[1])):
-                summed = pair_dot(stacked(ref, base, count), lower[...])
-                for k in range(count):
-                    piece = summed[k * rows : (k + 1) * rows]
-                    out[:, span(base + k * WIDE, WIDE)] = piece + widen(so_far, WIDE)
-                    so_far = so_far + jnp.broadcast_to(piece[:, WIDE - 1 :], (rows, LANES))
+                summed, totals = block_sums(stacked(ref, base, 2 * count, LANES), lower[...])
+                for k in range(2 * count):
+                    mine = slice(k * rows, (k + 1) * rows)
+                    out[:, span(base + k * LANES, LANES)] = summed[mine] + so_far
+                    so_far = so_far + totals[mine]
                 made.append(so_far)
             return tuple(made)
 
@@ -307,60 +317,56 @@
     return copies
 
 
+def partner_scan(turn, slot, message, so_far, first_block, tie, last, upper, lower, kept, inv_one, inv_two):
+    _, rows, share = kept.shape
+    steps = share // PIECE
+    count = PIECE // WIDE
+    at_base = (steps - 1 - turn) * PIECE
+    coded = jnp.concatenate([message[0, :, span(at_base + k * WIDE, WIDE)] for k in range(count)], axis=0)
+    values = jnp.exp(coded.astype(jnp.int32).astype(F32) * (1.0 / CODE))
+    seen = jnp.concatenate([message[1, :, span(at_base + k * WIDE, WIDE)] for k in range(count)], axis=0)
+    observed = seen.astype(jnp.int32)
+    counts = jnp.dot(observed.astype(F32).astype(BF16), lower[...], preferred_element_type=F32)
+    blocks = [values[k * rows : (k + 1) * rows, half * LANES : (half + 1) * LANES] for k in range(count) for half in (0, 1)]
+    summed, totals = block_sums(jnp.concatenate(blocks, axis=0), upper[...])
+    for k in range(count - 1, -1, -1):
+        mine = slice(k * rows, (k + 1) * rows)
+        kept[slot, :, span(at_base + k * WIDE, WIDE)] = values[mine]
+        for half in (1, 0):
+            here = slice((2 * k + half) * rows, (2 * k + half + 1) * rows)
+            lanes = slice(half * LANES, (half + 1) * LANES)
+            at = span(at_base + k * WIDE + half * LANES, LANES)
+            block = pl.ds(first_block + (at_base + k * WIDE) // LANES + half, 1)
+            grouped = group_events(
+                observed[mine, lanes],
+                counts[mine, lanes],
+                jnp.broadcast_to(tie[block, :], (rows // FIELDS, LANES)),
+                jnp.broadcast_to(last[block, :], (rows // FIELDS, LANES)),
+            )
+            inverse = 1.0 / (summed[here] + so_far)
+            so_far = so_far + totals[here]
+            first = unpack(grouped) * inverse
+            inv_one[slot, :, at] = first
+            inv_two[slot, :, at] = first * inverse
+    return so_far
+
+
 def finish_body(partners, *refs):
-    meta, tie, last = refs[:3]
-    refs = refs[3:]
+    meta, refs = refs[0], refs[1:]
     messages, base = refs[: len(partners)], refs[len(partners) : 2 * len(partners)]
-    own, pred_in, out, pred, scratch, kept, inv_one, inv_two, upper, lower, sems, own_sems, fetch_sem = refs[2 * len(partners) :]
+    own, kept, inv_one, inv_two, pred_in, out, pred, scratch, lower, sems, own_sems, fetch_sem = refs[2 * len(partners) :]
     fetch = pltpu.make_async_copy(pred_in, pred, fetch_sem)
     fetch.start()
     own_copies = place_pieces(meta, [0], [own], out, own_sems)
     for copy in own_copies:
         copy.start()
     _, rows, share = kept.shape
-    count = share // (WIDE * sems.shape[2])
-    steps = share // (WIDE * count)
-    turn_width = WIDE * count
-    first_block = share_of(meta, 0, share) // LANES
-    upper[...] = triangle(True)
-    lower[...] = triangle(False)
-
-    def one(turn, carry):
-        at_base = (steps - 1 - turn) * turn_width
-        made = []
-        for slot in range(len(partners)):
-            coded = jnp.concatenate([messages[slot][0, :, span(at_base + k * WIDE, WIDE)] for k in range(count)], axis=0)
-            values = jnp.exp(coded.astype(jnp.int32).astype(F32) * (1.0 / CODE))
-            seen = jnp.concatenate([messages[slot][1, :, span(at_base + k * WIDE, WIDE)] for k in range(count)], axis=0)
-            observed = seen.astype(jnp.int32)
-            counts = jnp.dot(observed.astype(F32).astype(BF16), lower[...], preferred_element_type=F32)
-            summed = pair_dot(values, upper[...])
-            so_far = carry[slot]
-            for k in range(count - 1, -1, -1):
-                mine = slice(k * rows, (k + 1) * rows)
-                kept[slot, :, span(at_base + k * WIDE, WIDE)] = values[mine]
-                for half in (0, 1):
-                    lanes = slice(half * LANES, (half + 1) * LANES)
-                    at = span(at_base + k * WIDE + half * LANES, LANES)
-                    block = pl.ds(first_block + (at_base + k * WIDE) // LANES + half, 1)
-                    grouped = group_events(
-                        observed[mine, lanes],
-                        counts[mine, lanes],
-                        jnp.broadcast_to(tie[block, :], (rows // FIELDS, LANES)),
-                        jnp.broadcast_to(last[block, :], (rows // FIELDS, LANES)),
-                    )
-                    inverse = 1.0 / (summed[mine, lanes] + so_far)
-                    first = unpack(grouped) * inverse
-                    inv_one[slot, :, at] = first
-                    inv_two[slot, :, at] = first * inverse
-                so_far = so_far + jnp.broadcast_to(summed[mine, 0:1], (rows, LANES))
-            made.append(so_far)
-        return tuple(made)
-
-    lax.fori_loop(0, steps, one, tuple(b[:rows, :] for b in base))
+    steps = share // PIECE
+    count = PIECE // WIDE
+    lower[...] = scan_matrix(False)
 
     def copies(turn):
-        lanes = span(turn * turn_width, turn_width)
+        lanes = span(turn * PIECE, PIECE)
         made = []
         for slot, d in enumerate(partners):
             where = pl.ds(pl.multiple_of(share_of(meta, d, rows), rows), rows)
@@ -370,32 +376,32 @@
             ]
         return made
 
-    def two(turn, carry):
-        at_base = turn * turn_width
+    def one(turn, carry):
+        at_base = turn * PIECE
         made = []
         for slot in range(len(partners)):
-            sum_one = pair_dot(stacked(inv_one.at[slot], at_base, count), lower[...])
-            sum_two = pair_dot(stacked(inv_two.at[slot], at_base, count), lower[...])
+            sum_one, total_one = block_sums(stacked(inv_one.at[slot], at_base, 2 * count, LANES), lower[...])
+            sum_two, total_two = block_sums(stacked(inv_two.at[slot], at_base, 2 * count, LANES), lower[...])
             so_one, so_two = carry[slot]
-            for k in range(count):
+            for k in range(2 * count):
                 mine = slice(k * rows, (k + 1) * rows)
-                at = span(at_base + k * WIDE, WIDE)
+                at = span(at_base + k * LANES, LANES)
                 grad, hess = derivatives(
                     kept[slot, :, at],
                     messages[slot][1, :, at].astype(jnp.int32).astype(F32),
-                    sum_one[mine] + widen(so_one, WIDE),
-                    sum_two[mine] + widen(so_two, WIDE),
+                    sum_one[mine] + so_one,
+                    sum_two[mine] + so_two,
                 )
                 scratch[slot, 0, :, at] = grad.astype(BF16)
                 scratch[slot, 1, :, at] = hess.astype(BF16)
-                so_one = so_one + jnp.broadcast_to(sum_one[mine, WIDE - 1 :], (rows, LANES))
-                so_two = so_two + jnp.broadcast_to(sum_two[mine, WIDE - 1 :], (rows, LANES))
+                so_one = so_one + total_one[mine]
+                so_two = so_two + total_two[mine]
             made.append((so_one, so_two))
         for copy in copies(turn):
             copy.start()
         return tuple(made)
 
-    lax.fori_loop(0, steps, two, tuple((b[rows : 2 * rows, :], b[2 * rows :, :]) for b in base))
+    lax.fori_loop(0, steps, one, tuple((b[rows : 2 * rows, :], b[2 * rows :, :]) for b in base))
     for turn in range(steps):
         for copy in copies(turn):
             copy.wait()
@@ -437,58 +443,93 @@
         acc[group] += lax.dot_general(left, right, (((1,), (1,)), ((), ())), preferred_element_type=F32)
 
 
-def leaf_shares(shares, size, meta, ins, outs, acc):
-    step = min(size, 2048)
-    for k, d in enumerate(shares):
+def leaf_first_body(shares, size, meta, *refs):
+    ins, outs, acc = refs[:6], refs[6:-1], refs[-1]
+    acc[...] = jnp.zeros_like(acc)
+    for d, out in zip(shares, outs):
         start = share_of(meta, d, size)
 
         def one(turn, carry):
-            at = turn * step
-            leaf_step(span(start + at, step), *ins, acc, outs[k] if k < len(outs) else None, span(at, step))
+            leaf_step(span(start + turn * PIECE, PIECE), *ins, acc, out, span(turn * PIECE, PIECE))
             return carry
 
-        lax.fori_loop(0, size // step, one, 0, unroll=4)
-
-
-def leaf_first_body(shares, size, meta, *refs):
-    acc = refs[-1]
-    acc[...] = jnp.zeros_like(acc)
-    leaf_shares(shares, size, meta, refs[:6], refs[6:-1], acc)
-
-
-def leaf_rest_body(shares, size, meta, *refs):
-    own, sums, acc = refs[-3:]
-    leaf_shares(shares, size, meta, refs[:6], [own], acc)
+        lax.fori_loop(0, size // PIECE, one, 0, unroll=4)
+
+
+def leaf_rest_body(links, size, meta, *refs):
+    ins, tie, last = refs[:6], refs[6], refs[7]
+    messages, base = refs[8 : 8 + len(links)], refs[8 + len(links) : 8 + 2 * len(links)]
+    own, sums, kept, inv_one, inv_two, acc, upper, lower = refs[-8:]
+    upper[...] = scan_matrix(True)
+    lower[...] = triangle(False)
+    rows = kept.shape[1]
+    first_block = share_of(meta, 0, size) // LANES
+
+    def one(turn, carry):
+        at = turn * PIECE
+        made = []
+        leaf_step(span(share_of(meta, 0, size) + at, PIECE), *ins, acc, own, span(at, PIECE))
+        for slot, d in enumerate(links):
+            made.append(
+                partner_scan(
+                    turn, slot, messages[slot], carry[slot], first_block, tie, last, upper, lower, kept, inv_one, inv_two
+                )
+            )
+            leaf_step(span(share_of(meta, d, size) + at, PIECE), *ins, acc, None, None)
+        return tuple(made)
+
+    lax.fori_loop(0, size // PIECE, one, tuple(b[:rows, :] for b in base))
     width = LOW * GROUP
     side = HIGH * GROUP
     same = lax.broadcasted_iota(jnp.int32, (side, width), 0) % GROUP == lax.broadcasted_iota(jnp.int32, (side, width), 1) % GROUP
+    held = []
+    for group in range(rows // GROUP):
+        for value in (0, 1):
+            both = acc[group, 2 * value * side : (2 * value + 1) * side] + acc[group, (2 * value + 1) * side : (2 * value + 2) * side]
+            held.append(jnp.where(same, both, 0.0))
+    held = jnp.concatenate(held, axis=0)
     source = lax.broadcasted_iota(jnp.int32, (width, LANES), 0) // GROUP
-    target = lax.broadcasted_iota(jnp.int32, (width, LANES), 1)
-    for group in range(acc.shape[0]):
+    place = (source == lax.broadcasted_iota(jnp.int32, (width, LANES), 1)).astype(BF16)
+    by_low = jnp.zeros((held.shape[0], LANES), F32)
+    for _ in range(3):
+        part = held.astype(BF16)
+        held = held - part.astype(F32)
+        by_low = by_low + jnp.dot(part, place, preferred_element_type=F32)
+    for group in range(rows // GROUP):
         out = jnp.zeros((GROUP, LANES), F32)
         for value in (0, 1):
-            both = acc[group, 2 * value * side : (2 * value + 1) * side] + acc[group, (2 * value + 1) * side : (2 * value + 2) * side]
-            both = jnp.where(same, both, 0.0)
             for h in range(HIGH):
-                place = (target == source + (h * LOW + value * LEAVES)).astype(F32)
-                out = out + jnp.dot(
-                    both[h * GROUP : (h + 1) * GROUP], place, precision=lax.Precision.HIGHEST, preferred_element_type=F32
-                )
+                at = ((group * 2 + value) * HIGH + h) * GROUP
+                out = out + pltpu.roll(by_low[at : at + GROUP], h * LOW + value * LEAVES, 1)
         sums[group * GROUP : (group + 1) * GROUP, :] = out
 
 
-def update_body(turns, partners, meta, pred, leaf, *refs):
-    arrived, refs = refs[: len(partners)], refs[len(partners) + 1 :]
-    sums, (new_pred, leaf_weights, out, scratch, sems, piece_sems) = refs[:-6], refs[-6:]
-    rows, length = leaf.shape
-    copies = place_pieces(meta, partners, arrived, out, piece_sems)
+def place_body(partners, cuts, meta, *refs):
+    out, sems = refs[-2:]
+    copies = []
+    for k, (d, piece) in enumerate(zip(partners, refs)):
+        _, rows, size = piece.shape
+        where = pl.ds(pl.multiple_of(share_of(meta, d, rows), rows), rows)
+        for v in (0, 1):
+            for cut in range(cuts):
+                lanes = pl.ds(cut * (size // cuts), size // cuts)
+                copies.append(pltpu.make_async_copy(piece.at[v, :, lanes], out.at[v, where, lanes], sems.at[k, v, cut]))
     for copy in copies:
         copy.start()
+    for copy in copies:
+        copy.wait()
+
+
+def update_body(turns, pred, leaf, *refs):
+    sums, (new_pred, leaf_weights, scratch, weights, sems) = refs[:-5], refs[-5:]
+    rows, length = leaf.shape
     both = [ref[...] for ref in sums]
     while len(both) > 1:
         both = [a + b for a, b in zip(both[::2], both[1::2])]
     table = -both[0] / (pltpu.roll(both[0], LANES - LEAVES, 1) + 1.0)
-    leaf_weights[...] = table[:, :LEAVES]
+    weights[...] = table[:, :LEAVES]
+    copies = [pltpu.make_async_copy(weights, leaf_weights, sems.at[turns])]
+    copies[0].start()
     width = length // turns
     step = min(width, 512)
     for turn in range(turns):
@@ -621,22 +662,23 @@
         limit=2,
     )
     arrived = [swap(m, "ep", d) for d, m in zip(diagonals, sent)]
-    own, own_sums, _ = call(
-        functools.partial(leaf_rest_body, [0] + links, share),
-        [finished, resident((rows, LANES), F32), sums_shape],
-        meta,
-        leaf,
-        *scans,
-        bases,
+    piece = resident((len(links), rows, share), F32)
+    received = [*[coded[d] for d in links], *[base[d] for d in links]]
+    args = [meta, leaf, *scans, bases, tie, last, *received]
+    own, own_sums, *held, _ = call(
+        functools.partial(leaf_rest_body, links, share),
+        [finished, resident((rows, LANES), F32)] + [piece] * 3 + [sums_shape],
+        *args,
         acc,
         *sent,
-        aliases={7: 2},
+        aliases={len(args): 5},
+        scratch=[pltpu.VMEM((WIDE, WIDE), BF16)] * 2,
         name="leaf_rest",
-        us=9,
+        us=10,
+        limit=16,
     )
     both, others = across(own_sums, "tm", base.values())
-    piece = pltpu.VMEM((len(links), rows, share), F32)
-    args = [meta, tie, last, *[coded[d] for d in links], *[base[d] for d in links], own]
+    args = [meta, *received, own, *held]
     grad_hess, pred = call(
         functools.partial(finish_body, links),
         [jax.ShapeDtypeStruct((2, rows * parts, share), BF16), resident(wide, F32)],
@@ -644,31 +686,44 @@
         far(predictions),
         hbm=(len(args),),
         hbm_out=(0,),
-        scratch=[pltpu.VMEM((len(links), 2, rows, share), BF16)]
-        + [piece] * 3
-        + [pltpu.VMEM((WIDE, WIDE), BF16)] * 2
-        + [dma((len(links), 2, 4)), dma((1, 2)), dma],
+        scratch=[
+            pltpu.VMEM((len(links), 2, rows, share), BF16),
+            pltpu.VMEM((WIDE, WIDE), BF16),
+            dma((len(links), 2, share // PIECE)),
+            dma((1, 2)),
+            dma,
+        ],
         name="finish",
-        us=8,
-        limit=14,
-    )
-    at_out = 3 + len(diagonals)
-    new_pred, leaf_weights, grad_hess = call(
-        functools.partial(update_body, turns, diagonals),
-        [jax.ShapeDtypeStruct(wide, F32), jax.ShapeDtypeStruct((rows, LEAVES), F32), jax.ShapeDtypeStruct(grad_hess.shape, BF16)],
-        meta,
+        us=4,
+        limit=10,
+    )
+    new_pred, leaf_weights = call(
+        functools.partial(update_body, turns),
+        [jax.ShapeDtypeStruct(wide, F32), jax.ShapeDtypeStruct((rows, LEAVES), F32)],
         pred,
         leaf,
-        *arrived,
-        grad_hess,
         both,
         *others[1:],
-        hbm=range(3, at_out + 1),
-        hbm_out=(0, 2),
-        aliases={at_out: 2},
-        scratch=[pltpu.VMEM(wide, F32), dma((turns,)), dma((max(1, len(diagonals)), 2))],
+        hbm_out=(0, 1),
+        scratch=[pltpu.VMEM(wide, F32), pltpu.VMEM((rows, LEAVES), F32), dma((turns + 1,))],
         name="update",
         us=4,
+    )
+    cuts = 4
+    (grad_hess,) = call(
+        functools.partial(place_body, diagonals, cuts),
+        [jax.ShapeDtypeStruct(grad_hess.shape, BF16)],
+        meta,
+        *[near(x) for x in arrived],
+        grad_hess,
+        far(new_pred),
+        hbm=(1 + len(arrived), 2 + len(arrived)),
+        hbm_out=(0,),
+        aliases={1 + len(arrived): 0},
+        scratch=[dma((max(1, len(arrived)), 2, cuts))],
+        name="place",
+        us=1,
+        limit=2,
     )
     return new_pred, leaf_weights, grad_hess.reshape(2, rows * parts, 1, share)
 

time: 67.1 us -> 63.5 us (0.946)
  waiting for transfers between devices: 7.41 us -> 5.55 us
  Pallas kernels: 37.7 us -> 36.1 us
    ppermute x17, waiting for transfers between devices: 7.41 us -> 5.55 us  [swap(): lax.ppermute(array, axis, [(i, i ^ d) for i in range(lax.axis_size(axis))])]
    pallas_call x13 -> x14, Pallas kernels: 37.7 us -> 36.1 us  [call(): pl.pallas_call(body, out_shape=outs, in_specs=[anywhere if k in hbm else...]
  transfers between devices with their start and end apart: 17 -> 17, of which waited for: 8 -> 7; matrix products, arithmetic and copies ran while one was open for 0% -> 0% of each run, Pallas kernels for 42% -> 48%
where the time goes in v4:
time: 63.5 us; the launch traced here: 63.4 us
  Pallas kernels  36.1 us (57%)
  starting transfers between devices  20.8 us (33%)
  waiting for transfers between devices  5.55 us (9%)
  between operations  0.78 us (1%)
    pallas_call x14, Pallas kernels, call(): pl.pallas_call(body, out_shape=outs, in_specs=[anywhere if k in hbm else...  36.1 us
    ppermute x17, starting transfers between devices, swap(): lax.ppermute(array, axis, [(i, i ^ d) for i in range(lax.axis_size(axis))])  20.8 us
    ppermute x17, waiting for transfers between devices, swap(): lax.ppermute(array, axis, [(i, i ^ d) for i in range(lax.axis_size(axis))])  5.55 us
  transfers between devices with their start and end apart: 17, of which 7 were waited for; matrix products, arithmetic and copies ran while one was open for 0% of the time, Pallas kernels for 48%

profile of v4, /device:TPU:0, one launch (start us, length us, event | category | flops | bytes accessed | tf_op | source)
XLA Modules:
  0.0 63.4 jit_solution(11476593205120202680)
XLA Ops:
  0.6 0.1 pad_add_fusion.meta.refs_0_
  0.7 4.4 %front.1 = (s32[32,32768]{1,0:T(8,128)S(1)}, f32[32,32768]{1,0:T(8,128)S(1)}, f32[32,128]{1,0:T(8,128)S(1)}, s16[2,32,8192]{2,1,0:T(8,128)(2,1)S(1)}, s16[2,32,8192]{2,1,0:T(8,128)(2,1)S(1)}) custom-call(s32[2]{0:T(128)S(1)} %pad_add_fusion.meta.refs_0_, f32[32,32768]{1,0:T(8,128)} %refs_9_.1, s32[32,32768]{1,0:T(8,128)} %events_in.1), custom_call_target="tpu_custom_call" | custom-call | bytes 14000000 | tf_op jit(solution)/shard_map/front/pallas_call | solution.py:39
  5.1 3.0 %collective-permute-start = (s16[2,32,8192]{2,1,0:T(8,128)(2,1)S(1)}, s16[2,32,8192]{2,1,0:T(8,128)(2,1)S(1)}, u32[]{:S(2)}, u32[]{:S(2)}) collective-permute-start(s16[2,32,8192]{2,1,0:T(8,128)(2,1)S(1)} %get-tuple-element.33), channel_id=1, source_target_pairs={{0,8},{8,0},{16,24},{24,16},{1,9},{9,1},{17,25},{25,17},{2,10},{10... | collective-permute-start | bytes 3145736 | tf_op jit(solution)/shard_map/ppermute | solution.py:553
  8.1 1.5 %collective-permute-start.1 = (s16[2,32,8192]{2,1,0:T(8,128)(2,1)S(1)}, s16[2,32,8192]{2,1,0:T(8,128)(2,1)S(1)}, u32[]{:S(2)}, u32[]{:S(2)}) collective-permute-start(s16[2,32,8192]{2,1,0:T(8,128)(2,1)S(1)} %get-tuple-element.34), channel_id=1, source_target_pairs={{0,16},{8,24},{16,0},{24,8},{1,17},{9,25},{17,1},{25,9},{2,18},{10... | collective-permute-start | bytes 3145736 | tf_op jit(solution)/shard_map/ppermute | solution.py:553
  9.6 1.2 %collective-permute-done.2.right.refs_1_ = f32[32,128]{1,0:T(8,128)S(1)} collective-permute-done((f32[32,128]{1,0:T(8,128)S(1)}, f32[32,128]{1,0:T(8,128)S(1)}, u32[]{:S(2)}, u32[]{:S(2)}) %collective-permute-start.2) | collective-permute-done | bytes 16416 | tf_op jit(solution)/shard_map/ppermute | solution.py:553
  10.8 3.6 %collective-permute-start.5 = (f32[32,128]{1,0:T(8,128)S(1)}, f32[32,128]{1,0:T(8,128)S(1)}, u32[]{:S(2)}, u32[]{:S(2)}) collective-permute-start(f32[32,128]{1,0:T(8,128)S(1)} %pair.3), channel_id=1, source_target_pairs={{0,6},{1,7},{2,4},{3,5},{4,2},{5,3},{6,0},{7,1},{8,14},{9,15},{10,... | collective-permute-start | bytes 49160 | tf_op jit(solution)/shard_map/ppermute | solution.py:553
  14.4 0.8 %collective-permute-start.3 = (f32[32,128]{1,0:T(8,128)S(1)}, f32[32,128]{1,0:T(8,128)S(1)}, u32[]{:S(2)}, u32[]{:S(2)}) collective-permute-start(f32[32,128]{1,0:T(8,128)S(1)} %pair.3), channel_id=1, source_target_pairs={{0,2},{1,3},{2,0},{3,1},{4,6},{5,7},{6,4},{7,5},{8,10},{9,11},{10,... | collective-permute-start | bytes 49160 | tf_op jit(solution)/shard_map/ppermute | solution.py:553
  15.2 3.7 %scan.1 = (f32[32,32768]{1,0:T(8,128)S(1)}, s32[8,32768]{1,0:T(8,128)S(1)}, s32[256,128]{1,0:T(8,128)S(1)}, s32[32,32768]{1,0:T(8,128)S(1)}) custom-call(f32[32,32768]{1,0:T(8,128)S(1)} %get-tuple-element.36.weight.refs_1_, s32[32,32768]{1,0:T(8,128)S(1)} %get-tuple-element.37.events.refs_2_, s32[256,128]{1,0:T(8,128)S(1)} %bitcast.6, s32[32,32768]{1,0:T(8,128)} %leaf_in.1), custom_call_target="tpu_custom_call" | custom-call | bytes 17500000 | tf_op jit(solution)/shard_map/scan/pallas_call | solution.py:39
  18.9 0.2 collective-permute-done.4.refs_3_
  19.0 2.2 %inverse.1 = (f32[32,32768]{1,0:T(8,128)S(1)}, f32[32,32768]{1,0:T(8,128)S(1)}, f32[64,128]{1,0:T(8,128)S(1)}, f32[4,32,128]{2,1,0:T(8,128)S(1)}) custom-call(s32[2]{0:T(128)S(1)} %pad_add_fusion.meta.refs_0_, f32[32,128]{1,0:T(8,128)S(1)} %collective-permute-done.2.right.refs_1_, ...), custom_call_target="tpu_custom_call", output_to_operand_aliasing={{0}: (5, {})} | custom-call | bytes 5250000 | tf_op jit(solution)/shard_map/inverse/pallas_call | solution.py:39
  21.2 0.1 collective-permute-start.6
  21.3 1.2 %collective-permute-done.6.right.refs_1_ = f32[64,128]{1,0:T(8,128)S(1)} collective-permute-done((f32[64,128]{1,0:T(8,128)S(1)}, f32[64,128]{1,0:T(8,128)S(1)}, u32[]{:S(2)}, u32[]{:S(2)}) %collective-permute-start.6) | collective-permute-done | bytes 32800 | tf_op jit(solution)/shard_map/ppermute | solution.py:553
  22.5 3.4 %collective-permute-start.9 = (f32[64,128]{1,0:T(8,128)S(1)}, f32[64,128]{1,0:T(8,128)S(1)}, u32[]{:S(2)}, u32[]{:S(2)}) collective-permute-start(f32[64,128]{1,0:T(8,128)S(1)} %pair.4), channel_id=1, source_target_pairs={{0,6},{1,7},{2,4},{3,5},{4,2},{5,3},{6,0},{7,1},{8,14},{9,15},{10,... | collective-permute-start | bytes 98312 | tf_op jit(solution)/shard_map/ppermute | solution.py:553
  25.9 0.9 %collective-permute-start.7 = (f32[64,128]{1,0:T(8,128)S(1)}, f32[64,128]{1,0:T(8,128)S(1)}, u32[]{:S(2)}, u32[]{:S(2)}) collective-permute-start(f32[64,128]{1,0:T(8,128)S(1)} %pair.4), channel_id=1, source_target_pairs={{0,2},{1,3},{2,0},{3,1},{4,6},{5,7},{6,4},{7,5},{8,10},{9,11},{10,... | collective-permute-start | bytes 98312 | tf_op jit(solution)/shard_map/ppermute | solution.py:553
  26.9 2.7 %accum.1 = (f32[32,32768]{1,0:T(8,128)S(1)}, f32[32,32768]{1,0:T(8,128)S(1)}, f32[4,64,128]{2,1,0:T(8,128)S(1)}) custom-call(f32[32,32768]{1,0:T(8,128)S(1)} %get-tuple-element.42.inv_one, f32[32,32768]{1,0:T(8,128)S(1)} %get-tuple-element.43.inv_two), custom_call_target="tpu_custom_call", output_to_operand_aliasing={{0}: (0, {}), {1}: (1, {})} | custom-call | bytes 10500000 | tf_op jit(solution)/shard_map/accum/pallas_call | solution.py:39
  29.5 0.0 copy-start
  29.6 1.2 %collective-permute-done.8.refs_3_ = f32[64,128]{1,0:T(8,128)S(1)} collective-permute-done((f32[64,128]{1,0:T(8,128)S(1)}, f32[64,128]{1,0:T(8,128)S(1)}, u32[]{:S(2)}, u32[]{:S(2)}) %collective-permute-start.8) | collective-permute-done | bytes 32800 | tf_op jit(solution)/shard_map/ppermute | solution.py:553
  30.7 0.6 bases.1
  31.3 0.6 collective-permute-start.10
  31.9 0.5 collective-permute-start.11
  32.4 2.9 %leaf_first.1 = (bf16[2,32,8192]{2,1,0:T(8,128)(2,1)S(1)}, f32[2,256,256]{2,1,0:T(8,128)S(1)}) custom-call(s32[2]{0:T(128)S(1)} %pad_add_fusion.meta.refs_0_, s32[32,32768]{1,0:T(8,128)S(1)} %get-tuple-element.47.refs_0_.leaf, f32[32,32768]{1,0:T(8,128)S(1)} %get-tuple-element.36.weight.refs_1_, s32[32,32768]{1,0:T(8,128)S(1)} %get-tuple-element.37.events.refs_2_, ...), custom_call_target="tpu_custom_call" | custom-call | bytes 10500000 | tf_op jit(solution)/shard_map/leaf_first/pallas_call | solution.py:39
  35.4 0.1 collective-permute-done.10.refs_1_.refs_10_.refs_3_.refs_0_
  35.5 0.5 collective-permute-done.11.refs_2_.refs_11_.refs_4_.refs_1_
  36.0 1.9 %collective-permute-start.16 = (bf16[2,32,8192]{2,1,0:T(8,128)(2,1)S(1)}, bf16[2,32,8192]{2,1,0:T(8,128)(2,1)S(1)}, u32[]{:S(2)}, u32[]{:S(2)}) collective-permute-start(bf16[2,32,8192]{2,1,0:T(8,128)(2,1)S(1)} %release.1.refs_13_), channel_id=1, source_target_pairs={{0,24},{8,16},{16,8},{24,0},{1,25},{9,17},{17,9},{25,1},{2,26},{10... | collective-permute-start | bytes 3145736 | tf_op jit(solution)/shard_map/ppermute | solution.py:553
  37.9 10.2 %leaf_rest.1 = (bf16[2,32,8192]{2,1,0:T(8,128)(2,1)S(1)}, f32[32,128]{1,0:T(8,128)S(1)}, f32[2,32,8192]{2,1,0:T(8,128)S(1)}, f32[2,32,8192]{2,1,0:T(8,128)S(1)},...) custom-call(s32[2]{0:T(128)S(1)} %pad_add_fusion.meta.refs_0_, ...), custom_call_target="tpu_custom_call", output_to_operand_aliasing={{5}: (13, {})} | custom-call | bytes 35000000 | tf_op jit(solution)/shard_map/leaf_rest/pallas_call | solution.py:39
  48.1 0.1 collective-permute-start.12
  48.2 1.2 %collective-permute-done.12.right = f32[32,128]{1,0:T(8,128)S(1)} collective-permute-done((f32[32,128]{1,0:T(8,128)S(1)}, f32[32,128]{1,0:T(8,128)S(1)}, u32[]{:S(2)}, u32[]{:S(2)}) %collective-permute-start.12) | collective-permute-done | bytes 16416 | tf_op jit(solution)/shard_map/ppermute | solution.py:553
  49.4 2.3 %collective-permute-start.15 = (f32[32,128]{1,0:T(8,128)S(1)}, f32[32,128]{1,0:T(8,128)S(1)}, u32[]{:S(2)}, u32[]{:S(2)}) collective-permute-start(f32[32,128]{1,0:T(8,128)S(1)} %pair.5.refs_0_), channel_id=1, source_target_pairs={{0,6},{1,7},{2,4},{3,5},{4,2},{5,3},{6,0},{7,1},{8,14},{9,15},{10,... | collective-permute-start | bytes 49160 | tf_op jit(solution)/shard_map/ppermute | solution.py:553
  51.7 2.1 %collective-permute-start.13 = (f32[32,128]{1,0:T(8,128)S(1)}, f32[32,128]{1,0:T(8,128)S(1)}, u32[]{:S(2)}, u32[]{:S(2)}) collective-permute-start(f32[32,128]{1,0:T(8,128)S(1)} %pair.5.refs_0_), channel_id=1, source_target_pairs={{0,2},{1,3},{2,0},{3,1},{4,6},{5,7},{6,4},{7,5},{8,10},{9,11},{10,... | collective-permute-start | bytes 49160 | tf_op jit(solution)/shard_map/ppermute | solution.py:553
  53.8 4.0 %finish.1 = (bf16[2,128,8192]{2,1,0:T(8,128)(2,1)}, f32[32,32768]{1,0:T(8,128)S(1)}) custom-call(s32[2]{0:T(128)S(1)} %pad_add_fusion.meta.refs_0_, s16[2,32,8192]{2,1,0:T(8,128)(2,1)S(1)} %collective-permute-done.refs_3_.refs_8_.refs_1_, s16[2,32,8192]{2,1,0:T(8,128)(2,1)S(1)} %collective-permute-done.1.refs_4_.refs_9_.refs_2_, ...), custom_call_target="tpu_custom_call" | custom-call | bytes 14000000 | tf_op jit(solution)/shard_map/finish/pallas_call | solution.py:39
  57.9 3.9 %update.1 = (f32[32,32768]{1,0:T(8,128)}, f32[32,64]{1,0:T(8,128)}) custom-call(f32[32,32768]{1,0:T(8,128)S(1)} %get-tuple-element.58.pred, s32[32,32768]{1,0:T(8,128)S(1)} %get-tuple-element.47.refs_0_.leaf, f32[32,128]{1,0:T(8,128)S(1)} %pair.5.refs_0_, f32[32,128]{1,0:T(8,128)S(1)} %collective-permute-done.13.refs_1_, ...), custom_call_target="tpu_custom_call" | custom-call | bytes 14000000 | tf_op jit(solution)/shard_map/update/pallas_call | solution.py:39
  61.8 1.6 %place.1 = bf16[2,128,8192]{2,1,0:T(8,128)(2,1)} custom-call(s32[2]{0:T(128)S(1)} %pad_add_fusion.meta.refs_0_, bf16[2,32,8192]{2,1,0:T(8,128)(2,1)S(1)} %collective-permute-done.16.refs_0_, bf16[2,128,8192]{2,1,0:T(8,128)(2,1)} %get-tuple-element.62.refs_1_, f32[32,32768]{1,0:T(8,128)} %get-tuple-element.63.refs_2_), custom_call_target="tpu_custom_call", output_to_operand_aliasing={{}: (2, {})} | custom-call | bytes 3500000 | tf_op jit(solution)/shard_map/place/pallas_call | solution.py:39
  (23 shorter events, 0.1 us)
Async XLA Ops:
  0.7 14.5 %copy-start.2 = (s32[32768]{0:T(1024)S(1)}, s32[32768]{0:T(1024)}, u32[]{:S(2)}) copy-start(s32[32768]{0:T(1024)} %param.7) | copy-start | bytes 393220
  5.1 30.9 %collective-permute-start = (s16[2,32,8192]{2,1,0:T(8,128)(2,1)S(1)}, s16[2,32,8192]{2,1,0:T(8,128)(2,1)S(1)}, u32[]{:S(2)}, u32[]{:S(2)}) collective-permute-start(s16[2,32,8192]{2,1,0:T(8,128)(2,1)S(1)} %get-tuple-element.33), channel_id=1, source_target_pairs={{0,8},{8,0},{16,24},{24,16},{1,9},{9,1},{17,25},{25,17},{2,10},{10... | collective-permute-start | bytes 3145736 | tf_op jit(solution)/shard_map/ppermute | solution.py:553
  8.1 27.9 %collective-permute-start.1 = (s16[2,32,8192]{2,1,0:T(8,128)(2,1)S(1)}, s16[2,32,8192]{2,1,0:T(8,128)(2,1)S(1)}, u32[]{:S(2)}, u32[]{:S(2)}) collective-permute-start(s16[2,32,8192]{2,1,0:T(8,128)(2,1)S(1)} %get-tuple-element.34), channel_id=1, source_target_pairs={{0,16},{8,24},{16,0},{24,8},{1,17},{9,25},{17,1},{25,9},{2,18},{10... | collective-permute-start | bytes 3145736 | tf_op jit(solution)/shard_map/ppermute | solution.py:553
  9.6 1.2 %collective-permute-start.2 = (f32[32,128]{1,0:T(8,128)S(1)}, f32[32,128]{1,0:T(8,128)S(1)}, u32[]{:S(2)}, u32[]{:S(2)}) collective-permute-start(f32[32,128]{1,0:T(8,128)S(1)} %get-tuple-element.35.left), channel_id=1, source_target_pairs={{0,1},{1,0},{2,3},{3,2},{4,5},{5,4},{6,7},{7,6},{8,9},{9,8},{10,11... | collective-permute-start | bytes 49160 | tf_op jit(solution)/shard_map/ppermute | solution.py:553
  10.8 8.1 %collective-permute-start.5 = (f32[32,128]{1,0:T(8,128)S(1)}, f32[32,128]{1,0:T(8,128)S(1)}, u32[]{:S(2)}, u32[]{:S(2)}) collective-permute-start(f32[32,128]{1,0:T(8,128)S(1)} %pair.3), channel_id=1, source_target_pairs={{0,6},{1,7},{2,4},{3,5},{4,2},{5,3},{6,0},{7,1},{8,14},{9,15},{10,... | collective-permute-start | bytes 49160 | tf_op jit(solution)/shard_map/ppermute | solution.py:553
  14.4 4.6 %collective-permute-start.4 = (f32[32,128]{1,0:T(8,128)S(1)}, f32[32,128]{1,0:T(8,128)S(1)}, u32[]{:S(2)}, u32[]{:S(2)}) collective-permute-start(f32[32,128]{1,0:T(8,128)S(1)} %pair.3), channel_id=1, source_target_pairs={{0,4},{1,5},{2,6},{3,7},{4,0},{5,1},{6,2},{7,3},{8,12},{9,13},{10,... | collective-permute-start | bytes 49160 | tf_op jit(solution)/shard_map/ppermute | solution.py:553
  14.4 4.6 %collective-permute-start.3 = (f32[32,128]{1,0:T(8,128)S(1)}, f32[32,128]{1,0:T(8,128)S(1)}, u32[]{:S(2)}, u32[]{:S(2)}) collective-permute-start(f32[32,128]{1,0:T(8,128)S(1)} %pair.3), channel_id=1, source_target_pairs={{0,2},{1,3},{2,0},{3,1},{4,6},{5,7},{6,4},{7,5},{8,10},{9,11},{10,... | collective-permute-start | bytes 49160 | tf_op jit(solution)/shard_map/ppermute | solution.py:553
  21.2 1.3 %collective-permute-start.6 = (f32[64,128]{1,0:T(8,128)S(1)}, f32[64,128]{1,0:T(8,128)S(1)}, u32[]{:S(2)}, u32[]{:S(2)}) collective-permute-start(f32[64,128]{1,0:T(8,128)S(1)} %get-tuple-element.40.left), channel_id=1, source_target_pairs={{0,1},{1,0},{2,3},{3,2},{4,5},{5,4},{6,7},{7,6},{8,9},{9,8},{10,11... | collective-permute-start | bytes 98312 | tf_op jit(solution)/shard_map/ppermute | solution.py:553
  22.5 7.1 %collective-permute-start.9 = (f32[64,128]{1,0:T(8,128)S(1)}, f32[64,128]{1,0:T(8,128)S(1)}, u32[]{:S(2)}, u32[]{:S(2)}) collective-permute-start(f32[64,128]{1,0:T(8,128)S(1)} %pair.4), channel_id=1, source_target_pairs={{0,6},{1,7},{2,4},{3,5},{4,2},{5,3},{6,0},{7,1},{8,14},{9,15},{10,... | collective-permute-start | bytes 98312 | tf_op jit(solution)/shard_map/ppermute | solution.py:553
  25.9 4.8 %collective-permute-start.8 = (f32[64,128]{1,0:T(8,128)S(1)}, f32[64,128]{1,0:T(8,128)S(1)}, u32[]{:S(2)}, u32[]{:S(2)}) collective-permute-start(f32[64,128]{1,0:T(8,128)S(1)} %pair.4), channel_id=1, source_target_pairs={{0,4},{1,5},{2,6},{3,7},{4,0},{5,1},{6,2},{7,3},{8,12},{9,13},{10,... | collective-permute-start | bytes 98312 | tf_op jit(solution)/shard_map/ppermute | solution.py:553
  25.9 4.8 %collective-permute-start.7 = (f32[64,128]{1,0:T(8,128)S(1)}, f32[64,128]{1,0:T(8,128)S(1)}, u32[]{:S(2)}, u32[]{:S(2)}) collective-permute-start(f32[64,128]{1,0:T(8,128)S(1)} %pair.4), channel_id=1, source_target_pairs={{0,2},{1,3},{2,0},{3,1},{4,6},{5,7},{6,4},{7,5},{8,10},{9,11},{10,... | collective-permute-start | bytes 98312 | tf_op jit(solution)/shard_map/ppermute | solution.py:553
  29.5 5.8 %copy-start = (f32[32,32768]{1,0:T(8,128)}, f32[32,32768]{1,0:T(8,128)S(1)}, u32[]{:S(2)}) copy-start(f32[32,32768]{1,0:T(8,128)S(1)} %get-tuple-element.49.refs_4_) | copy-start | bytes 12582916
  31.3 4.2 %collective-permute-start.10 = (f32[96,128]{1,0:T(8,128)S(1)}, f32[96,128]{1,0:T(8,128)S(1)}, u32[]{:S(2)}, u32[]{:S(2)}) collective-permute-start(f32[96,128]{1,0:T(8,128)S(1)} %get-tuple-element.45), channel_id=1, source_target_pairs={{0,8},{8,0},{16,24},{24,16},{1,9},{9,1},{17,25},{25,17},{2,10},{10... | collective-permute-start | bytes 147464 | tf_op jit(solution)/shard_map/ppermute | solution.py:553
  31.9 4.1 %collective-permute-start.11 = (f32[96,128]{1,0:T(8,128)S(1)}, f32[96,128]{1,0:T(8,128)S(1)}, u32[]{:S(2)}, u32[]{:S(2)}) collective-permute-start(f32[96,128]{1,0:T(8,128)S(1)} %get-tuple-element.46), channel_id=1, source_target_pairs={{0,16},{8,24},{16,0},{24,8},{1,17},{9,25},{17,1},{25,9},{2,18},{10... | collective-permute-start | bytes 147464 | tf_op jit(solution)/shard_map/ppermute | solution.py:553
  35.5 2.5 %copy-start.1 = (f32[32,32768]{1,0:T(8,128)S(1)}, f32[32,32768]{1,0:T(8,128)}, u32[]{:S(2)}) copy-start(f32[32,32768]{1,0:T(8,128)} %copy-done) | copy-start | bytes 12582916
  36.0 25.8 %collective-permute-start.16 = (bf16[2,32,8192]{2,1,0:T(8,128)(2,1)S(1)}, bf16[2,32,8192]{2,1,0:T(8,128)(2,1)S(1)}, u32[]{:S(2)}, u32[]{:S(2)}) collective-permute-start(bf16[2,32,8192]{2,1,0:T(8,128)(2,1)S(1)} %release.1.refs_13_), channel_id=1, source_target_pairs={{0,24},{8,16},{16,8},{24,0},{1,25},{9,17},{17,9},{25,1},{2,26},{10... | collective-permute-start | bytes 3145736 | tf_op jit(solution)/shard_map/ppermute | solution.py:553
  48.1 1.2 %collective-permute-start.12 = (f32[32,128]{1,0:T(8,128)S(1)}, f32[32,128]{1,0:T(8,128)S(1)}, u32[]{:S(2)}, u32[]{:S(2)}) collective-permute-start(f32[32,128]{1,0:T(8,128)S(1)} %get-tuple-element.59.left), channel_id=1, source_target_pairs={{0,1},{1,0},{2,3},{3,2},{4,5},{5,4},{6,7},{7,6},{8,9},{9,8},{10,11... | collective-permute-start | bytes 49160 | tf_op jit(solution)/shard_map/ppermute | solution.py:553
  49.4 8.4 %collective-permute-start.15 = (f32[32,128]{1,0:T(8,128)S(1)}, f32[32,128]{1,0:T(8,128)S(1)}, u32[]{:S(2)}, u32[]{:S(2)}) collective-permute-start(f32[32,128]{1,0:T(8,128)S(1)} %pair.5.refs_0_), channel_id=1, source_target_pairs={{0,6},{1,7},{2,4},{3,5},{4,2},{5,3},{6,0},{7,1},{8,14},{9,15},{10,... | collective-permute-start | bytes 49160 | tf_op jit(solution)/shard_map/ppermute | solution.py:553
  51.7 6.1 %collective-permute-start.14 = (f32[32,128]{1,0:T(8,128)S(1)}, f32[32,128]{1,0:T(8,128)S(1)}, u32[]{:S(2)}, u32[]{:S(2)}) collective-permute-start(f32[32,128]{1,0:T(8,128)S(1)} %pair.5.refs_0_), channel_id=1, source_target_pairs={{0,4},{1,5},{2,6},{3,7},{4,0},{5,1},{6,2},{7,3},{8,12},{9,13},{10,... | collective-permute-start | bytes 49160 | tf_op jit(solution)/shard_map/ppermute | solution.py:553
  51.7 6.1 %collective-permute-start.13 = (f32[32,128]{1,0:T(8,128)S(1)}, f32[32,128]{1,0:T(8,128)S(1)}, u32[]{:S(2)}, u32[]{:S(2)}) collective-permute-start(f32[32,128]{1,0:T(8,128)S(1)} %pair.5.refs_0_), channel_id=1, source_target_pairs={{0,2},{1,3},{2,0},{3,1},{4,6},{5,7},{6,4},{7,5},{8,10},{9,11},{10,... | collective-permute-start | bytes 49160 | tf_op jit(solution)/shard_map/ppermute | solution.py:553

commit v5 on v4

--- a/solution.py
+++ b/solution.py
@@ -32,7 +32,7 @@
     return pltpu.with_memory_space_constraint(array, pltpu.HBM)
 
 
-def call(body, outs, *args, scratch=(), name=None, us=1.0, aliases=None, limit=12, hbm=(), hbm_out=()):
+def call(body, outs, *args, scratch=(), name=None, us=1.0, aliases=None, limit=8, hbm=(), hbm_out=()):
     vmem = pl.BlockSpec(memory_space=pltpu.VMEM)
     smem = pl.BlockSpec(memory_space=pltpu.SMEM)
     anywhere = pl.BlockSpec(memory_space=pltpu.HBM)
@@ -214,7 +214,7 @@
                 )
         return carry
 
-    lax.fori_loop(0, steps, one, jnp.zeros((rows, LANES), F32), unroll=2)
+    lax.fori_loop(0, steps, one, jnp.zeros((rows, LANES), F32), unroll=4)
     fetch.wait()
 
 
@@ -255,7 +255,7 @@
         return (sum_one + fold(first), sum_two + fold(second))
 
     empty = jnp.zeros((rows, LANES), F32)
-    sum_one, sum_two = lax.fori_loop(0, length // step, one, (empty, empty), unroll=2)
+    sum_one, sum_two = lax.fori_loop(0, length // step, one, (empty, empty), unroll=4)
     totals[:rows, :] = lane_sum(sum_one)
     totals[rows:, :] = lane_sum(sum_two)
 
@@ -354,9 +354,7 @@
 def finish_body(partners, *refs):
     meta, refs = refs[0], refs[1:]
     messages, base = refs[: len(partners)], refs[len(partners) : 2 * len(partners)]
-    own, kept, inv_one, inv_two, pred_in, out, pred, scratch, lower, sems, own_sems, fetch_sem = refs[2 * len(partners) :]
-    fetch = pltpu.make_async_copy(pred_in, pred, fetch_sem)
-    fetch.start()
+    own, kept, inv_one, inv_two, out, scratch, lower, sems, own_sems = refs[2 * len(partners) :]
     own_copies = place_pieces(meta, [0], [own], out, own_sems)
     for copy in own_copies:
         copy.start()
@@ -401,13 +399,12 @@
             copy.start()
         return tuple(made)
 
-    lax.fori_loop(0, steps, one, tuple((b[rows : 2 * rows, :], b[2 * rows :, :]) for b in base))
+    lax.fori_loop(0, steps, one, tuple((b[rows : 2 * rows, :], b[2 * rows :, :]) for b in base), unroll=2)
     for turn in range(steps):
         for copy in copies(turn):
             copy.wait()
     for copy in own_copies:
         copy.wait()
-    fetch.wait()
 
 
 GROUP = 16
@@ -459,7 +456,10 @@
 def leaf_rest_body(links, size, meta, *refs):
     ins, tie, last = refs[:6], refs[6], refs[7]
     messages, base = refs[8 : 8 + len(links)], refs[8 + len(links) : 8 + 2 * len(links)]
-    own, sums, kept, inv_one, inv_two, acc, upper, lower = refs[-8:]
+    pred_in = refs[-12]
+    own, sums, kept, inv_one, inv_two, pred, acc, upper, lower, sem = refs[-10:]
+    fetch = pltpu.make_async_copy(pred_in, pred, sem)
+    fetch.start()
     upper[...] = scan_matrix(True)
     lower[...] = triangle(False)
     rows = kept.shape[1]
@@ -478,7 +478,7 @@
             leaf_step(span(share_of(meta, d, size) + at, PIECE), *ins, acc, None, None)
         return tuple(made)
 
-    lax.fori_loop(0, size // PIECE, one, tuple(b[:rows, :] for b in base))
+    lax.fori_loop(0, size // PIECE, one, tuple(b[:rows, :] for b in base), unroll=2)
     width = LOW * GROUP
     side = HIGH * GROUP
     same = lax.broadcasted_iota(jnp.int32, (side, width), 0) % GROUP == lax.broadcasted_iota(jnp.int32, (side, width), 1) % GROUP
@@ -502,6 +502,7 @@
                 at = ((group * 2 + value) * HIGH + h) * GROUP
                 out = out + pltpu.roll(by_low[at : at + GROUP], h * LOW + value * LEAVES, 1)
         sums[group * GROUP : (group + 1) * GROUP, :] = out
+    fetch.wait()
 
 
 def place_body(partners, cuts, meta, *refs):
@@ -665,37 +666,35 @@
     piece = resident((len(links), rows, share), F32)
     received = [*[coded[d] for d in links], *[base[d] for d in links]]
     args = [meta, leaf, *scans, bases, tie, last, *received]
-    own, own_sums, *held, _ = call(
+    own, own_sums, *held, pred, _ = call(
         functools.partial(leaf_rest_body, links, share),
-        [finished, resident((rows, LANES), F32)] + [piece] * 3 + [sums_shape],
+        [finished, resident((rows, LANES), F32)] + [piece] * 3 + [resident(wide, F32), sums_shape],
         *args,
         acc,
         *sent,
-        aliases={len(args): 5},
-        scratch=[pltpu.VMEM((WIDE, WIDE), BF16)] * 2,
+        far(predictions),
+        bases,
+        hbm=(len(args) + 1 + len(sent),),
+        aliases={len(args): 6},
+        scratch=[pltpu.VMEM((WIDE, WIDE), BF16)] * 2 + [dma],
         name="leaf_rest",
         us=10,
-        limit=16,
     )
     both, others = across(own_sums, "tm", base.values())
     args = [meta, *received, own, *held]
-    grad_hess, pred = call(
+    (grad_hess,) = call(
         functools.partial(finish_body, links),
-        [jax.ShapeDtypeStruct((2, rows * parts, share), BF16), resident(wide, F32)],
+        [jax.ShapeDtypeStruct((2, rows * parts, share), BF16)],
         *args,
-        far(predictions),
-        hbm=(len(args),),
         hbm_out=(0,),
         scratch=[
             pltpu.VMEM((len(links), 2, rows, share), BF16),
             pltpu.VMEM((WIDE, WIDE), BF16),
             dma((len(links), 2, share // PIECE)),
             dma((1, 2)),
-            dma,
         ],
         name="finish",
         us=4,
-        limit=10,
     )
     new_pred, leaf_weights = call(
         functools.partial(update_body, turns),

time: 63.5 us -> 62.3 us (0.981)
  Pallas kernels: 36.1 us -> 34.8 us
    pallas_call x14, Pallas kernels: 36.1 us -> 34.8 us  [call(): pl.pallas_call(body, out_shape=outs, in_specs=[anywhere if k in hbm else...]
  transfers between devices with their start and end apart: 17 -> 17, of which waited for: 7 -> 7; matrix products, arithmetic and copies ran while one was open for 0% -> 0% of each run, Pallas kernels for 48% -> 46%
where the time goes in v5:
time: 62.3 us; the launch traced here: 62.2 us
  Pallas kernels  34.8 us (56%)
  starting transfers between devices  20.8 us (33%)
  waiting for transfers between devices  5.58 us (9%)
  between operations  0.93 us (1%)
    pallas_call x14, Pallas kernels, call(): pl.pallas_call(body, out_shape=outs, in_specs=[anywhere if k in hbm else...  34.8 us
    ppermute x17, starting transfers between devices, swap(): lax.ppermute(array, axis, [(i, i ^ d) for i in range(lax.axis_size(axis))])  20.8 us
    ppermute x17, waiting for transfers between devices, swap(): lax.ppermute(array, axis, [(i, i ^ d) for i in range(lax.axis_size(axis))])  5.58 us
  transfers between devices with their start and end apart: 17, of which 7 were waited for; matrix products, arithmetic and copies ran while one was open for 0% of the time, Pallas kernels for 46%

profile of v5, /device:TPU:0, one launch (start us, length us, event | category | flops | bytes accessed | tf_op | source)
XLA Modules:
  0.0 62.2 jit_solution(8904030344613230556)
XLA Ops:
  0.6 0.1 pad_add_fusion.meta.refs_0_
  0.7 4.4 %front.1 = (s32[32,32768]{1,0:T(8,128)S(1)}, f32[32,32768]{1,0:T(8,128)S(1)}, f32[32,128]{1,0:T(8,128)S(1)}, s16[2,32,8192]{2,1,0:T(8,128)(2,1)S(1)}, s16[2,32,8192]{2,1,0:T(8,128)(2,1)S(1)}) custom-call(s32[2]{0:T(128)S(1)} %pad_add_fusion.meta.refs_0_, f32[32,32768]{1,0:T(8,128)} %refs_14_.1, s32[32,32768]{1,0:T(8,128)} %events_in.1), custom_call_target="tpu_custom_call" | custom-call | bytes 14000000 | tf_op jit(solution)/shard_map/front/pallas_call | solution.py:39
  5.1 3.0 %collective-permute-start.8 = (s16[2,32,8192]{2,1,0:T(8,128)(2,1)S(1)}, s16[2,32,8192]{2,1,0:T(8,128)(2,1)S(1)}, u32[]{:S(2)}, u32[]{:S(2)}) collective-permute-start(s16[2,32,8192]{2,1,0:T(8,128)(2,1)S(1)} %get-tuple-element.47), channel_id=1, source_target_pairs={{0,8},{8,0},{16,24},{24,16},{1,9},{9,1},{17,25},{25,17},{2,10},{10... | collective-permute-start | bytes 3145736 | tf_op jit(solution)/shard_map/ppermute | solution.py:554
  8.1 1.5 %collective-permute-start.9 = (s16[2,32,8192]{2,1,0:T(8,128)(2,1)S(1)}, s16[2,32,8192]{2,1,0:T(8,128)(2,1)S(1)}, u32[]{:S(2)}, u32[]{:S(2)}) collective-permute-start(s16[2,32,8192]{2,1,0:T(8,128)(2,1)S(1)} %get-tuple-element.48), channel_id=1, source_target_pairs={{0,16},{8,24},{16,0},{24,8},{1,17},{9,25},{17,1},{25,9},{2,18},{10... | collective-permute-start | bytes 3145736 | tf_op jit(solution)/shard_map/ppermute | solution.py:554
  9.6 1.2 %collective-permute-done.right.refs_1_ = f32[32,128]{1,0:T(8,128)S(1)} collective-permute-done((f32[32,128]{1,0:T(8,128)S(1)}, f32[32,128]{1,0:T(8,128)S(1)}, u32[]{:S(2)}, u32[]{:S(2)}) %collective-permute-start) | collective-permute-done | bytes 16416 | tf_op jit(solution)/shard_map/ppermute | solution.py:554
  10.8 3.6 %collective-permute-start.3 = (f32[32,128]{1,0:T(8,128)S(1)}, f32[32,128]{1,0:T(8,128)S(1)}, u32[]{:S(2)}, u32[]{:S(2)}) collective-permute-start(f32[32,128]{1,0:T(8,128)S(1)} %pair.3), channel_id=1, source_target_pairs={{0,6},{1,7},{2,4},{3,5},{4,2},{5,3},{6,0},{7,1},{8,14},{9,15},{10,... | collective-permute-start | bytes 49160 | tf_op jit(solution)/shard_map/ppermute | solution.py:554
  14.4 0.8 %collective-permute-start.1 = (f32[32,128]{1,0:T(8,128)S(1)}, f32[32,128]{1,0:T(8,128)S(1)}, u32[]{:S(2)}, u32[]{:S(2)}) collective-permute-start(f32[32,128]{1,0:T(8,128)S(1)} %pair.3), channel_id=1, source_target_pairs={{0,2},{1,3},{2,0},{3,1},{4,6},{5,7},{6,4},{7,5},{8,10},{9,11},{10,... | collective-permute-start | bytes 49160 | tf_op jit(solution)/shard_map/ppermute | solution.py:554
  15.2 3.5 %scan.1 = (f32[32,32768]{1,0:T(8,128)S(1)}, s32[8,32768]{1,0:T(8,128)S(1)}, s32[256,128]{1,0:T(8,128)S(1)}, s32[32,32768]{1,0:T(8,128)S(1)}) custom-call(f32[32,32768]{1,0:T(8,128)S(1)} %get-tuple-element.32.weight.refs_1_, s32[32,32768]{1,0:T(8,128)S(1)} %get-tuple-element.33.events.refs_2_, s32[256,128]{1,0:T(8,128)S(1)} %bitcast.6, s32[32,32768]{1,0:T(8,128)} %leaf_in.1), custom_call_target="tpu_custom_call" | custom-call | bytes 17500000 | tf_op jit(solution)/shard_map/scan/pallas_call | solution.py:39
  18.7 0.0 collective-permute-done.3.refs_4_
  18.8 0.3 collective-permute-done.2.refs_3_
  19.0 2.1 %inverse.1 = (f32[32,32768]{1,0:T(8,128)S(1)}, f32[32,32768]{1,0:T(8,128)S(1)}, f32[64,128]{1,0:T(8,128)S(1)}, f32[4,32,128]{2,1,0:T(8,128)S(1)}) custom-call(s32[2]{0:T(128)S(1)} %pad_add_fusion.meta.refs_0_, f32[32,128]{1,0:T(8,128)S(1)} %collective-permute-done.right.refs_1_, ...), custom_call_target="tpu_custom_call", output_to_operand_aliasing={{0}: (5, {})} | custom-call | bytes 5250000 | tf_op jit(solution)/shard_map/inverse/pallas_call | solution.py:39
  21.1 0.0 collective-permute-start.4
  21.2 1.2 %collective-permute-done.4.right.refs_1_ = f32[64,128]{1,0:T(8,128)S(1)} collective-permute-done((f32[64,128]{1,0:T(8,128)S(1)}, f32[64,128]{1,0:T(8,128)S(1)}, u32[]{:S(2)}, u32[]{:S(2)}) %collective-permute-start.4) | collective-permute-done | bytes 32800 | tf_op jit(solution)/shard_map/ppermute | solution.py:554
  22.4 3.3 %collective-permute-start.7 = (f32[64,128]{1,0:T(8,128)S(1)}, f32[64,128]{1,0:T(8,128)S(1)}, u32[]{:S(2)}, u32[]{:S(2)}) collective-permute-start(f32[64,128]{1,0:T(8,128)S(1)} %pair.4), channel_id=1, source_target_pairs={{0,6},{1,7},{2,4},{3,5},{4,2},{5,3},{6,0},{7,1},{8,14},{9,15},{10,... | collective-permute-start | bytes 98312 | tf_op jit(solution)/shard_map/ppermute | solution.py:554
  25.7 1.1 %collective-permute-start.5 = (f32[64,128]{1,0:T(8,128)S(1)}, f32[64,128]{1,0:T(8,128)S(1)}, u32[]{:S(2)}, u32[]{:S(2)}) collective-permute-start(f32[64,128]{1,0:T(8,128)S(1)} %pair.4), channel_id=1, source_target_pairs={{0,2},{1,3},{2,0},{3,1},{4,6},{5,7},{6,4},{7,5},{8,10},{9,11},{10,... | collective-permute-start | bytes 98312 | tf_op jit(solution)/shard_map/ppermute | solution.py:554
  26.7 2.7 %accum.1 = (f32[32,32768]{1,0:T(8,128)S(1)}, f32[32,32768]{1,0:T(8,128)S(1)}, f32[4,64,128]{2,1,0:T(8,128)S(1)}) custom-call(f32[32,32768]{1,0:T(8,128)S(1)} %get-tuple-element.38.inv_one, f32[32,32768]{1,0:T(8,128)S(1)} %get-tuple-element.39.inv_two), custom_call_target="tpu_custom_call", output_to_operand_aliasing={{0}: (0, {}), {1}: (1, {})} | custom-call | bytes 10500000 | tf_op jit(solution)/shard_map/accum/pallas_call | solution.py:39
  29.4 1.1 %collective-permute-done.6.refs_3_ = f32[64,128]{1,0:T(8,128)S(1)} collective-permute-done((f32[64,128]{1,0:T(8,128)S(1)}, f32[64,128]{1,0:T(8,128)S(1)}, u32[]{:S(2)}, u32[]{:S(2)}) %collective-permute-start.6) | collective-permute-done | bytes 32800 | tf_op jit(solution)/shard_map/ppermute | solution.py:554
  30.5 0.6 bases.1
  31.1 0.6 collective-permute-start.10
  31.7 0.5 collective-permute-start.11
  32.2 2.9 %leaf_first.1 = (bf16[2,32,8192]{2,1,0:T(8,128)(2,1)S(1)}, f32[2,256,256]{2,1,0:T(8,128)S(1)}) custom-call(s32[2]{0:T(128)S(1)} %pad_add_fusion.meta.refs_0_, s32[32,32768]{1,0:T(8,128)S(1)} %get-tuple-element.34.refs_0_.leaf, f32[32,32768]{1,0:T(8,128)S(1)} %get-tuple-element.32.weight.refs_1_, s32[32,32768]{1,0:T(8,128)S(1)} %get-tuple-element.33.events.refs_2_, ...), custom_call_target="tpu_custom_call" | custom-call | bytes 10500000 | tf_op jit(solution)/shard_map/leaf_first/pallas_call | solution.py:39
  35.1 0.1 collective-permute-done.10.refs_1_.refs_10_.refs_0_.refs_3_
  35.2 0.5 collective-permute-done.11.refs_2_.refs_11_.refs_1_.refs_4_
  35.8 1.9 %collective-permute-start.16 = (bf16[2,32,8192]{2,1,0:T(8,128)(2,1)S(1)}, bf16[2,32,8192]{2,1,0:T(8,128)(2,1)S(1)}, u32[]{:S(2)}, u32[]{:S(2)}) collective-permute-start(bf16[2,32,8192]{2,1,0:T(8,128)(2,1)S(1)} %release.1.refs_13_), channel_id=1, source_target_pairs={{0,24},{8,16},{16,8},{24,0},{1,25},{9,17},{17,9},{25,1},{2,26},{10... | collective-permute-start | bytes 3145736 | tf_op jit(solution)/shard_map/ppermute | solution.py:554
  37.7 9.9 %leaf_rest.1 = (bf16[2,32,8192]{2,1,0:T(8,128)(2,1)S(1)}, f32[32,128]{1,0:T(8,128)S(1)}, f32[2,32,8192]{2,1,0:T(8,128)S(1)}, f32[2,32,8192]{2,1,0:T(8,128)S(1)},...) custom-call(s32[2]{0:T(128)S(1)} %pad_add_fusion.meta.refs_0_, ...), custom_call_target="tpu_custom_call", output_to_operand_aliasing={{6}: (13, {})} | custom-call | bytes 35000000 | tf_op jit(solution)/shard_map/leaf_rest/pallas_call | solution.py:39
  47.5 0.1 collective-permute-start.12
  47.6 1.2 %collective-permute-done.12.right = f32[32,128]{1,0:T(8,128)S(1)} collective-permute-done((f32[32,128]{1,0:T(8,128)S(1)}, f32[32,128]{1,0:T(8,128)S(1)}, u32[]{:S(2)}, u32[]{:S(2)}) %collective-permute-start.12) | collective-permute-done | bytes 16416 | tf_op jit(solution)/shard_map/ppermute | solution.py:554
  48.8 2.3 %collective-permute-start.15 = (f32[32,128]{1,0:T(8,128)S(1)}, f32[32,128]{1,0:T(8,128)S(1)}, u32[]{:S(2)}, u32[]{:S(2)}) collective-permute-start(f32[32,128]{1,0:T(8,128)S(1)} %pair.5.refs_0_), channel_id=1, source_target_pairs={{0,6},{1,7},{2,4},{3,5},{4,2},{5,3},{6,0},{7,1},{8,14},{9,15},{10,... | collective-permute-start | bytes 49160 | tf_op jit(solution)/shard_map/ppermute | solution.py:554
  51.1 2.1 %collective-permute-start.13 = (f32[32,128]{1,0:T(8,128)S(1)}, f32[32,128]{1,0:T(8,128)S(1)}, u32[]{:S(2)}, u32[]{:S(2)}) collective-permute-start(f32[32,128]{1,0:T(8,128)S(1)} %pair.5.refs_0_), channel_id=1, source_target_pairs={{0,2},{1,3},{2,0},{3,1},{4,6},{5,7},{6,4},{7,5},{8,10},{9,11},{10,... | collective-permute-start | bytes 49160 | tf_op jit(solution)/shard_map/ppermute | solution.py:554
  53.2 3.3 %finish.1.refs_1_ = bf16[2,128,8192]{2,1,0:T(8,128)(2,1)} custom-call(s32[2]{0:T(128)S(1)} %pad_add_fusion.meta.refs_0_, s16[2,32,8192]{2,1,0:T(8,128)(2,1)S(1)} %collective-permute-done.8.refs_3_.refs_8_.refs_1_, s16[2,32,8192]{2,1,0:T(8,128)(2,1)S(1)} %collective-permute-done.9.refs_4_.refs_9_.refs_2_, ...), custom_call_target="tpu_custom_call" | custom-call | bytes 14000000 | tf_op jit(solution)/shard_map/finish/pallas_call | solution.py:39
  56.5 3.9 %update.1 = (f32[32,32768]{1,0:T(8,128)}, f32[32,64]{1,0:T(8,128)}) custom-call(f32[32,32768]{1,0:T(8,128)S(1)} %get-tuple-element.53.pred, s32[32,32768]{1,0:T(8,128)S(1)} %get-tuple-element.34.refs_0_.leaf, f32[32,128]{1,0:T(8,128)S(1)} %pair.5.refs_0_, f32[32,128]{1,0:T(8,128)S(1)} %collective-permute-done.13.refs_1_, ...), custom_call_target="tpu_custom_call" | custom-call | bytes 14000000 | tf_op jit(solution)/shard_map/update/pallas_call | solution.py:39
  60.4 1.6 %place.1 = bf16[2,128,8192]{2,1,0:T(8,128)(2,1)} custom-call(s32[2]{0:T(128)S(1)} %pad_add_fusion.meta.refs_0_, bf16[2,32,8192]{2,1,0:T(8,128)(2,1)S(1)} %collective-permute-done.16.refs_0_, bf16[2,128,8192]{2,1,0:T(8,128)(2,1)} %finish.1.refs_1_, f32[32,32768]{1,0:T(8,128)} %get-tuple-element.61.refs_2_), custom_call_target="tpu_custom_call", output_to_operand_aliasing={{}: (2, {})} | custom-call | bytes 3500000 | tf_op jit(solution)/shard_map/place/pallas_call | solution.py:39
  (19 shorter events, 0.1 us)
Async XLA Ops:
  0.7 14.5 %copy-start = (s32[32768]{0:T(1024)S(1)}, s32[32768]{0:T(1024)}, u32[]{:S(2)}) copy-start(s32[32768]{0:T(1024)} %param.7) | copy-start | bytes 393220
  5.1 30.7 %collective-permute-start.8 = (s16[2,32,8192]{2,1,0:T(8,128)(2,1)S(1)}, s16[2,32,8192]{2,1,0:T(8,128)(2,1)S(1)}, u32[]{:S(2)}, u32[]{:S(2)}) collective-permute-start(s16[2,32,8192]{2,1,0:T(8,128)(2,1)S(1)} %get-tuple-element.47), channel_id=1, source_target_pairs={{0,8},{8,0},{16,24},{24,16},{1,9},{9,1},{17,25},{25,17},{2,10},{10... | collective-permute-start | bytes 3145736 | tf_op jit(solution)/shard_map/ppermute | solution.py:554
  8.1 27.7 %collective-permute-start.9 = (s16[2,32,8192]{2,1,0:T(8,128)(2,1)S(1)}, s16[2,32,8192]{2,1,0:T(8,128)(2,1)S(1)}, u32[]{:S(2)}, u32[]{:S(2)}) collective-permute-start(s16[2,32,8192]{2,1,0:T(8,128)(2,1)S(1)} %get-tuple-element.48), channel_id=1, source_target_pairs={{0,16},{8,24},{16,0},{24,8},{1,17},{9,25},{17,1},{25,9},{2,18},{10... | collective-permute-start | bytes 3145736 | tf_op jit(solution)/shard_map/ppermute | solution.py:554
  9.6 1.2 %collective-permute-start = (f32[32,128]{1,0:T(8,128)S(1)}, f32[32,128]{1,0:T(8,128)S(1)}, u32[]{:S(2)}, u32[]{:S(2)}) collective-permute-start(f32[32,128]{1,0:T(8,128)S(1)} %get-tuple-element.35.left), channel_id=1, source_target_pairs={{0,1},{1,0},{2,3},{3,2},{4,5},{5,4},{6,7},{7,6},{8,9},{9,8},{10,11... | collective-permute-start | bytes 49160 | tf_op jit(solution)/shard_map/ppermute | solution.py:554
  10.8 7.9 %collective-permute-start.3 = (f32[32,128]{1,0:T(8,128)S(1)}, f32[32,128]{1,0:T(8,128)S(1)}, u32[]{:S(2)}, u32[]{:S(2)}) collective-permute-start(f32[32,128]{1,0:T(8,128)S(1)} %pair.3), channel_id=1, source_target_pairs={{0,6},{1,7},{2,4},{3,5},{4,2},{5,3},{6,0},{7,1},{8,14},{9,15},{10,... | collective-permute-start | bytes 49160 | tf_op jit(solution)/shard_map/ppermute | solution.py:554
  14.4 4.6 %collective-permute-start.2 = (f32[32,128]{1,0:T(8,128)S(1)}, f32[32,128]{1,0:T(8,128)S(1)}, u32[]{:S(2)}, u32[]{:S(2)}) collective-permute-start(f32[32,128]{1,0:T(8,128)S(1)} %pair.3), channel_id=1, source_target_pairs={{0,4},{1,5},{2,6},{3,7},{4,0},{5,1},{6,2},{7,3},{8,12},{9,13},{10,... | collective-permute-start | bytes 49160 | tf_op jit(solution)/shard_map/ppermute | solution.py:554
  14.4 4.6 %collective-permute-start.1 = (f32[32,128]{1,0:T(8,128)S(1)}, f32[32,128]{1,0:T(8,128)S(1)}, u32[]{:S(2)}, u32[]{:S(2)}) collective-permute-start(f32[32,128]{1,0:T(8,128)S(1)} %pair.3), channel_id=1, source_target_pairs={{0,2},{1,3},{2,0},{3,1},{4,6},{5,7},{6,4},{7,5},{8,10},{9,11},{10,... | collective-permute-start | bytes 49160 | tf_op jit(solution)/shard_map/ppermute | solution.py:554
  21.1 1.2 %collective-permute-start.4 = (f32[64,128]{1,0:T(8,128)S(1)}, f32[64,128]{1,0:T(8,128)S(1)}, u32[]{:S(2)}, u32[]{:S(2)}) collective-permute-start(f32[64,128]{1,0:T(8,128)S(1)} %get-tuple-element.42.left), channel_id=1, source_target_pairs={{0,1},{1,0},{2,3},{3,2},{4,5},{5,4},{6,7},{7,6},{8,9},{9,8},{10,11... | collective-permute-start | bytes 98312 | tf_op jit(solution)/shard_map/ppermute | solution.py:554
  22.4 7.1 %collective-permute-start.7 = (f32[64,128]{1,0:T(8,128)S(1)}, f32[64,128]{1,0:T(8,128)S(1)}, u32[]{:S(2)}, u32[]{:S(2)}) collective-permute-start(f32[64,128]{1,0:T(8,128)S(1)} %pair.4), channel_id=1, source_target_pairs={{0,6},{1,7},{2,4},{3,5},{4,2},{5,3},{6,0},{7,1},{8,14},{9,15},{10,... | collective-permute-start | bytes 98312 | tf_op jit(solution)/shard_map/ppermute | solution.py:554
  25.7 4.8 %collective-permute-start.6 = (f32[64,128]{1,0:T(8,128)S(1)}, f32[64,128]{1,0:T(8,128)S(1)}, u32[]{:S(2)}, u32[]{:S(2)}) collective-permute-start(f32[64,128]{1,0:T(8,128)S(1)} %pair.4), channel_id=1, source_target_pairs={{0,4},{1,5},{2,6},{3,7},{4,0},{5,1},{6,2},{7,3},{8,12},{9,13},{10,... | collective-permute-start | bytes 98312 | tf_op jit(solution)/shard_map/ppermute | solution.py:554
  25.7 4.8 %collective-permute-start.5 = (f32[64,128]{1,0:T(8,128)S(1)}, f32[64,128]{1,0:T(8,128)S(1)}, u32[]{:S(2)}, u32[]{:S(2)}) collective-permute-start(f32[64,128]{1,0:T(8,128)S(1)} %pair.4), channel_id=1, source_target_pairs={{0,2},{1,3},{2,0},{3,1},{4,6},{5,7},{6,4},{7,5},{8,10},{9,11},{10,... | collective-permute-start | bytes 98312 | tf_op jit(solution)/shard_map/ppermute | solution.py:554
  31.1 4.2 %collective-permute-start.10 = (f32[96,128]{1,0:T(8,128)S(1)}, f32[96,128]{1,0:T(8,128)S(1)}, u32[]{:S(2)}, u32[]{:S(2)}) collective-permute-start(f32[96,128]{1,0:T(8,128)S(1)} %get-tuple-element.49), channel_id=1, source_target_pairs={{0,8},{8,0},{16,24},{24,16},{1,9},{9,1},{17,25},{25,17},{2,10},{10... | collective-permute-start | bytes 147464 | tf_op jit(solution)/shard_map/ppermute | solution.py:554
  31.7 4.1 %collective-permute-start.11 = (f32[96,128]{1,0:T(8,128)S(1)}, f32[96,128]{1,0:T(8,128)S(1)}, u32[]{:S(2)}, u32[]{:S(2)}) collective-permute-start(f32[96,128]{1,0:T(8,128)S(1)} %get-tuple-element.50), channel_id=1, source_target_pairs={{0,16},{8,24},{16,0},{24,8},{1,17},{9,25},{17,1},{25,9},{2,18},{10... | collective-permute-start | bytes 147464 | tf_op jit(solution)/shard_map/ppermute | solution.py:554
  35.8 24.7 %collective-permute-start.16 = (bf16[2,32,8192]{2,1,0:T(8,128)(2,1)S(1)}, bf16[2,32,8192]{2,1,0:T(8,128)(2,1)S(1)}, u32[]{:S(2)}, u32[]{:S(2)}) collective-permute-start(bf16[2,32,8192]{2,1,0:T(8,128)(2,1)S(1)} %release.1.refs_13_), channel_id=1, source_target_pairs={{0,24},{8,16},{16,8},{24,0},{1,25},{9,17},{17,9},{25,1},{2,26},{10... | collective-permute-start | bytes 3145736 | tf_op jit(solution)/shard_map/ppermute | solution.py:554
  47.5 1.2 %collective-permute-start.12 = (f32[32,128]{1,0:T(8,128)S(1)}, f32[32,128]{1,0:T(8,128)S(1)}, u32[]{:S(2)}, u32[]{:S(2)}) collective-permute-start(f32[32,128]{1,0:T(8,128)S(1)} %get-tuple-element.54.left), channel_id=1, source_target_pairs={{0,1},{1,0},{2,3},{3,2},{4,5},{5,4},{6,7},{7,6},{8,9},{9,8},{10,11... | collective-permute-start | bytes 49160 | tf_op jit(solution)/shard_map/ppermute | solution.py:554
  48.8 7.7 %collective-permute-start.15 = (f32[32,128]{1,0:T(8,128)S(1)}, f32[32,128]{1,0:T(8,128)S(1)}, u32[]{:S(2)}, u32[]{:S(2)}) collective-permute-start(f32[32,128]{1,0:T(8,128)S(1)} %pair.5.refs_0_), channel_id=1, source_target_pairs={{0,6},{1,7},{2,4},{3,5},{4,2},{5,3},{6,0},{7,1},{8,14},{9,15},{10,... | collective-permute-start | bytes 49160 | tf_op jit(solution)/shard_map/ppermute | solution.py:554
  51.1 5.4 %collective-permute-start.14 = (f32[32,128]{1,0:T(8,128)S(1)}, f32[32,128]{1,0:T(8,128)S(1)}, u32[]{:S(2)}, u32[]{:S(2)}) collective-permute-start(f32[32,128]{1,0:T(8,128)S(1)} %pair.5.refs_0_), channel_id=1, source_target_pairs={{0,4},{1,5},{2,6},{3,7},{4,0},{5,1},{6,2},{7,3},{8,12},{9,13},{10,... | collective-permute-start | bytes 49160 | tf_op jit(solution)/shard_map/ppermute | solution.py:554
  51.1 5.4 %collective-permute-start.13 = (f32[32,128]{1,0:T(8,128)S(1)}, f32[32,128]{1,0:T(8,128)S(1)}, u32[]{:S(2)}, u32[]{:S(2)}) collective-permute-start(f32[32,128]{1,0:T(8,128)S(1)} %pair.5.refs_0_), channel_id=1, source_target_pairs={{0,2},{1,3},{2,0},{3,1},{4,6},{5,7},{6,4},{7,5},{8,10},{9,11},{10,... | collective-permute-start | bytes 49160 | tf_op jit(solution)/shard_map/ppermute | solution.py:554
